TPU v7x, 128 devices: a whole 4x4x4 slice. The times are simulated.
128 devices in a mesh: pp: 4 (over x), ep: 32 (over z, y, core).
Axes of the slice: x: 4, y: 4, z: 4, core: 2. Of those that a mesh axis runs over, the one named last changes fastest.
Arguments:
- hidden_rows: bfloat16 [4096, 7168], P('ep'), may hold values from -6 to 6
- emb_rows: bfloat16 [4096, 7168], P('ep', 'pp'), may hold values from -4 to 4
- expert_ids: int32 [4096, 2], P('ep'), may hold values from 0 to 31, all different within a row; in each aligned block of 128 rows (0 to 127, 128 to 255, ...) at most 16 rows name the same one
- gate_scores: float32 [4096, 2], P('ep'), may hold values from 0.1 to 1
- gain_hidden: float32 [7168], replicated, may hold values from 0.1 to 1.9
- gain_emb: float32 [7168], replicated, may hold values from 0.1 to 1.9
- gate_weight: bfloat16 [32, 7168, 2048], P('ep', None, 'pp'), may hold values from -0.0625 to 0.0625
- up_weight: bfloat16 [32, 7168, 2048], P('ep', None, 'pp'), may hold values from -0.0625 to 0.0625
- down_weight: bfloat16 [32, 2048, 7168], P('ep', 'pp'), may hold values from -0.125 to 0.125
- output_grad: bfloat16 [4096, 7168], P('ep', 'pp'), may hold values from -0.796875 to 0.796875
Outputs:
- moe_out: bfloat16 [4096, 7168], P('ep', 'pp')
- grad_gate: float32 [4096, 2], P('ep')
- grad_hidden: bfloat16 [4096, 7168], P('ep', 'pp')
- grad_emb: bfloat16 [4096, 7168], P('ep', 'pp')
Inputs may be any that keep to these rules, and one draw needn't show every extreme that they name: `expert_ids`: each row names 2 different experts. Among the rows of one device no expert is named more than 16 times, and in every draw some device names some expert exactly 16 times.
All inputs are finite; a program needn't handle non-finite values.
Results may differ from a plain program's by a relative error of at most 0.015.
Values may be sent and summed in bfloat16 or wider, within the bound.
No kernel may reach another device: no remote copies, remote signals or barrier semaphores. Data moves between devices by JAX's collectives and lax.ppermute only.
A program may use at most 128 MiB of HBM per device.

v0:
```python
from functools import reduce

import jax
import jax.numpy as jnp
from jax import lax
from jax.sharding import PartitionSpec as P

EPS = 1e-06


def root_mean(values):
    return jnp.sqrt(jnp.mean(values * values, axis=-1, keepdims=True) + EPS)


def contract_first(left, right):
    return lax.dot_general(
        left, right, (((0,), (0,)), ((), ())), preferred_element_type=jnp.float32
    )


def contract_last(left, right):
    return lax.dot_general(
        left, right, (((1,), (1,)), ((), ())), preferred_element_type=jnp.float32
    )


def per_device(
    hidden_rows,
    emb_rows,
    expert_ids,
    gate_scores,
    gain_hidden,
    gain_emb,
    gate_weight,
    up_weight,
    down_weight,
    output_grad,
):
    width = hidden_rows.shape[1]
    quarter = emb_rows.shape[1]
    start = lax.axis_index("pp") * quarter
    emb_full = lax.all_gather(emb_rows, "pp", axis=1, tiled=True)
    hidden_f = hidden_rows.astype(jnp.float32)
    emb_f = emb_full.astype(jnp.float32)
    hidden_scale = root_mean(hidden_f)
    emb_scale = root_mean(emb_f)
    mixed_input = (hidden_f / hidden_scale * gain_hidden + emb_f / emb_scale * gain_emb).astype(
        jnp.bfloat16
    )
    count_tok, routes = expert_ids.shape
    experts = lax.axis_size("ep")
    capacity = 2 * count_tok * routes // experts
    flat_ids = expert_ids.reshape(-1)
    onehot = (flat_ids[:, None] == jnp.arange(experts, dtype=jnp.int32)[None, :]).astype(jnp.int32)
    ranking = jnp.sum(jnp.cumsum(onehot, axis=0) * onehot, axis=1) - 1
    slot_ids = (flat_ids * capacity + ranking).reshape(count_tok, routes)
    slot_range = jnp.arange(experts * capacity, dtype=jnp.int32)
    selectors = [slot_ids[:, route][:, None] == slot_range[None, :] for route in range(routes)]
    placement = reduce(jnp.logical_or, selectors).astype(jnp.bfloat16)
    weighting = reduce(
        jnp.add,
        [
            selectors[route].astype(jnp.float32) * gate_scores[:, route : route + 1]
            for route in range(routes)
        ],
    )
    slot_score = jnp.sum(weighting, axis=0)
    send_rows = (
        contract_first(placement, mixed_input)
        .astype(jnp.bfloat16)
        .reshape(experts, capacity, width)
    )
    expert_rows = lax.all_to_all(send_rows, "ep", split_axis=0, concat_axis=0, tiled=True)
    expert_rows = expert_rows.reshape(experts * capacity, width)
    gate_mat = gate_weight[0]
    up_mat = up_weight[0]
    down_mat = down_weight[0]
    gate_pre = jnp.dot(expert_rows, gate_mat, preferred_element_type=jnp.float32)
    up_proj = jnp.dot(expert_rows, up_mat, preferred_element_type=jnp.float32)
    sigmoid_g = jax.nn.sigmoid(gate_pre)
    activated = (gate_pre * sigmoid_g * up_proj).astype(jnp.bfloat16)
    partial_value = jnp.dot(activated, down_mat, preferred_element_type=jnp.float32).reshape(
        experts, capacity, width
    )
    summed = lax.psum_scatter(
        partial_value.astype(jnp.bfloat16), "pp", scatter_dimension=2, tiled=True
    )
    returned = lax.all_to_all(summed, "ep", split_axis=0, concat_axis=0, tiled=True).reshape(
        experts * capacity, quarter
    )
    route_outputs = [
        jnp.dot(selector.astype(jnp.bfloat16), returned, preferred_element_type=jnp.float32)
        for selector in selectors
    ]
    moe_out = reduce(
        jnp.add,
        [gate_scores[:, route : route + 1] * route_outputs[route] for route in range(routes)],
    ).astype(jnp.bfloat16)
    grad_f = output_grad.astype(jnp.float32)
    grad_send = (
        (contract_first(placement, output_grad) * slot_score[:, None])
        .astype(jnp.bfloat16)
        .reshape(experts, capacity, quarter)
    )
    grad_arrived = lax.all_to_all(grad_send, "ep", split_axis=0, concat_axis=0, tiled=True)
    grad_rows = lax.all_gather(grad_arrived, "pp", axis=2, tiled=True).reshape(
        experts * capacity, width
    )
    grad_inner = contract_last(grad_rows, down_mat)
    grad_gate_pre = (
        grad_inner * up_proj * sigmoid_g * (1.0 + gate_pre * (1.0 - sigmoid_g))
    ).astype(jnp.bfloat16)
    grad_up = (grad_inner * gate_pre * sigmoid_g).astype(jnp.bfloat16)
    input_part = (contract_last(grad_gate_pre, gate_mat) + contract_last(grad_up, up_mat)).reshape(
        experts, capacity, width
    )
    input_sum = lax.psum_scatter(
        input_part.astype(jnp.bfloat16), "pp", scatter_dimension=2, tiled=True
    )
    input_back = lax.all_to_all(input_sum, "ep", split_axis=0, concat_axis=0, tiled=True).reshape(
        experts * capacity, quarter
    )
    input_grad = jnp.dot(placement, input_back, preferred_element_type=jnp.float32)
    gate_partial = jnp.stack(
        [jnp.sum(grad_f * route_outputs[route], axis=1) for route in range(routes)], axis=1
    )
    hidden_cols = lax.dynamic_slice_in_dim(hidden_f, start, quarter, 1)
    emb_cols = emb_rows.astype(jnp.float32)
    gain_hidden_cols = lax.dynamic_slice_in_dim(gain_hidden, start, quarter, 0)
    gain_emb_cols = lax.dynamic_slice_in_dim(gain_emb, start, quarter, 0)
    hidden_part = jnp.sum(input_grad * gain_hidden_cols * hidden_cols, axis=1)
    emb_part = jnp.sum(input_grad * gain_emb_cols * emb_cols, axis=1)
    grad_gate, hidden_dot, emb_dot = lax.psum((gate_partial, hidden_part, emb_part), "pp")
    hidden_cube = hidden_scale * hidden_scale * hidden_scale
    emb_cube = emb_scale * emb_scale * emb_scale
    grad_hidden = gain_hidden_cols * input_grad / hidden_scale - hidden_cols * hidden_dot[
        :, None
    ] / (width * hidden_cube)
    grad_emb = gain_emb_cols * input_grad / emb_scale - emb_cols * emb_dot[:, None] / (
        width * emb_cube
    )
    return (moe_out, grad_gate, grad_hidden.astype(jnp.bfloat16), grad_emb.astype(jnp.bfloat16))


def solution(mesh):
    in_specs = (
        P("ep", None),
        P("ep", "pp"),
        P("ep", None),
        P("ep", None),
        P(),
        P(),
        P("ep", None, "pp"),
        P("ep", None, "pp"),
        P("ep", "pp", None),
        P("ep", "pp"),
    )
    out_specs = (P("ep", "pp"), P("ep", None), P("ep", "pp"), P("ep", "pp"))
    return jax.shard_map(
        per_device, mesh=mesh, in_specs=in_specs, out_specs=out_specs, check_vma=False
    )
```

profile of v0, /device:TPU:0, one launch (start us, length us, event | category | flops | bytes accessed | tf_op | source)
XLA Modules:
  0.0 366.1 jit_solution(5216071035765112117)
XLA Ops:
  7.2 0.0 all-gather.3.cloned.1.call-start
  7.2 0.7 all-gather.3.cloned.1.call-update
  7.9 0.8 copy.29
  8.7 0.1 eq.59
  8.8 0.1 eq.55
  9.0 0.6 reduce-window.6
  9.6 0.2 slice_reduce_fusion
  9.8 0.1 fusion.44
  9.9 0.1 sub.16
  10.1 0.1 copy.32
  10.1 0.7 multiply_add_fusion
  10.8 0.8 slice_bitcast_fusion.3
  11.6 0.2 add_reduce_fusion
  11.7 3.0 multiply_convert_fusion
  14.8 8.4 %all-to-all-start.2 = ((bf16[32,16,1792]{2,1,0:T(8,128)(2,1)}), bf16[32,16,1792]{2,1,0:T(8,128)(2,1)S(1)}, u32[]{:S(2)}, u32[]{:S(2)}) async-start(bf16[32,16,1792]{2,1,0:T(8,128)(2,1)} %bitcast.65), calls=%async_computation.3 | async-start | bytes 3670016 | tf_op jit(solution)/shard_map/all_to_all | solution.py:105
  23.2 0.0 copy-start.7
  23.2 0.0 copy-start.8
  23.2 0.0 all-gather.5.cloned.1.call-start
  23.3 1.9 multiply_reduce_fusion
  25.2 24.9 %all-to-all-done.2 = bf16[32,16,1792]{2,1,0:T(8,128)(2,1)S(1)} async-done(((bf16[32,16,1792]{2,1,0:T(8,128)(2,1)}), bf16[32,16,1792]{2,1,0:T(8,128)(2,1)S(1)}, u32[]{:S(2)}, u32[]{:S(2)}) %all-to-all-start.2) | async-done | bytes 1835040 | tf_op jit(solution)/shard_map/all_to_all | solution.py:105
  50.1 1.3 copy-done
  51.5 0.0 all-gather.5.cloned.1.call-update
  51.5 0.0 reduce-scatter.3.cloned.1.call-start
  51.5 0.0 all-gather.3.cloned.1.call-done
  51.6 0.0 slice-start
  51.6 2.1 fusion.10
  53.7 0.0 copy-done.7
  53.7 0.0 copy-done.8
  53.7 0.0 slice-start.1
  53.7 4.5 %convolution_convert_fusion.1 = bf16[512,7168]{1,0:T(8,128)(2,1)S(1)} fusion(bf16[128,7168]{1,0:T(8,128)(2,1)} %all-gather.3.cloned.1.call-done, f32[7168]{0:T(1024)S(1)} %copy-done.7, f32[128]{0:T(128)S(1)} %get-tuple-element.19, f32[7168]{0:T(1024)S(1)} %copy-done.8, f32[128]{0:T(128)S(1)} %get-tuple-element.21, bf16[128,7168]{1,0:T(8,128)(2,1)} %param.10, ...), kind=kOutput, calls=%fused_computation.2 | convolution fusion | flops 950730752 | bytes 11069440 | tf_op jit(solution)/shard_map/dot_general | solution.py:16
  58.2 0.0 slice-start.4
  58.2 88.1 %all_to_all.20 = bf16[32,16,7168]{2,1,0:T(8,128)(2,1)S(1)} all-to-all(bf16[32,16,7168]{2,1,0:T(8,128)(2,1)S(1)} %bitcast.64), channel_id=1, replica_groups=mesh['pp'=4,'ep'=32] {'ep'}, dimensions={0} | all-to-all | bytes 14680064 | tf_op jit(solution)/shard_map/all_to_all | solution.py:73
  146.3 0.0 slice-done
  146.3 0.0 slice-done.1
  146.3 3.9 %fusion.8 = f32[512,512]{1,0:T(8,128)S(1)} fusion(bf16[512,7168]{1,0:T(8,128)(2,1)S(1)} %bitcast.62, bf16[1,7168,512]{2,1,0:T(8,128)(2,1)S(1)} %bitcast.67), kind=kOutput, calls=%fused_computation.11 | convolution fusion | flops 3758096384 | bytes 15728640 | tf_op jit(solution)/shard_map/dot_general | solution.py:78
  150.2 0.0 slice-done.4
  150.3 0.0 slice-done.5
  150.3 0.0 copy-start.1
  150.3 4.9 %multiply_convert_fusion.3 = (bf16[512,512]{1,0:T(8,128)(2,1)S(1)}, f32[512,512]{1,0:T(8,128)}) fusion(f32[512,512]{1,0:T(8,128)S(1)} %fusion.8, bf16[512,7168]{1,0:T(8,128)(2,1)S(1)} %bitcast.63, bf16[1,7168,512]{2,1,0:T(8,128)(2,1)S(1)} %bitcast.71), kind=kOutput, calls=%fused_computation.32 | convolution fusion | flops 3759669248 | bytes 17301504 | tf_op jit(solution)/shard_map/dot_general | solution.py:79
  155.2 0.0 copy-done.1
  155.2 9.3 %convolution_convert_fusion = bf16[32,16,7168]{2,1,0:T(8,128)(2,1)} fusion(bf16[32,16,512]{2,1,0:T(8,128)(2,1)S(1)} %bitcast.75, bf16[1,512,7168]{2,1,0:T(8,128)(2,1)} %param.18), kind=kOutput, calls=%fused_computation.1 | convolution fusion | flops 3761766400 | bytes 15204352 | tf_op jit(solution)/shard_map/dot_general | solution.py:82
  164.5 0.0 reduce-scatter.3.cloned.1.call-update
  164.5 0.3 reduce-scatter.5.cloned.1.call-start
  164.8 0.0 all-gather.5.cloned.1.call-done
  164.8 0.0 slice-start.3
  164.8 8.7 %fusion.1 = f32[512,512]{1,0:T(8,128)S(1)} fusion(bf16[512,7168]{1,0:T(8,128)(2,1)} %bitcast.74, bf16[1,512,7168]{2,1,0:T(8,128)(2,1)} %param.18), kind=kOutput, calls=%fused_computation.4 | convolution fusion | flops 3758096384 | bytes 15728640 | tf_op jit(solution)/shard_map/dot_general | solution.py:22
  173.5 0.0 copy-start.3
  173.5 1.0 copy-done.3
  174.5 7.7 %fusion.6 = f32[512,7168]{1,0:T(8,128)} fusion(bf16[1,7168,512]{2,1,0:T(8,128)(2,1)S(1)} %bitcast.69, f32[512,512]{1,0:T(8,128)S(1)} %copy-done.2, f32[512,512]{1,0:T(8,128)S(1)} %fusion.1, f32[512,512]{1,0:T(8,128)S(1)} %copy-done.6), kind=kOutput, calls=%fused_computation.9 | convolution fusion | flops 3760717824 | bytes 25165824 | tf_op jit(solution)/shard_map/dot_general | solution.py:22
  182.3 15.1 %add_convert_fusion = bf16[512,7168]{1,0:T(8,128)(2,1)} fusion(f32[512,7168]{1,0:T(8,128)} %fusion.6, bf16[1,7168,512]{2,1,0:T(8,128)(2,1)} %param.17, f32[512,512]{1,0:T(8,128)} %copy-done.3, f32[512,512]{1,0:T(8,128)} %copy-done.1), kind=kOutput, calls=%fused_computation | convolution fusion | flops 3767009280 | bytes 31457280 | tf_op jit(solution)/shard_map/dot_general | solution.py:22
  197.4 0.0 reduce-scatter.5.cloned.1.call-update
  197.4 39.3 %reduce-scatter.3.cloned.1.call-done = bf16[32,16,1792]{2,1,0:T(8,128)(2,1)} async-done(((bf16[32,16,7168]{2,1,0:T(8,128)(2,1)}), bf16[32,16,1792]{2,1,0:T(8,128)(2,1)}) %reduce-scatter.3.cloned.1.call-update) | async-done | bytes 1835024 | tf_op jit(solution)/shard_map/reduce_scatter | solution.py:85
  236.7 33.1 %all_to_all.21 = bf16[32,16,1792]{2,1,0:T(8,128)(2,1)S(1)} all-to-all(bf16[32,16,1792]{2,1,0:T(8,128)(2,1)} %reduce-scatter.3.cloned.1.call-done), channel_id=1, replica_groups=mesh['pp'=4,'ep'=32] {'ep'}, dimensions={0} | all-to-all | bytes 3670016 | tf_op jit(solution)/shard_map/all_to_all | solution.py:88
  269.7 41.5 %reduce-scatter.5.cloned.1.call-done = bf16[32,16,1792]{2,1,0:T(8,128)(2,1)} async-done(((bf16[32,16,7168]{2,1,0:T(8,128)(2,1)}), bf16[32,16,1792]{2,1,0:T(8,128)(2,1)}) %reduce-scatter.5.cloned.1.call-update) | async-done | bytes 1835024 | tf_op jit(solution)/shard_map/reduce_scatter | solution.py:117
  311.2 7.4 %all-to-all-start.3 = ((bf16[32,16,1792]{2,1,0:T(8,128)(2,1)}), bf16[32,16,1792]{2,1,0:T(8,128)(2,1)}, u32[]{:S(2)}, u32[]{:S(2)}) async-start(bf16[32,16,1792]{2,1,0:T(8,128)(2,1)} %reduce-scatter.5.cloned.1.call-done), calls=%async_computation.5 | async-start | bytes 3670016 | tf_op jit(solution)/shard_map/all_to_all | solution.py:120
  318.6 0.1 dynamic_slice.11
  318.7 0.1 dynamic_slice.9
  318.8 3.7 %convert_element_type.59 = f32[128,7168]{1,0:T(8,128)} convert(bf16[128,7168]{1,0:T(8,128)(2,1)} %param.10) | non-fusion elementwise | flops 917504 | bytes 5505024 | tf_op jit(solution)/shard_map/convert_element_type | solution.py:43
  322.5 0.4 fusion.28
  322.9 1.3 fusion.20
  324.3 21.2 %all-to-all-done.3 = bf16[32,16,1792]{2,1,0:T(8,128)(2,1)} async-done(((bf16[32,16,1792]{2,1,0:T(8,128)(2,1)}), bf16[32,16,1792]{2,1,0:T(8,128)(2,1)}, u32[]{:S(2)}, u32[]{:S(2)}) %all-to-all-start.3) | async-done | bytes 1835040 | tf_op jit(solution)/shard_map/all_to_all | solution.py:120
  345.5 2.3 fusion.22
  347.8 9.2 %all-reduce = (f32[128,2]{0,1:T(2,128)}, f32[128]{0:T(128)S(1)}, f32[128]{0:T(128)S(1)}) all-reduce(f32[128,2]{0,1:T(2,128)S(1)} %pad_maximum_fusion, f32[128]{0:T(128)S(1)} %get-tuple-element.5, f32[128]{0:T(128)S(1)} %get-tuple-element.4), channel_id=1, replica_groups=mesh['pp'=4,'ep'=32] {'pp'}, use_global_device_ids=true, to_apply=%region_8.9 | all-reduce | flops 512 | bytes 4096 | tf_op jit(solution)/shard_map/psum | solution.py:133
  357.1 2.5 fusion.25
  (24 shorter events, 0.1 us)
Async XLA Ops:
  7.2 44.4 %all-gather.3.cloned.1.call-start = ((), (), s32[]{:S(2)}) async-start(), calls=%async_computation.6 | async-start | bytes 2293760 | tf_op jit(solution)/shard_map/all_gather | solution.py:42
  14.8 35.4 %all-to-all-start.2 = ((bf16[32,16,1792]{2,1,0:T(8,128)(2,1)}), bf16[32,16,1792]{2,1,0:T(8,128)(2,1)S(1)}, u32[]{:S(2)}, u32[]{:S(2)}) async-start(bf16[32,16,1792]{2,1,0:T(8,128)(2,1)} %bitcast.65), calls=%async_computation.3 | async-start | bytes 3670016 | tf_op jit(solution)/shard_map/all_to_all | solution.py:105
  23.2 30.5 %copy-start.7 = (f32[7168]{0:T(1024)S(1)}, f32[7168]{0:T(1024)}, u32[]{:S(2)}) copy-start(f32[7168]{0:T(1024)} %param.15) | copy-start | bytes 86020
  23.2 30.5 %copy-start.8 = (f32[7168]{0:T(1024)S(1)}, f32[7168]{0:T(1024)}, u32[]{:S(2)}) copy-start(f32[7168]{0:T(1024)} %param.14) | copy-start | bytes 86020
  23.2 141.6 %all-gather.5.cloned.1.call-start = ((), (), s32[]{:S(2)}) async-start(), calls=%async_computation.8 | async-start | bytes 9175040 | tf_op jit(solution)/shard_map/all_gather | solution.py:106
  50.1 1.3 copy-start
  51.5 185.2 %reduce-scatter.3.cloned.1.call-start = ((), (), s32[]{:S(2)}) async-start(), calls=%async_computation.7 | async-start | bytes 9175040 | tf_op jit(solution)/shard_map/reduce_scatter | solution.py:85
  51.6 94.7 %slice-start = ((s8[7340032]{0:T(1024)(128)(4,1)}), s8[4194304]{0:T(1024)(128)(4,1)S(1)}, s32[]{:S(2)}) async-start(s8[7340032]{0:T(1024)(128)(4,1)} %bitcast.66), calls=%async_computation.10 | async-start | bytes 8388608
  53.7 92.6 %slice-start.1 = ((s8[7340032]{0:T(1024)(128)(4,1)}), s8[3145728]{0:T(1024)(128)(4,1)S(1)}, s32[]{:S(2)}) async-start(s8[7340032]{0:T(1024)(128)(4,1)} %bitcast.66), calls=%async_computation.11 | async-start | bytes 6291456
  58.2 92.0 %slice-start.4 = ((s8[7340032]{0:T(1024)(128)(4,1)}), s8[3145728]{0:T(1024)(128)(4,1)S(1)}, s32[]{:S(2)}) async-start(s8[7340032]{0:T(1024)(128)(4,1)} %bitcast.70), calls=%async_computation.14 | async-start | bytes 6291456
  146.3 4.0 %slice-start.5 = ((s8[7340032]{0:T(1024)(128)(4,1)}), s8[4194304]{0:T(1024)(128)(4,1)S(1)}, s32[]{:S(2)}) async-start(s8[7340032]{0:T(1024)(128)(4,1)} %bitcast.70), calls=%async_computation.15 | async-start | bytes 8388608
  150.3 4.9 %copy-start.1 = (f32[512,512]{1,0:T(8,128)}, f32[512,512]{1,0:T(8,128)S(1)}, u32[]{:S(2)}) copy-start(f32[512,512]{1,0:T(8,128)S(1)} %fusion.8) | copy-start | bytes 3145732
  164.5 10.0 %slice-start.2 = ((s8[7340032]{0:T(1024)(128)(4,1)}), s8[3145728]{0:T(1024)(128)(4,1)S(1)}, s32[]{:S(2)}) async-start(s8[7340032]{0:T(1024)(128)(4,1)} %bitcast.68), calls=%async_computation.12 | async-start | bytes 6291456
  164.5 146.7 %reduce-scatter.5.cloned.1.call-start = ((), (), s32[]{:S(2)}) async-start(), calls=%async_computation.9 | async-start | bytes 9175040 | tf_op jit(solution)/shard_map/reduce_scatter | solution.py:117
  164.8 9.7 %slice-start.3 = ((s8[7340032]{0:T(1024)(128)(4,1)}), s8[4194304]{0:T(1024)(128)(4,1)S(1)}, s32[]{:S(2)}) async-start(s8[7340032]{0:T(1024)(128)(4,1)} %bitcast.68), calls=%async_computation.13 | async-start | bytes 8388608
  164.8 9.7 %copy-start.2 = (f32[512,512]{1,0:T(8,128)S(1)}, f32[512,512]{1,0:T(8,128)}, u32[]{:S(2)}) copy-start(f32[512,512]{1,0:T(8,128)} %copy-done.1) | copy-start | bytes 3145732
  164.8 9.7 %copy-start.6 = (f32[512,512]{1,0:T(8,128)S(1)}, f32[512,512]{1,0:T(8,128)}, u32[]{:S(2)}) copy-start(f32[512,512]{1,0:T(8,128)} %get-tuple-element.23) | copy-start | bytes 3145732
  173.5 1.0 copy-start.3
  311.2 34.3 %all-to-all-start.3 = ((bf16[32,16,1792]{2,1,0:T(8,128)(2,1)}), bf16[32,16,1792]{2,1,0:T(8,128)(2,1)}, u32[]{:S(2)}, u32[]{:S(2)}) async-start(bf16[32,16,1792]{2,1,0:T(8,128)(2,1)} %reduce-scatter.5.cloned.1.call-done), calls=%async_computation.5 | async-start | bytes 3670016 | tf_op jit(solution)/shard_map/all_to_all | solution.py:120
  318.7 4.2 %copy-start.5 = (bf16[128,1792]{1,0:T(8,128)(2,1)S(1)}, bf16[128,1792]{1,0:T(8,128)(2,1)}, u32[]{:S(2)}) copy-start(bf16[128,1792]{1,0:T(8,128)(2,1)} %param.19) | copy-start | bytes 1376260
  322.5 23.0 %copy-start.4 = (bf16[128,1792]{1,0:T(8,128)(2,1)S(1)}, bf16[128,1792]{1,0:T(8,128)(2,1)}, u32[]{:S(2)}) copy-start(bf16[128,1792]{1,0:T(8,128)(2,1)} %param.11) | copy-start | bytes 1376260
Sparse Core Ops, SparseCore 0:
  9.7 31.0 all-gather.2
  51.6 71.3 all-gather.4
  164.6 72.0 reduce-scatter.2
  238.9 72.2 reduce-scatter.4
where the time goes:
time: 367 us; the launch traced here: 366 us
  blocking collectives  130 us (35%)
  waiting for transfers between devices  128 us (35%)
  matrix products  61.3 us (17%)
  starting transfers between devices  16.2 us (4%)
  between operations  14 us (4%)
  other arithmetic  11.9 us (3%)
  local copies, waits for them, and re-layouts  4.73 us (1%)
    all_to_all x1, blocking collectives, per_device(): lax.all_to_all(send_rows, 'ep', split_axis=0, concat_axis=0, tiled=True)  88.1 us
    reduce_scatter x1, waiting for transfers between devices, per_device(): lax.psum_scatter(input_part.astype(jnp.bfloat16), 'pp', scatter_dimension...  41.5 us
    reduce_scatter x1, waiting for transfers between devices, per_device(): lax.psum_scatter(partial_value.astype(jnp.bfloat16), 'pp', scatter_dimens...  39.3 us
    all_to_all x1, blocking collectives, per_device(): lax.all_to_all(summed, 'ep', split_axis=0, concat_axis=0, tiled=True)  33.1 us
    dot_general x3, matrix products, contract_last(): lax.dot_general(left, right, (((1,), (1,)), ((), ())), preferred_element_...  31.5 us
    all_to_all x1, waiting for transfers between devices, per_device(): lax.all_to_all(grad_send, 'ep', split_axis=0, concat_axis=0, tiled=True)  24.9 us
    all_to_all x1, waiting for transfers between devices, per_device(): lax.all_to_all(input_sum, 'ep', split_axis=0, concat_axis=0, tiled=True)  21.2 us
    dot_general x1, matrix products, per_device(): jnp.dot(activated, down_mat, preferred_element_type=jnp.float32)  9.26 us
  transfers between devices with their start and end apart: 6, of which 4 were waited for; matrix products, arithmetic and copies ran while one was open for 19% of the time, Pallas kernels for 0%

commit v1 on v0

v1 whole, which is shorter than its diff:
```python
import jax
import jax.numpy as jnp
from jax import lax
from jax.experimental import pallas as pl
from jax.experimental.pallas import tpu as pltpu
from jax.sharding import PartitionSpec as P

EPS = 1e-06
BF = jnp.bfloat16
F32 = jnp.float32


def dot(left, right, dims):
    return lax.dot_general(left, right, (dims, ((), ())), preferred_element_type=F32)


def shift(value, step):
    ring = lax.axis_size("pp")
    return lax.ppermute(value, "pp", [(i, (i + step) % ring) for i in range(ring)])


def after(value, *others):
    def nothing(*refs):
        pass

    anywhere = pl.BlockSpec(memory_space=pl.ANY)
    return pl.pallas_call(
        nothing,
        out_shape=jax.ShapeDtypeStruct(value.shape, value.dtype),
        in_specs=[anywhere] * (1 + len(others)),
        out_specs=anywhere,
        input_output_aliases={0: 0},
    )(value, *others)


ANYWHERE = pl.BlockSpec(memory_space=pl.ANY)


def params():
    return pltpu.CompilerParams(vmem_limit_bytes=50 * 1024 * 1024)


def ring_gather(own):
    half = own.shape[0] // 2
    below = shift(own, 1)
    above = shift(own, -1)
    return own, above, below, shift(below[:half], 1), shift(above[half:], -1)


def add_halves(up, down, from_below, from_above, *others):
    rows, width = from_below.shape

    def body(up_ref, down_ref, below_ref, above_ref, *refs):
        up_out, down_out = refs[-2:]
        up_out[...] = (up_ref[...].astype(F32) + below_ref[...].astype(F32)).astype(BF)
        down_out[...] = (down_ref[...].astype(F32) + above_ref[...].astype(F32)).astype(BF)

    block = (rows, width // 2)
    first = pl.BlockSpec(block, lambda i: (0, i))
    last = pl.BlockSpec(block, lambda i: (1, i))
    return pl.pallas_call(
        body,
        grid=(2,),
        out_shape=[jax.ShapeDtypeStruct(up.shape, BF)] * 2,
        in_specs=[first, last, first, first] + [ANYWHERE] * len(others),
        out_specs=[first, last],
        input_output_aliases={0: 0, 1: 1},
        compiler_params=params(),
    )(up, down, from_below, from_above, *others)


def ring_scatter(far_low, far_high, rest, *others):
    from_below = shift(far_low, 1)
    from_above = shift(far_high, -1)
    up, down, own = rest()
    up, down = add_halves(up, down, from_below, from_above, *others)
    parts = (own, shift(up, 1), shift(down, -1))
    return parts, (up, down), (from_below, from_above)


def sum_beside(left, parts, *others):
    count, quarter = left.shape
    blocks = 2
    width = quarter // blocks

    def body(left_ref, a_ref, b_ref, c_ref, *refs):
        out = refs[-1]

        @pl.when(pl.program_id(0) < blocks)
        def _():
            out[...] = left_ref[...]

        @pl.when(pl.program_id(0) >= blocks)
        def _():
            total = a_ref[...].astype(F32) + b_ref[...].astype(F32) + c_ref[...].astype(F32)
            out[...] = total.astype(BF)

    copied = pl.BlockSpec((count, width), lambda i: (0, jnp.minimum(i, blocks - 1)))
    added = pl.BlockSpec((count, width), lambda i: (0, jnp.maximum(i - blocks, 0)))
    return pl.pallas_call(
        body,
        grid=(2 * blocks,),
        out_shape=jax.ShapeDtypeStruct((count, 2 * quarter), BF),
        in_specs=[copied, added, added, added] + [ANYWHERE] * len(others),
        out_specs=pl.BlockSpec((count, width), lambda i: (0, i)),
        compiler_params=params(),
    )(left, *parts, *others)


def row_half(array, part, *others):
    rows, width = array.shape

    def body(array_ref, *refs):
        refs[-1][...] = array_ref[...]

    return pl.pallas_call(
        body,
        grid=(1,),
        out_shape=jax.ShapeDtypeStruct((rows // 2, width), array.dtype),
        in_specs=[pl.BlockSpec((rows // 2, width), lambda i: (part, 0))]
        + [ANYWHERE] * len(others),
        out_specs=pl.BlockSpec((rows // 2, width), lambda i: (0, 0)),
        compiler_params=params(),
    )(array, *others)


def cut_columns(here, array, offset, part, *others):
    rows, width = array.shape
    quarter = width // 4
    steps = 2 if part is None else 1
    first = 0 if part is None else part
    block = rows // 2

    def body(here_ref, array_ref, *refs):
        refs[-1][...] = array_ref[...]

    return pl.pallas_call(
        body,
        grid_spec=pltpu.PrefetchScalarGridSpec(
            num_scalar_prefetch=1,
            grid=(steps,),
            in_specs=[
                pl.BlockSpec((block, quarter), lambda i, here: (i + first, (here[0] + offset) % 4))
            ]
            + [ANYWHERE] * len(others),
            out_specs=pl.BlockSpec((block, quarter), lambda i, here: (i, 0)),
        ),
        out_shape=jax.ShapeDtypeStruct((block * steps, quarter), array.dtype),
        compiler_params=params(),
    )(here, array, *others)


def inner_share(grads, pieces, *others):
    count, quarter = grads.shape
    units = pieces[0].shape[0]
    half = count // 2
    number = len(pieces)

    def body(grads_ref, *refs):
        outs = refs[number + len(others) :]
        shares = [
            dot(grads_ref[...], refs[j][...], ((1,), (1,))).astype(BF) for j in range(number)
        ]
        for i in range(2):

            @pl.when(pl.program_id(0) == i)
            def _():
                for j in range(number):
                    outs[i][:, j * units : (j + 1) * units] = shares[j]

    whole = pl.BlockSpec((units, quarter), lambda i: (0, 0))
    return pl.pallas_call(
        body,
        grid=(2,),
        out_shape=[jax.ShapeDtypeStruct((half, number * units), BF)] * 2,
        in_specs=[pl.BlockSpec((half, quarter), lambda i: (i, 0))]
        + [whole] * number
        + [ANYWHERE] * len(others),
        out_specs=[pl.BlockSpec((half, number * units), lambda i: (0, 0))] * 2,
        compiler_params=params(),
    )(grads, *pieces, *others)


def forward(rows, gate_mat, up_mat, *others):
    count, width = rows.shape
    units = gate_mat.shape[1]
    depth = 1024

    def body(rows_ref, gate_ref, up_ref, *refs):
        gate_out, up_out, act_out = refs[-3:]
        step = pl.program_id(0)

        @pl.when(step == 0)
        def _():
            gate_out[...] = jnp.zeros_like(gate_out)
            up_out[...] = jnp.zeros_like(up_out)

        gate_out[...] += jnp.dot(rows_ref[...], gate_ref[...], preferred_element_type=F32)
        up_out[...] += jnp.dot(rows_ref[...], up_ref[...], preferred_element_type=F32)

        @pl.when(step == pl.num_programs(0) - 1)
        def _():
            gate = gate_out[...]
            act_out[...] = (gate * jax.nn.sigmoid(gate) * up_out[...]).astype(BF)

    whole = pl.BlockSpec((count, units), lambda k: (0, 0))
    weight = pl.BlockSpec((depth, units), lambda k: (k, 0))
    return pl.pallas_call(
        body,
        grid=(width // depth,),
        out_shape=[
            jax.ShapeDtypeStruct((count, units), F32),
            jax.ShapeDtypeStruct((count, units), F32),
            jax.ShapeDtypeStruct((count, units), BF),
        ],
        in_specs=[pl.BlockSpec((count, depth), lambda k: (0, k)), weight, weight]
        + [ANYWHERE] * len(others),
        out_specs=[whole, whole, whole],
        compiler_params=params(),
    )(rows, gate_mat, up_mat, *others)


def backward_far(here, h, gate_pre, up_proj, grad_inner, gate_mat, up_mat, *others):
    count, units = gate_pre.shape
    experts, capacity, _ = grad_inner.shape
    quarter = gate_mat.shape[0] // 4
    block = quarter // 2
    half = count // 2

    def body(here_ref, gate_pre_ref, up_ref, inner_ref, gate_w, up_w, *refs):
        ggp, gup, low, high = refs[-4:]

        @pl.when(pl.program_id(0) == 0)
        def _():
            inner = inner_ref[...].reshape(count, units)
            gate = gate_pre_ref[...]
            sig = jax.nn.sigmoid(gate)
            ggp[...] = (inner * up_ref[...] * sig * (1.0 + gate * (1.0 - sig))).astype(BF)
            gup[...] = (inner * gate * sig).astype(BF)

        piece = dot(ggp[...], gate_w[...], ((1,), (1,))) + dot(gup[...], up_w[...], ((1,), (1,)))
        low[...] = piece[:half].astype(BF)
        high[...] = piece[half:].astype(BF)

    whole = pl.BlockSpec((count, units), lambda j, here: (0, 0))
    weight = pl.BlockSpec((block, units), lambda j, here: (((here[0] + 2) % 4) * 2 + j, 0))
    out = pl.BlockSpec((half, block), lambda j, here: (0, j))
    return pl.pallas_call(
        body,
        grid_spec=pltpu.PrefetchScalarGridSpec(
            num_scalar_prefetch=1,
            grid=(2,),
            in_specs=[
                whole,
                whole,
                pl.BlockSpec((experts, capacity // 2, units), lambda j, here: (0, h, 0)),
                weight,
                weight,
            ]
            + [ANYWHERE] * len(others),
            out_specs=[whole, whole, out, out],
        ),
        out_shape=[
            jax.ShapeDtypeStruct((count, units), BF),
            jax.ShapeDtypeStruct((count, units), BF),
            jax.ShapeDtypeStruct((half, quarter), BF),
            jax.ShapeDtypeStruct((half, quarter), BF),
        ],
        compiler_params=params(),
    )(here, gate_pre, up_proj, grad_inner, gate_mat, up_mat, *others)


def backward_rest(here, grad_gate_pre, grad_up, gate_mat, up_mat):
    count, units = grad_up.shape
    quarter = gate_mat.shape[0] // 4
    block = quarter // 2

    def body(here_ref, ggp, gup, gate_w, up_w, *outs):
        step = pl.program_id(0)
        piece = dot(ggp[...], gate_w[...], ((1,), (1,))) + dot(gup[...], up_w[...], ((1,), (1,)))
        piece = piece.astype(BF)
        for i in range(3):

            @pl.when(step // 2 == i)
            def _():
                outs[i][...] = piece

    whole = pl.BlockSpec((count, units), lambda s, here: (0, 0))

    def weight_block(s, here):
        r = jnp.where(s // 2 == 0, 1, jnp.where(s // 2 == 1, 3, 0))
        return (((here[0] + r) % 4) * 2 + s % 2, 0)

    def out_spec(i):
        return pl.BlockSpec((count, block), lambda s, here: (0, jnp.clip(s - 2 * i, 0, 1)))

    weight = pl.BlockSpec((block, units), weight_block)
    return pl.pallas_call(
        body,
        grid_spec=pltpu.PrefetchScalarGridSpec(
            num_scalar_prefetch=1,
            grid=(6,),
            in_specs=[whole, whole, weight, weight],
            out_specs=[out_spec(i) for i in range(3)],
        ),
        out_shape=[jax.ShapeDtypeStruct((count, quarter), BF) for _ in range(3)],
        compiler_params=params(),
    )(here, grad_gate_pre, grad_up, gate_mat, up_mat)


def down_product(acts, downs, *others):
    count, units = acts[0].shape
    quarter = downs[0].shape[1]
    block = 256
    half_units = units // 2

    def body(a0, a1, a3, a2_low, a2_high, *refs):
        down_refs, (out, far) = refs[: len(downs)], refs[-2:]

        @pl.when(pl.program_id(0) == 0)
        def _():
            far[: count // 2] = a2_low[...]
            far[count // 2 :] = a2_high[...]

        total = jnp.dot(a0[...], down_refs[0][...], preferred_element_type=F32)
        total += jnp.dot(a1[...], down_refs[1][...], preferred_element_type=F32)
        total += jnp.dot(a3[...], down_refs[2][...], preferred_element_type=F32)
        for part in range(2):
            left = far[:, part * half_units : (part + 1) * half_units]
            total += jnp.dot(left, down_refs[3 + part][...], preferred_element_type=F32)
        out[...] = total.astype(BF)

    def held(array):
        return pl.BlockSpec(array.shape, lambda j: (0, 0))

    def streamed(array):
        return pl.BlockSpec((array.shape[0], block), lambda j: (0, j))

    return pl.pallas_call(
        body,
        grid=(quarter // block,),
        out_shape=jax.ShapeDtypeStruct((count, quarter), BF),
        in_specs=[held(a) for a in acts]
        + [streamed(d) for d in downs]
        + [ANYWHERE] * len(others),
        out_specs=pl.BlockSpec((count, block), lambda j: (0, j)),
        scratch_shapes=[pltpu.VMEM((count, units), BF)],
        compiler_params=params(),
    )(*acts, *downs, *others)


def exchange(value):
    return lax.all_to_all(value, "ep", split_axis=0, concat_axis=0, tiled=True)


def per_device(
    hidden_rows,
    emb_rows,
    expert_ids,
    gate_scores,
    gain_hidden,
    gain_emb,
    gate_weight,
    up_weight,
    down_weight,
    output_grad,
):
    tokens, width = hidden_rows.shape
    quarter = emb_rows.shape[1]
    routes = expert_ids.shape[1]
    experts = lax.axis_size("ep")
    ring = lax.axis_size("pp")
    here = lax.axis_index("pp")
    capacity = 2 * tokens * routes // experts
    part = capacity // 2
    gate_mat, up_mat, down_mat = gate_weight[0], up_weight[0], down_weight[0]
    hidden_units = down_mat.shape[0]

    def columns(array, r):
        return lax.dynamic_slice_in_dim(array, ((here + r) % ring) * quarter, quarter, 1)

    flat_ids = expert_ids.reshape(-1)
    onehot = (flat_ids[:, None] == jnp.arange(experts, dtype=jnp.int32)[None, :]).astype(jnp.int32)
    ranking = jnp.sum(jnp.cumsum(onehot, axis=0) * onehot, axis=1) - 1
    ranking = ranking.reshape(tokens, routes)
    slot_ids = expert_ids * capacity + ranking
    slot_range = jnp.arange(experts * capacity, dtype=jnp.int32)
    selectors = [slot_ids[:, k][:, None] == slot_range[None, :] for k in range(routes)]
    placement = (selectors[0] | selectors[1]).astype(BF)
    slot_score = jnp.sum(
        sum(selectors[k].astype(F32) * gate_scores[:, k : k + 1] for k in range(routes)), axis=0
    )
    part_ids = jnp.where(
        ranking < part,
        expert_ids * part + ranking,
        experts * part + expert_ids * part + ranking - part,
    )
    part_range = jnp.arange(experts * part, dtype=jnp.int32)
    part_selectors = [
        [part_ids[:, k][:, None] == (part_range + h * experts * part)[None, :] for k in range(routes)]
        for h in range(2)
    ]
    part_placement = [(part_selectors[h][0] | part_selectors[h][1]).astype(BF) for h in range(2)]

    emb_own, emb_above, emb_below, emb_low, emb_high = ring_gather(emb_rows)
    emb_pieces = [emb_own, emb_above, jnp.concatenate([emb_low, emb_high], axis=0), emb_below]

    place = here.reshape(1)
    down_low, down_high = (cut_columns(place, down_mat, 2, i) for i in range(2))
    pass_low, pass_high = shift(down_low, 1), shift(down_high, -1)
    far_low, far_high = shift(pass_low, 1), shift(pass_high, -1)

    grad_send = (dot(placement, output_grad, ((0,), (0,))) * slot_score[:, None]).astype(BF)
    grad_send = after(grad_send, down_low, down_high)
    grad_slots = exchange(grad_send.reshape(experts, capacity, quarter))
    grad_slots = grad_slots.reshape(experts * capacity, quarter)

    emb_twice = jnp.concatenate(emb_pieces + emb_pieces, axis=1)
    emb_full = lax.dynamic_slice_in_dim(emb_twice, ((ring - here) % ring) * quarter, width, 1)
    hidden_f = hidden_rows.astype(F32)
    emb_f = emb_full.astype(F32)
    hidden_scale = jnp.sqrt(jnp.mean(hidden_f * hidden_f, axis=1, keepdims=True) + EPS)
    emb_scale = jnp.sqrt(jnp.mean(emb_f * emb_f, axis=1, keepdims=True) + EPS)
    mixed_input = (hidden_f / hidden_scale * gain_hidden + emb_f / emb_scale * gain_emb).astype(BF)
    send_rows = [
        dot(part_placement[h], mixed_input, ((0,), (0,))).astype(BF) for h in range(2)
    ]
    down_up = cut_columns(place, down_mat, 1, None, send_rows[0])
    down_back = cut_columns(place, down_mat, 3, None, send_rows[0])
    down_below, down_above = shift(down_up, 1), shift(down_back, -1)
    down_own = cut_columns(place, down_mat, 0, None, grad_slots)
    far = inner_share(grad_slots, (far_low, far_high))
    own = dot(grad_slots, down_own, ((1,), (1,)))
    send_rows[0] = after(send_rows[0], far_low, far_high, down_up, down_back)
    send_rows[1] = after(send_rows[1], down_above, down_below, *far, own)
    arrived = [
        exchange(send_rows[h].reshape(experts, part, width)).reshape(experts * part, width)
        for h in range(2)
    ]
    downs = (down_own, down_above, down_below, far_low, far_high)
    up = jnp.concatenate(inner_share(grad_slots, (down_above,)), axis=0)
    down = jnp.concatenate(inner_share(grad_slots, (down_below,)), axis=0)
    inner_shares, passed, _ = ring_scatter(*far, lambda: (up, down, own))

    gate_pre, up_proj, act = forward(arrived[0], gate_mat, up_mat, *passed)
    act_below, act_above = shift(act, 1), shift(act, -1)
    inner_shares = (after(own, act), *inner_shares[1:])
    grad_inner = sum(share.astype(F32) for share in inner_shares)
    grad_inner = grad_inner.reshape(experts, capacity, hidden_units)
    grad_gate_pre, grad_up, low, high = backward_far(
        place, 0, gate_pre, up_proj, grad_inner, gate_mat, up_mat
    )
    rest = backward_rest(place, grad_gate_pre, grad_up, gate_mat, up_mat)
    act_low = shift(row_half(act_below, 0, rest[0]), 1)
    act_high = shift(row_half(act_above, 1, rest[0]), -1)
    first_acts = (act, act_above, act_below, act_low, act_high)

    gate_pre, up_proj, act = forward(arrived[1], gate_mat, up_mat, rest[0])
    first, passed, _ = ring_scatter(low, high, lambda: rest, act_low, act_high, act)
    act_below, act_above = shift(act, 1), shift(act, -1)
    grad_gate_pre, grad_up, low, high = backward_far(
        place, 1, gate_pre, up_proj, grad_inner, gate_mat, up_mat, *passed
    )
    first_output = down_product(first_acts, downs, low)
    last = backward_rest(place, grad_gate_pre, grad_up, gate_mat, up_mat)
    act_low = shift(row_half(act_below, 0, last[0]), 1)
    act_high = shift(row_half(act_above, 1, last[0]), -1)
    acts = (act, act_above, act_below, act_low, act_high)
    second, passed, came = ring_scatter(low, high, lambda: last, act_low, act_high)
    output = down_product(acts, downs, *passed)

    returned = [
        exchange(both.reshape(experts, part, 2 * quarter))
        for both in (sum_beside(first_output, first, *came), sum_beside(output, second))
    ]
    returned = [both.reshape(experts * part, 2 * quarter) for both in returned]
    back = [both[:, :quarter] for both in returned]
    grads_back = [both[:, quarter:] for both in returned]

    route_outputs = [
        sum(dot(part_selectors[h][k].astype(BF), back[h], ((1,), (0,))) for h in range(2))
        for k in range(routes)
    ]
    moe_out = sum(gate_scores[:, k : k + 1] * route_outputs[k] for k in range(routes)).astype(BF)
    input_grad = sum(dot(part_placement[h], grads_back[h], ((1,), (0,))) for h in range(2))

    grad_f = output_grad.astype(F32)
    hidden_cols = columns(hidden_rows, 0).astype(F32)
    emb_cols = emb_rows.astype(F32)
    gain_hidden_cols = lax.dynamic_slice_in_dim(gain_hidden, here * quarter, quarter, 0)
    gain_emb_cols = lax.dynamic_slice_in_dim(gain_emb, here * quarter, quarter, 0)
    partial = jnp.stack(
        [jnp.sum(grad_f * route_outputs[k], axis=1) for k in range(routes)]
        + [
            jnp.sum(input_grad * gain_hidden_cols * hidden_cols, axis=1),
            jnp.sum(input_grad * gain_emb_cols * emb_cols, axis=1),
        ],
        axis=0,
    )
    total = partial + shift(partial, 1) + shift(partial, 2) + shift(partial, 3)
    grad_gate = total[:routes].T
    hidden_dot, emb_dot = total[routes][:, None], total[routes + 1][:, None]
    hidden_cube = hidden_scale * hidden_scale * hidden_scale
    emb_cube = emb_scale * emb_scale * emb_scale
    grad_hidden = gain_hidden_cols * input_grad / hidden_scale - hidden_cols * hidden_dot / (
        width * hidden_cube
    )
    grad_emb = gain_emb_cols * input_grad / emb_scale - emb_cols * emb_dot / (width * emb_cube)
    return moe_out, grad_gate, grad_hidden.astype(BF), grad_emb.astype(BF)


def solution(mesh):
    in_specs = (
        P("ep", None),
        P("ep", "pp"),
        P("ep", None),
        P("ep", None),
        P(),
        P(),
        P("ep", None, "pp"),
        P("ep", None, "pp"),
        P("ep", "pp", None),
        P("ep", "pp"),
    )
    out_specs = (P("ep", "pp"), P("ep", None), P("ep", "pp"), P("ep", "pp"))
    return jax.shard_map(
        per_device, mesh=mesh, in_specs=in_specs, out_specs=out_specs, check_vma=False
    )
```

time: 367 us -> 336 us (0.916)
  blocking collectives: 130 us -> 0 us
  Pallas kernels: 0 us -> 83.5 us
  starting transfers between devices: 16.2 us -> 87.3 us
  matrix products: 61.3 us -> 24.4 us
  waiting for transfers between devices: 128 us -> 107 us
  local copies, waits for them, and re-layouts: 4.73 us -> 22.3 us
  between operations: 14 us -> 1.63 us
  other arithmetic: 11.9 us -> 8.01 us
    all_to_all x2 -> x0, blocking collectives: 121 us -> none  [the longest x1 88.1 us: per_device(): lax.all_to_all(send_rows, 'ep', split_axis=0, concat_axis=0, tiled=True)]
    ppermute x0 -> x33, waiting for transfers between devices: none -> 85.9 us  [shift(): lax.ppermute(value, 'pp', [(i, (i + step) % ring) for i in range(ring)])]
    pallas_call x0 -> x29, Pallas kernels: none -> 83.5 us  [the longest x2 20 us: forward(): pl.pallas_call(body, grid=(width // depth,), out_shape=[jax.ShapeDtypeStr...]
    reduce_scatter x2 -> x0, waiting for transfers between devices: 80.7 us -> none  [the longest x1 41.5 us: per_device(): lax.psum_scatter(input_part.astype(jnp.bfloat16), 'pp', scatter_dimension...]
    ppermute x0 -> x33, starting transfers between devices: none -> 50.6 us  [shift(): lax.ppermute(value, 'pp', [(i, (i + step) % ring) for i in range(ring)])]
    dot_general x11 -> x10, matrix products: 61.3 us -> 24.4 us  [dot(): lax.dot_general(left, right, (dims, ((), ())), preferred_element_type=F32)]
    all_to_all x2 -> x5, waiting for transfers between devices: 46.1 us -> 21 us  [exchange(): return lax.all_to_all(value, 'ep', split_axis=0, concat_axis=0, tiled=True)]
    all_to_all x2 -> x5, starting transfers between devices: 15.8 us -> 36.7 us  [exchange(): return lax.all_to_all(value, 'ep', split_axis=0, concat_axis=0, tiled=True)]
  transfers between devices with their start and end apart: 6 -> 38, of which waited for: 4 -> 14; matrix products, arithmetic and copies ran while one was open for 19% -> 10% of each run, Pallas kernels for 0% -> 23%
where the time goes in v1:
time: 336 us; the launch traced here: 334 us
  waiting for transfers between devices  107 us (32%)
  starting transfers between devices  87.3 us (26%)
  Pallas kernels  83.5 us (25%)
  matrix products  24.4 us (7%)
  local copies, waits for them, and re-layouts  22.3 us (7%)
  other arithmetic  8.01 us (2%)
    ppermute x33, waiting for transfers between devices, shift(): lax.ppermute(value, 'pp', [(i, (i + step) % ring) for i in range(ring)])  85.9 us
    ppermute x33, starting transfers between devices, shift(): lax.ppermute(value, 'pp', [(i, (i + step) % ring) for i in range(ring)])  50.6 us
    all_to_all x5, starting transfers between devices, exchange(): return lax.all_to_all(value, 'ep', split_axis=0, concat_axis=0, tiled=True)  36.7 us
    dot_general x10, matrix products, dot(): lax.dot_general(left, right, (dims, ((), ())), preferred_element_type=F32)  24.4 us
    all_to_all x5, waiting for transfers between devices, exchange(): return lax.all_to_all(value, 'ep', split_axis=0, concat_axis=0, tiled=True)  21 us
    pallas_call x2, Pallas kernels, forward(): pl.pallas_call(body, grid=(width // depth,), out_shape=[jax.ShapeDtypeStr...  20 us
    unnamed x116, local copies, waits for them, and re-layouts  16.5 us
    pallas_call x2, Pallas kernels, backward_rest(): pl.pallas_call(body, grid_spec=pltpu.PrefetchScalarGridSpec(num_scalar_pr...  16.4 us
  transfers between devices with their start and end apart: 38, of which 14 were waited for; matrix products, arithmetic and copies ran while one was open for 10% of the time, Pallas kernels for 23%

profile of v1, /device:TPU:0, one launch (start us, length us, event | category | flops | bytes accessed | tf_op | source)
XLA Modules:
  0.0 334.0 jit_solution(13089133628858082445)
XLA Ops:
  0.6 2.9 collective-permute-start
  5.7 2.2 shard_map.130.refs_2_
  7.9 2.9 collective-permute-start.6
  13.1 2.0 multiply_convert_fusion.refs_0_
  15.1 8.5 %all-to-all-start.1 = ((bf16[32,16,1792]{2,1,0:T(8,128)(2,1)}), bf16[32,16,1792]{2,1,0:T(8,128)(2,1)S(1)}, u32[]{:S(2)}, u32[]{:S(2)}) async-start(bf16[32,16,1792]{2,1,0:T(8,128)(2,1)} %bitcast.83), calls=%async_computation.1 | async-start | bytes 3670016 | tf_op jit(solution)/shard_map/all_to_all | solution.py:353
  23.5 1.9 fusion
  26.5 1.7 collective-permute-start.3
  30.7 7.4 %collective-permute-done.3 = bf16[64,1792]{1,0:T(8,128)(2,1)S(1)} collective-permute-done((bf16[64,1792]{1,0:T(8,128)(2,1)S(1)}, bf16[64,1792]{1,0:T(8,128)(2,1)S(1)}, u32[]{:S(2)}, u32[]{:S(2)}) %collective-permute-start.3) | collective-permute-done | bytes 229408 | tf_op jit(solution)/shard_map/ppermute | solution.py:19
  38.1 3.4 %collective-permute-done.2 = bf16[64,1792]{1,0:T(8,128)(2,1)S(1)} collective-permute-done((bf16[64,1792]{1,0:T(8,128)(2,1)S(1)}, bf16[64,1792]{1,0:T(8,128)(2,1)S(1)}, u32[]{:S(2)}, u32[]{:S(2)}) %collective-permute-start.2) | collective-permute-done | bytes 229408 | tf_op jit(solution)/shard_map/ppermute | solution.py:19
  45.9 3.2 collective-permute-start.7
  51.4 3.1 convolution_convert_fusion.1.refs_0_
  54.5 1.5 shard_map.131.refs_3_
  57.3 1.5 shard_map.132.refs_4_
  60.1 8.2 %collective-permute-done.5.refs_1_.refs_0_.refs_3_ = bf16[256,1792]{1,0:T(8,128)(2,1)S(1)} collective-permute-done((bf16[256,1792]{1,0:T(8,128)(2,1)}, bf16[256,1792]{1,0:T(8,128)(2,1)S(1)}, u32[]{:S(2)}, u32[]{:S(2)}) %collective-permute-start.5) | collective-permute-done | bytes 917536 | tf_op jit(solution)/shard_map/ppermute | solution.py:19
  69.3 8.4 %all-to-all-start = ((bf16[32,8,7168]{2,1,0:T(8,128)(2,1)}), bf16[32,8,7168]{2,1,0:T(8,128)(2,1)}, u32[]{:S(2)}, u32[]{:S(2)}) async-start(bf16[32,8,7168]{2,1,0:T(8,128)(2,1)} %bitcast.81), calls=%async_computation | async-start | bytes 7340032 | tf_op jit(solution)/shard_map/all_to_all | solution.py:353
  77.7 2.1 collective-permute-start.8
  79.9 4.5 %convolution_convert_fusion.refs_0_ = bf16[256,7168]{1,0:T(8,128)(2,1)} fusion(bf16[128,7168]{1,0:T(8,128)(2,1)} %copy-done.35, s32[256]{0:T(256)S(1)} %iota_add_fusion, s32[128]{0:T(128)S(1)} %get-tuple-element.84, s32[128]{0:T(128)S(1)} %get-tuple-element.83), kind=kOutput, calls=%fused_computation | convolution fusion | flops 471695360 | bytes 5507072 | tf_op jit(solution)/shard_map/dot_general | solution.py:14
  84.4 1.5 shard_map.140.refs_0_
  87.2 2.1 fusion.57.refs_0_.refs_5_
  89.3 2.9 shard_map.137
  93.6 26.6 %collective-permute-done.8.refs_0_.refs_1_ = bf16[512,1792]{1,0:T(8,128)(2,1)} collective-permute-done((bf16[512,1792]{1,0:T(8,128)(2,1)}, bf16[512,1792]{1,0:T(8,128)(2,1)}, u32[]{:S(2)}, u32[]{:S(2)}) %collective-permute-start.8) | collective-permute-done | bytes 1835040 | tf_op jit(solution)/shard_map/ppermute | solution.py:19
  120.2 3.0 collective-permute-done.9.refs_0_.refs_2_
  123.2 2.2 all-to-all-done
  125.4 5.4 %all-to-all-start.2 = ((bf16[32,8,7168]{2,1,0:T(8,128)(2,1)}), bf16[32,8,7168]{2,1,0:T(8,128)(2,1)}, u32[]{:S(2)}, u32[]{:S(2)}) async-start(bf16[32,8,7168]{2,1,0:T(8,128)(2,1)} %bitcast.82), calls=%async_computation.2 | async-start | bytes 7340032 | tf_op jit(solution)/shard_map/all_to_all | solution.py:353
  130.9 3.2 collective-permute-start.11
  134.1 2.9 shard_map.135
  137.0 2.9 shard_map.136
  140.8 3.0 collective-permute-start.15
  143.8 10.0 %shard_map.139 = (f32[256,512]{1,0:T(8,128)S(1)}, f32[256,512]{1,0:T(8,128)S(1)}, bf16[256,512]{1,0:T(8,128)(2,1)S(1)}) custom-call(bf16[256,7168]{1,0:T(8,128)(2,1)} %bitcast.7.rows_ref, bf16[7168,512]{1,0:T(8,128)(2,1)} %bitcast.64, bf16[7168,512]{1,0:T(8,128)(2,1)} %bitcast.70, bf16[512,512]{1,0:T(8,128)(2,1)S(1)} %get-tuple-element.42.refs_0_, ...), custom_call_target="tpu_custom_call" | custom-call | tf_op jit(solution)/shard_map/pallas_call | solution.py:208
  154.5 3.3 %collective-permute-done.14 = bf16[512,512]{1,0:T(8,128)(2,1)} collective-permute-done((bf16[512,512]{1,0:T(8,128)(2,1)S(1)}, bf16[512,512]{1,0:T(8,128)(2,1)}, u32[]{:S(2)}, u32[]{:S(2)}) %collective-permute-start.14) | collective-permute-done | bytes 524320 | tf_op jit(solution)/shard_map/ppermute | solution.py:19
  157.9 1.6 convert_add_fusion
  159.4 4.4 %shard_map.142 = (bf16[256,512]{1,0:T(8,128)(2,1)S(1)}, bf16[256,512]{1,0:T(8,128)(2,1)S(1)}, bf16[128,1792]{1,0:T(8,128)(2,1)}, bf16[128,1792]{1,0:T(8,128)(2,1)}) custom-call(s32[1]{0:T(128)} %bitcast.4.here_ref, f32[256,512]{1,0:T(8,128)S(1)} %get-tuple-element.45.gate_pre_ref, f32[256,512]{1,0:T(8,128)S(1)} %get-tuple-element.46.up_ref, ...), custom_call_target="tpu_custom_call" | custom-call | tf_op jit(solution)/shard_map/pallas_call | solution.py:248
  163.8 3.2 collective-permute-start.19
  167.1 3.2 collective-permute-start.12
  170.3 8.2 %shard_map.143 = (bf16[256,1792]{1,0:T(8,128)(2,1)S(1)}, bf16[256,1792]{1,0:T(8,128)(2,1)S(1)}, bf16[256,1792]{1,0:T(8,128)(2,1)S(1)}) custom-call(s32[1]{0:T(128)} %bitcast.4.here_ref, bf16[256,512]{1,0:T(8,128)(2,1)S(1)} %get-tuple-element.47.ggp, bf16[256,512]{1,0:T(8,128)(2,1)S(1)} %get-tuple-element.48.gup, bf16[7168,512]{1,0:T(8,128)(2,1)} %bitcast.66, ...), custom_call_target="tpu_custom_call" | custom-call | tf_op jit(solution)/shard_map/pallas_call | solution.py:298
  178.5 2.7 collective-permute-done.13.array_ref.a3
  182.7 2.6 collective-permute-start.17
  185.3 10.0 %shard_map.147 = (f32[256,512]{1,0:T(8,128)S(1)}, f32[256,512]{1,0:T(8,128)S(1)}, bf16[256,512]{1,0:T(8,128)(2,1)S(1)}) custom-call(bf16[256,7168]{1,0:T(8,128)(2,1)} %bitcast.17.rows_ref, bf16[7168,512]{1,0:T(8,128)(2,1)} %bitcast.67, bf16[7168,512]{1,0:T(8,128)(2,1)} %bitcast.73, bf16[256,1792]{1,0:T(8,128)(2,1)S(1)} %get-tuple-element.49.refs_0_.up_ref), custom_call_target="tpu_custom_call" | custom-call | tf_op jit(solution)/shard_map/pallas_call | solution.py:208
  195.4 1.5 shard_map.148
  197.0 3.2 collective-permute-start.21
  200.3 3.5 %shard_map.149 = (bf16[256,512]{1,0:T(8,128)(2,1)S(1)}, bf16[256,512]{1,0:T(8,128)(2,1)S(1)}, bf16[128,1792]{1,0:T(8,128)(2,1)S(1)}, bf16[128,1792]{1,0:T(8,128)(2,1)S(1)}) custom-call(s32[1]{0:T(128)} %bitcast.4.here_ref, f32[256,512]{1,0:T(8,128)S(1)} %get-tuple-element.50.gate_pre_ref, f32[256,512]{1,0:T(8,128)S(1)} %get-tuple-element.51.up_ref, ...), custom_call_target="tpu_custom_call" | custom-call | tf_op jit(solution)/shard_map/pallas_call | solution.py:248
  203.9 3.2 collective-permute-start.23
  209.0 6.5 %shard_map.150.left_ref = bf16[256,1792]{1,0:T(8,128)(2,1)S(1)} custom-call(bf16[256,512]{1,0:T(8,128)(2,1)S(1)} %copy-done.16, bf16[256,512]{1,0:T(8,128)(2,1)S(1)} %copy-done.20, bf16[256,512]{1,0:T(8,128)(2,1)S(1)} %copy-done.18, bf16[128,512]{1,0:T(8,128)(2,1)S(1)} %copy-done.24, bf16[128,512]{1,0:T(8,128)(2,1)S(1)} %copy-done.26, ...), custom_call_target="tpu_custom_call" | custom-call | tf_op jit(solution)/shard_map/pallas_call | solution.py:339
  215.5 11.4 %collective-permute-done.22.refs_0_.below_ref = bf16[128,1792]{1,0:T(8,128)(2,1)S(1)} collective-permute-done((bf16[128,1792]{1,0:T(8,128)(2,1)S(1)}, bf16[128,1792]{1,0:T(8,128)(2,1)S(1)}, u32[]{:S(2)}, u32[]{:S(2)}) %collective-permute-start.22) | collective-permute-done | bytes 458784 | tf_op jit(solution)/shard_map/ppermute | solution.py:19
  227.9 4.0 %shard_map.151 = bf16[256,3584]{1,0:T(8,128)(2,1)} custom-call(bf16[256,1792]{1,0:T(8,128)(2,1)S(1)} %shard_map.150.left_ref, bf16[256,1792]{1,0:T(8,128)(2,1)S(1)} %copy-done.22, bf16[256,1792]{1,0:T(8,128)(2,1)S(1)} %collective-permute-done.20.b_ref, bf16[256,1792]{1,0:T(8,128)(2,1)} %copy-done.42, ...), custom_call_target="tpu_custom_call" | custom-call | tf_op jit(solution)/shard_map/pallas_call | solution.py:100
  231.9 7.2 %all-to-all-start.3 = ((bf16[32,8,3584]{2,1,0:T(8,128)(2,1)}), bf16[32,8,3584]{2,1,0:T(8,128)(2,1)}, u32[]{:S(2)}, u32[]{:S(2)}) async-start(bf16[32,8,3584]{2,1,0:T(8,128)(2,1)} %bitcast.84), calls=%async_computation.3 | async-start | bytes 3670016 | tf_op jit(solution)/shard_map/all_to_all | solution.py:353
  239.2 3.2 collective-permute-start.24
  243.4 8.2 %shard_map.152 = (bf16[256,1792]{1,0:T(8,128)(2,1)S(1)}, bf16[256,1792]{1,0:T(8,128)(2,1)S(1)}, bf16[256,1792]{1,0:T(8,128)(2,1)S(1)}) custom-call(s32[1]{0:T(128)} %bitcast.4.here_ref, bf16[256,512]{1,0:T(8,128)(2,1)S(1)} %copy-done.28, bf16[256,512]{1,0:T(8,128)(2,1)S(1)} %copy-done.30, bf16[7168,512]{1,0:T(8,128)(2,1)} %bitcast.69, bf16[7168,512]{1,0:T(8,128)(2,1)} %bitcast.75), custom_call_target="tpu_custom_call" | custom-call | tf_op jit(solution)/shard_map/pallas_call | solution.py:298
  251.7 3.3 collective-permute-start.27
  255.0 3.0 collective-permute-done.26.refs_0_.a2_low
  258.6 3.2 collective-permute-start.29
  261.9 6.5 %shard_map.156.left_ref = bf16[256,1792]{1,0:T(8,128)(2,1)S(1)} custom-call(bf16[256,512]{1,0:T(8,128)(2,1)S(1)} %get-tuple-element.55.refs_2_.a0, bf16[256,512]{1,0:T(8,128)(2,1)S(1)} %collective-permute-done.24.array_ref.a1, bf16[256,512]{1,0:T(8,128)(2,1)S(1)} %collective-permute-done.25.array_ref.a3, ...), custom_call_target="tpu_custom_call" | custom-call | tf_op jit(solution)/shard_map/pallas_call | solution.py:339
  268.4 12.6 %collective-permute-done.28.b_ref = bf16[256,1792]{1,0:T(8,128)(2,1)S(1)} collective-permute-done((bf16[256,1792]{1,0:T(8,128)(2,1)S(1)}, bf16[256,1792]{1,0:T(8,128)(2,1)S(1)}, u32[]{:S(2)}, u32[]{:S(2)}) %collective-permute-start.28) | collective-permute-done | bytes 917536 | tf_op jit(solution)/shard_map/ppermute | solution.py:19
  281.0 2.4 shard_map.157
  283.4 7.2 %all-to-all-start.4 = ((bf16[32,8,3584]{2,1,0:T(8,128)(2,1)}), bf16[32,8,3584]{2,1,0:T(8,128)(2,1)}, u32[]{:S(2)}, u32[]{:S(2)}) async-start(bf16[32,8,3584]{2,1,0:T(8,128)(2,1)} %bitcast.85), calls=%async_computation.4 | async-start | bytes 3670016 | tf_op jit(solution)/shard_map/all_to_all | solution.py:353
  292.2 1.5 fusion.21
  293.7 2.4 fusion.23
  296.2 2.5 fusion.17
  298.7 18.8 %all-to-all-done.4 = bf16[32,8,3584]{2,1,0:T(8,128)(2,1)} async-done(((bf16[32,8,3584]{2,1,0:T(8,128)(2,1)}), bf16[32,8,3584]{2,1,0:T(8,128)(2,1)}, u32[]{:S(2)}, u32[]{:S(2)}) %all-to-all-start.4) | async-done | bytes 1835040 | tf_op jit(solution)/shard_map/all_to_all | solution.py:353
  317.5 1.6 convolution_add_fusion.1
  319.2 2.8 fusion.6
  322.0 1.8 fusion.8
  323.8 3.1 collective-permute-start.32
  328.2 3.8 %collective-permute-done.31 = f32[4,128]{1,0:T(4,128)S(1)} collective-permute-done((f32[4,128]{1,0:T(4,128)S(1)}, f32[4,128]{1,0:T(4,128)S(1)}, u32[]{:S(2)}, u32[]{:S(2)}) %collective-permute-start.31) | collective-permute-done | bytes 2080 | tf_op jit(solution)/shard_map/ppermute | solution.py:19
  (203 shorter events, 33.2 us)
Async XLA Ops:
  0.6 24.9 %collective-permute-start = (bf16[128,1792]{1,0:T(8,128)(2,1)}, bf16[128,1792]{1,0:T(8,128)(2,1)}, u32[]{:S(2)}, u32[]{:S(2)}) collective-permute-start(bf16[128,1792]{1,0:T(8,128)(2,1)} %param.11), channel_id=1, source_target_pairs={{0,96},{32,0},{64,32},{96,64},{1,97},{33,1},{65,33},{97,65},{2,98}... | collective-permute-start | bytes 1376264 | tf_op jit(solution)/shard_map/ppermute | solution.py:19
  3.5 24.7 %collective-permute-start.1 = (bf16[128,1792]{1,0:T(8,128)(2,1)}, bf16[128,1792]{1,0:T(8,128)(2,1)}, u32[]{:S(2)}, u32[]{:S(2)}) collective-permute-start(bf16[128,1792]{1,0:T(8,128)(2,1)} %param.11), channel_id=1, source_target_pairs={{0,32},{32,64},{64,96},{96,0},{1,33},{33,65},{65,97},{97,1},{2,34}... | collective-permute-start | bytes 1376264 | tf_op jit(solution)/shard_map/ppermute | solution.py:19
  4.8 7.5 %copy-start.54 = (f32[128,2]{0,1:T(2,128)S(1)}, f32[128,2]{0,1:T(2,128)}, u32[]{:S(2)}) copy-start(f32[128,2]{0,1:T(2,128)} %param.13) | copy-start | bytes 3076
  4.8 8.2 %copy-start.41 = (bf16[128,1792]{1,0:T(8,128)(2,1)S(1)}, bf16[128,1792]{1,0:T(8,128)(2,1)}, u32[]{:S(2)}) copy-start(bf16[128,1792]{1,0:T(8,128)(2,1)} %param.19) | copy-start | bytes 1376260
  4.8 41.1 %collective-permute-start.4 = (bf16[256,1792]{1,0:T(8,128)(2,1)S(1)}, bf16[256,1792]{1,0:T(8,128)(2,1)}, u32[]{:S(2)}, u32[]{:S(2)}) collective-permute-start(bf16[256,1792]{1,0:T(8,128)(2,1)S(1)} %shard_map.129.refs_1_), channel_id=1, source_target_pairs={{0,32},{32,64},{64,96},{96,0},{1,33},{33,65},{65,97},{97,1},{2,34}... | collective-permute-start | bytes 2752520 | tf_op jit(solution)/shard_map/ppermute | solution.py:19
  7.9 38.1 %collective-permute-start.6 = (bf16[256,1792]{1,0:T(8,128)(2,1)}, bf16[256,1792]{1,0:T(8,128)(2,1)}, u32[]{:S(2)}, u32[]{:S(2)}) collective-permute-start(bf16[256,1792]{1,0:T(8,128)(2,1)} %shard_map.130.refs_2_), channel_id=1, source_target_pairs={{0,96},{32,0},{64,32},{96,64},{1,97},{33,1},{65,33},{97,65},{2,98}... | collective-permute-start | bytes 2752520 | tf_op jit(solution)/shard_map/ppermute | solution.py:19
  15.1 10.4 %copy-start.38 = (bf16[128,1792]{1,0:T(8,128)(2,1)S(1)}, bf16[128,1792]{1,0:T(8,128)(2,1)}, u32[]{:S(2)}) copy-start(bf16[128,1792]{1,0:T(8,128)(2,1)} %param.11) | copy-start | bytes 1376260
  15.1 54.2 %all-to-all-start.1 = ((bf16[32,16,1792]{2,1,0:T(8,128)(2,1)}), bf16[32,16,1792]{2,1,0:T(8,128)(2,1)S(1)}, u32[]{:S(2)}, u32[]{:S(2)}) async-start(bf16[32,16,1792]{2,1,0:T(8,128)(2,1)} %bitcast.83), calls=%async_computation.1 | async-start | bytes 3670016 | tf_op jit(solution)/shard_map/all_to_all | solution.py:353
  26.5 11.6 %collective-permute-start.3 = (bf16[64,1792]{1,0:T(8,128)(2,1)S(1)}, bf16[64,1792]{1,0:T(8,128)(2,1)S(1)}, u32[]{:S(2)}, u32[]{:S(2)}) collective-permute-start(bf16[64,1792]{1,0:T(8,128)(2,1)S(1)} %slice.74), channel_id=1, source_target_pairs={{0,96},{32,0},{64,32},{96,64},{1,97},{33,1},{65,33},{97,65},{2,98}... | collective-permute-start | bytes 688136 | tf_op jit(solution)/shard_map/ppermute | solution.py:19
  29.2 12.3 %collective-permute-start.2 = (bf16[64,1792]{1,0:T(8,128)(2,1)S(1)}, bf16[64,1792]{1,0:T(8,128)(2,1)S(1)}, u32[]{:S(2)}, u32[]{:S(2)}) collective-permute-start(bf16[64,1792]{1,0:T(8,128)(2,1)S(1)} %slice.73), channel_id=1, source_target_pairs={{0,32},{32,64},{64,96},{96,0},{1,33},{33,65},{65,97},{97,1},{2,34}... | collective-permute-start | bytes 688136 | tf_op jit(solution)/shard_map/ppermute | solution.py:19
  30.7 18.5 %copy-start.36 = (bf16[128,7168]{1,0:T(8,128)(2,1)S(1)}, bf16[128,7168]{1,0:T(8,128)(2,1)}, u32[]{:S(2)}) copy-start(bf16[128,7168]{1,0:T(8,128)(2,1)} %param.10) | copy-start | bytes 5505028
  30.7 18.4 %copy-start.43 = (f32[7168]{0:T(1024)S(1)}, f32[7168]{0:T(1024)}, u32[]{:S(2)}) copy-start(f32[7168]{0:T(1024)} %param.14) | copy-start | bytes 86020
  30.7 18.4 %copy-start.44 = (f32[7168]{0:T(1024)S(1)}, f32[7168]{0:T(1024)}, u32[]{:S(2)}) copy-start(f32[7168]{0:T(1024)} %param.15) | copy-start | bytes 86020
  45.9 8.5 %copy-start.45 = (f32[128]{0:T(128)}, f32[128]{0:T(128)S(1)}, u32[]{:S(2)}) copy-start(f32[128]{0:T(128)S(1)} %get-tuple-element.90) | copy-start | bytes 1540
  45.9 22.3 %collective-permute-start.5 = (bf16[256,1792]{1,0:T(8,128)(2,1)}, bf16[256,1792]{1,0:T(8,128)(2,1)S(1)}, u32[]{:S(2)}, u32[]{:S(2)}) collective-permute-start(bf16[256,1792]{1,0:T(8,128)(2,1)} %collective-permute-done.4), channel_id=1, source_target_pairs={{0,32},{32,64},{64,96},{96,0},{1,33},{33,65},{65,97},{97,1},{2,34}... | collective-permute-start | bytes 2752520 | tf_op jit(solution)/shard_map/ppermute | solution.py:19
  45.9 22.3 %collective-permute-start.7 = (bf16[256,1792]{1,0:T(8,128)(2,1)}, bf16[256,1792]{1,0:T(8,128)(2,1)}, u32[]{:S(2)}, u32[]{:S(2)}) collective-permute-start(bf16[256,1792]{1,0:T(8,128)(2,1)} %collective-permute-done.6), channel_id=1, source_target_pairs={{0,96},{32,0},{64,32},{96,64},{1,97},{33,1},{65,33},{97,65},{2,98}... | collective-permute-start | bytes 2752520 | tf_op jit(solution)/shard_map/ppermute | solution.py:19
  69.3 16.7 %copy-start = (bf16[32,16,1792]{2,1,0:T(8,128)(2,1)}, bf16[32,16,1792]{2,1,0:T(8,128)(2,1)S(1)}, u32[]{:S(2)}) copy-start(bf16[32,16,1792]{2,1,0:T(8,128)(2,1)S(1)} %all-to-all-done.1) | copy-start | bytes 5505028
  69.3 56.1 %all-to-all-start = ((bf16[32,8,7168]{2,1,0:T(8,128)(2,1)}), bf16[32,8,7168]{2,1,0:T(8,128)(2,1)}, u32[]{:S(2)}, u32[]{:S(2)}) async-start(bf16[32,8,7168]{2,1,0:T(8,128)(2,1)} %bitcast.81), calls=%async_computation | async-start | bytes 7340032 | tf_op jit(solution)/shard_map/all_to_all | solution.py:353
  77.7 42.5 %collective-permute-start.8 = (bf16[512,1792]{1,0:T(8,128)(2,1)}, bf16[512,1792]{1,0:T(8,128)(2,1)}, u32[]{:S(2)}, u32[]{:S(2)}) collective-permute-start(bf16[512,1792]{1,0:T(8,128)(2,1)} %copy-done.8), channel_id=1, source_target_pairs={{0,96},{32,0},{64,32},{96,64},{1,97},{33,1},{65,33},{97,65},{2,98}... | collective-permute-start | bytes 5505032 | tf_op jit(solution)/shard_map/ppermute | solution.py:19
  79.9 43.4 %collective-permute-start.9 = (bf16[512,1792]{1,0:T(8,128)(2,1)}, bf16[512,1792]{1,0:T(8,128)(2,1)}, u32[]{:S(2)}, u32[]{:S(2)}) collective-permute-start(bf16[512,1792]{1,0:T(8,128)(2,1)} %copy-done.7), channel_id=1, source_target_pairs={{0,32},{32,64},{64,96},{96,0},{1,33},{33,65},{65,97},{97,1},{2,34}... | collective-permute-start | bytes 5505032 | tf_op jit(solution)/shard_map/ppermute | solution.py:19
  125.4 8.7 %copy-start.1 = (bf16[32,16,1792]{2,1,0:T(8,128)(2,1)S(1)}, bf16[32,16,1792]{2,1,0:T(8,128)(2,1)}, u32[]{:S(2)}) copy-start(bf16[32,16,1792]{2,1,0:T(8,128)(2,1)} %copy-done) | copy-start | bytes 5505028
  125.4 59.9 %all-to-all-start.2 = ((bf16[32,8,7168]{2,1,0:T(8,128)(2,1)}), bf16[32,8,7168]{2,1,0:T(8,128)(2,1)}, u32[]{:S(2)}, u32[]{:S(2)}) async-start(bf16[32,8,7168]{2,1,0:T(8,128)(2,1)} %bitcast.82), calls=%async_computation.2 | async-start | bytes 7340032 | tf_op jit(solution)/shard_map/all_to_all | solution.py:353
  130.8 9.7 %collective-permute-start.10 = (bf16[256,512]{1,0:T(8,128)(2,1)S(1)}, bf16[256,512]{1,0:T(8,128)(2,1)S(1)}, u32[]{:S(2)}, u32[]{:S(2)}) collective-permute-start(bf16[256,512]{1,0:T(8,128)(2,1)S(1)} %copy-done.34), channel_id=1, source_target_pairs={{0,32},{32,64},{64,96},{96,0},{1,33},{33,65},{65,97},{97,1},{2,34}... | collective-permute-start | bytes 786440 | tf_op jit(solution)/shard_map/ppermute | solution.py:19
  130.9 9.6 %collective-permute-start.11 = (bf16[256,512]{1,0:T(8,128)(2,1)S(1)}, bf16[256,512]{1,0:T(8,128)(2,1)S(1)}, u32[]{:S(2)}, u32[]{:S(2)}) collective-permute-start(bf16[256,512]{1,0:T(8,128)(2,1)S(1)} %copy-done.32), channel_id=1, source_target_pairs={{0,96},{32,0},{64,32},{96,64},{1,97},{33,1},{65,33},{97,65},{2,98}... | collective-permute-start | bytes 786440 | tf_op jit(solution)/shard_map/ppermute | solution.py:19
  140.8 13.7 %collective-permute-start.15 = (bf16[512,512]{1,0:T(8,128)(2,1)S(1)}, bf16[512,512]{1,0:T(8,128)(2,1)S(1)}, u32[]{:S(2)}, u32[]{:S(2)}) collective-permute-start(bf16[512,512]{1,0:T(8,128)(2,1)S(1)} %get-tuple-element.43.refs_1_), channel_id=1, source_target_pairs={{0,96},{32,0},{64,32},{96,64},{1,97},{33,1},{65,33},{97,65},{2,98}... | collective-permute-start | bytes 1572872 | tf_op jit(solution)/shard_map/ppermute | solution.py:19
  143.8 14.0 %collective-permute-start.14 = (bf16[512,512]{1,0:T(8,128)(2,1)S(1)}, bf16[512,512]{1,0:T(8,128)(2,1)}, u32[]{:S(2)}, u32[]{:S(2)}) collective-permute-start(bf16[512,512]{1,0:T(8,128)(2,1)S(1)} %get-tuple-element.42.refs_0_), channel_id=1, source_target_pairs={{0,32},{32,64},{64,96},{96,0},{1,33},{33,65},{65,97},{97,1},{2,34}... | collective-permute-start | bytes 1572872 | tf_op jit(solution)/shard_map/ppermute | solution.py:19
  159.4 7.6 %copy-start.15 = (bf16[256,512]{1,0:T(8,128)(2,1)S(1)}, bf16[256,512]{1,0:T(8,128)(2,1)}, u32[]{:S(2)}) copy-start(bf16[256,512]{1,0:T(8,128)(2,1)} %copy-done.14) | copy-start | bytes 786436
  163.8 31.6 %collective-permute-start.18 = (bf16[128,1792]{1,0:T(8,128)(2,1)}, bf16[128,1792]{1,0:T(8,128)(2,1)}, u32[]{:S(2)}, u32[]{:S(2)}) collective-permute-start(bf16[128,1792]{1,0:T(8,128)(2,1)} %get-tuple-element.53), channel_id=1, source_target_pairs={{0,32},{32,64},{64,96},{96,0},{1,33},{33,65},{65,97},{97,1},{2,34}... | collective-permute-start | bytes 1376264 | tf_op jit(solution)/shard_map/ppermute | solution.py:19
  163.8 31.6 %collective-permute-start.19 = (bf16[128,1792]{1,0:T(8,128)(2,1)}, bf16[128,1792]{1,0:T(8,128)(2,1)}, u32[]{:S(2)}, u32[]{:S(2)}) collective-permute-start(bf16[128,1792]{1,0:T(8,128)(2,1)} %get-tuple-element.54), channel_id=1, source_target_pairs={{0,96},{32,0},{64,32},{96,64},{1,97},{33,1},{65,33},{97,65},{2,98}... | collective-permute-start | bytes 1376264 | tf_op jit(solution)/shard_map/ppermute | solution.py:19
  167.1 14.2 %collective-permute-start.13 = (bf16[256,512]{1,0:T(8,128)(2,1)S(1)}, bf16[256,512]{1,0:T(8,128)(2,1)S(1)}, u32[]{:S(2)}, u32[]{:S(2)}) collective-permute-start(bf16[256,512]{1,0:T(8,128)(2,1)S(1)} %copy-done.15), channel_id=1, source_target_pairs={{0,32},{32,64},{64,96},{96,0},{1,33},{33,65},{65,97},{97,1},{2,34}... | collective-permute-start | bytes 786440 | tf_op jit(solution)/shard_map/ppermute | solution.py:19
  167.1 14.3 %collective-permute-start.12 = (bf16[256,512]{1,0:T(8,128)(2,1)S(1)}, bf16[256,512]{1,0:T(8,128)(2,1)S(1)}, u32[]{:S(2)}, u32[]{:S(2)}) collective-permute-start(bf16[256,512]{1,0:T(8,128)(2,1)S(1)} %copy-done.15), channel_id=1, source_target_pairs={{0,96},{32,0},{64,32},{96,64},{1,97},{33,1},{65,33},{97,65},{2,98}... | collective-permute-start | bytes 786440 | tf_op jit(solution)/shard_map/ppermute | solution.py:19
  181.3 14.1 %collective-permute-start.16 = (bf16[128,512]{1,0:T(8,128)(2,1)S(1)}, bf16[128,512]{1,0:T(8,128)(2,1)S(1)}, u32[]{:S(2)}, u32[]{:S(2)}) collective-permute-start(bf16[128,512]{1,0:T(8,128)(2,1)S(1)} %shard_map.144), channel_id=1, source_target_pairs={{0,32},{32,64},{64,96},{96,0},{1,33},{33,65},{65,97},{97,1},{2,34}... | collective-permute-start | bytes 393224 | tf_op jit(solution)/shard_map/ppermute | solution.py:19
  182.7 12.6 %collective-permute-start.17 = (bf16[128,512]{1,0:T(8,128)(2,1)}, bf16[128,512]{1,0:T(8,128)(2,1)S(1)}, u32[]{:S(2)}, u32[]{:S(2)}) collective-permute-start(bf16[128,512]{1,0:T(8,128)(2,1)} %shard_map.145), channel_id=1, source_target_pairs={{0,96},{32,0},{64,32},{96,64},{1,97},{33,1},{65,33},{97,65},{2,98}... | collective-permute-start | bytes 393224 | tf_op jit(solution)/shard_map/ppermute | solution.py:19
  195.4 8.4 %copy-start.23 = (bf16[128,512]{1,0:T(8,128)(2,1)}, bf16[128,512]{1,0:T(8,128)(2,1)S(1)}, u32[]{:S(2)}) copy-start(bf16[128,512]{1,0:T(8,128)(2,1)S(1)} %collective-permute-done.16.refs_0_.a2_low) | copy-start | bytes 393220
  195.4 8.4 %copy-start.25 = (bf16[128,512]{1,0:T(8,128)(2,1)}, bf16[128,512]{1,0:T(8,128)(2,1)S(1)}, u32[]{:S(2)}) copy-start(bf16[128,512]{1,0:T(8,128)(2,1)S(1)} %collective-permute-done.17.refs_1_.a2_high) | copy-start | bytes 393220
  196.9 30.0 %collective-permute-start.20 = (bf16[256,1792]{1,0:T(8,128)(2,1)S(1)}, bf16[256,1792]{1,0:T(8,128)(2,1)S(1)}, u32[]{:S(2)}, u32[]{:S(2)}) collective-permute-start(bf16[256,1792]{1,0:T(8,128)(2,1)S(1)} %get-tuple-element.56.refs_0_), channel_id=1, source_target_pairs={{0,32},{32,64},{64,96},{96,0},{1,33},{33,65},{65,97},{97,1},{2,34}... | collective-permute-start | bytes 2752520 | tf_op jit(solution)/shard_map/ppermute | solution.py:19
  197.0 29.9 %collective-permute-start.21 = (bf16[256,1792]{1,0:T(8,128)(2,1)S(1)}, bf16[256,1792]{1,0:T(8,128)(2,1)S(1)}, u32[]{:S(2)}, u32[]{:S(2)}) collective-permute-start(bf16[256,1792]{1,0:T(8,128)(2,1)S(1)} %get-tuple-element.57.refs_1_), channel_id=1, source_target_pairs={{0,96},{32,0},{64,32},{96,64},{1,97},{33,1},{65,33},{97,65},{2,98}... | collective-permute-start | bytes 2752520 | tf_op jit(solution)/shard_map/ppermute | solution.py:19
  200.2 6.9 %copy-start.18 = (bf16[256,512]{1,0:T(8,128)(2,1)S(1)}, bf16[256,512]{1,0:T(8,128)(2,1)}, u32[]{:S(2)}) copy-start(bf16[256,512]{1,0:T(8,128)(2,1)} %copy-done.17) | copy-start | bytes 786436
  200.3 6.9 %copy-start.20 = (bf16[256,512]{1,0:T(8,128)(2,1)S(1)}, bf16[256,512]{1,0:T(8,128)(2,1)}, u32[]{:S(2)}) copy-start(bf16[256,512]{1,0:T(8,128)(2,1)} %copy-done.19) | copy-start | bytes 786436
  203.8 11.7 %copy-start.27 = (bf16[256,512]{1,0:T(8,128)(2,1)}, bf16[256,512]{1,0:T(8,128)(2,1)S(1)}, u32[]{:S(2)}) copy-start(bf16[256,512]{1,0:T(8,128)(2,1)S(1)} %get-tuple-element.61.ggp) | copy-start | bytes 786436
  203.8 11.7 %copy-start.29 = (bf16[256,512]{1,0:T(8,128)(2,1)}, bf16[256,512]{1,0:T(8,128)(2,1)S(1)}, u32[]{:S(2)}) copy-start(bf16[256,512]{1,0:T(8,128)(2,1)S(1)} %get-tuple-element.62.gup) | copy-start | bytes 786436
  203.8 23.1 %collective-permute-start.22 = (bf16[128,1792]{1,0:T(8,128)(2,1)S(1)}, bf16[128,1792]{1,0:T(8,128)(2,1)S(1)}, u32[]{:S(2)}, u32[]{:S(2)}) collective-permute-start(bf16[128,1792]{1,0:T(8,128)(2,1)S(1)} %get-tuple-element.58.refs_5_), channel_id=1, source_target_pairs={{0,32},{32,64},{64,96},{96,0},{1,33},{33,65},{65,97},{97,1},{2,34}... | collective-permute-start | bytes 1376264 | tf_op jit(solution)/shard_map/ppermute | solution.py:19
  203.9 24.0 %copy-start.22 = (bf16[256,1792]{1,0:T(8,128)(2,1)S(1)}, bf16[256,1792]{1,0:T(8,128)(2,1)}, u32[]{:S(2)}) copy-start(bf16[256,1792]{1,0:T(8,128)(2,1)} %copy-done.21) | copy-start | bytes 2752516
  203.9 23.0 %collective-permute-start.23 = (bf16[128,1792]{1,0:T(8,128)(2,1)S(1)}, bf16[128,1792]{1,0:T(8,128)(2,1)S(1)}, u32[]{:S(2)}, u32[]{:S(2)}) collective-permute-start(bf16[128,1792]{1,0:T(8,128)(2,1)S(1)} %get-tuple-element.60), channel_id=1, source_target_pairs={{0,96},{32,0},{64,32},{96,64},{1,97},{33,1},{65,33},{97,65},{2,98}... | collective-permute-start | bytes 1376264 | tf_op jit(solution)/shard_map/ppermute | solution.py:19
  227.9 14.5 %copy-start.28 = (bf16[256,512]{1,0:T(8,128)(2,1)S(1)}, bf16[256,512]{1,0:T(8,128)(2,1)}, u32[]{:S(2)}) copy-start(bf16[256,512]{1,0:T(8,128)(2,1)} %copy-done.27) | copy-start | bytes 786436
  231.9 51.5 %all-to-all-start.3 = ((bf16[32,8,3584]{2,1,0:T(8,128)(2,1)}), bf16[32,8,3584]{2,1,0:T(8,128)(2,1)}, u32[]{:S(2)}, u32[]{:S(2)}) async-start(bf16[32,8,3584]{2,1,0:T(8,128)(2,1)} %bitcast.84), calls=%async_computation.3 | async-start | bytes 3670016 | tf_op jit(solution)/shard_map/all_to_all | solution.py:353
  239.1 12.5 %collective-permute-start.25 = (bf16[256,512]{1,0:T(8,128)(2,1)S(1)}, bf16[256,512]{1,0:T(8,128)(2,1)S(1)}, u32[]{:S(2)}, u32[]{:S(2)}) collective-permute-start(bf16[256,512]{1,0:T(8,128)(2,1)S(1)} %get-tuple-element.55.refs_2_.a0), channel_id=1, source_target_pairs={{0,32},{32,64},{64,96},{96,0},{1,33},{33,65},{65,97},{97,1},{2,34}... | collective-permute-start | bytes 786440 | tf_op jit(solution)/shard_map/ppermute | solution.py:19
  239.2 12.5 %collective-permute-start.24 = (bf16[256,512]{1,0:T(8,128)(2,1)S(1)}, bf16[256,512]{1,0:T(8,128)(2,1)S(1)}, u32[]{:S(2)}, u32[]{:S(2)}) collective-permute-start(bf16[256,512]{1,0:T(8,128)(2,1)S(1)} %get-tuple-element.55.refs_2_.a0), channel_id=1, source_target_pairs={{0,96},{32,0},{64,32},{96,64},{1,97},{33,1},{65,33},{97,65},{2,98}... | collective-permute-start | bytes 786440 | tf_op jit(solution)/shard_map/ppermute | solution.py:19
  243.4 14.7 %copy-start.13 = (bf16[128,1792]{1,0:T(8,128)(2,1)S(1)}, bf16[128,1792]{1,0:T(8,128)(2,1)}, u32[]{:S(2)}) copy-start(bf16[128,1792]{1,0:T(8,128)(2,1)} %copy-done.12) | copy-start | bytes 1376260
  251.6 6.4 %collective-permute-start.26 = (bf16[128,512]{1,0:T(8,128)(2,1)S(1)}, bf16[128,512]{1,0:T(8,128)(2,1)S(1)}, u32[]{:S(2)}, u32[]{:S(2)}) collective-permute-start(bf16[128,512]{1,0:T(8,128)(2,1)S(1)} %shard_map.153), channel_id=1, source_target_pairs={{0,32},{32,64},{64,96},{96,0},{1,33},{33,65},{65,97},{97,1},{2,34}... | collective-permute-start | bytes 393224 | tf_op jit(solution)/shard_map/ppermute | solution.py:19
  251.7 6.3 %collective-permute-start.27 = (bf16[128,512]{1,0:T(8,128)(2,1)S(1)}, bf16[128,512]{1,0:T(8,128)(2,1)S(1)}, u32[]{:S(2)}, u32[]{:S(2)}) collective-permute-start(bf16[128,512]{1,0:T(8,128)(2,1)S(1)} %shard_map.154), channel_id=1, source_target_pairs={{0,96},{32,0},{64,32},{96,64},{1,97},{33,1},{65,33},{97,65},{2,98}... | collective-permute-start | bytes 393224 | tf_op jit(solution)/shard_map/ppermute | solution.py:19
  258.6 22.5 %collective-permute-start.28 = (bf16[256,1792]{1,0:T(8,128)(2,1)S(1)}, bf16[256,1792]{1,0:T(8,128)(2,1)S(1)}, u32[]{:S(2)}, u32[]{:S(2)}) collective-permute-start(bf16[256,1792]{1,0:T(8,128)(2,1)S(1)} %get-tuple-element.65.refs_5_), channel_id=1, source_target_pairs={{0,32},{32,64},{64,96},{96,0},{1,33},{33,65},{65,97},{97,1},{2,34}... | collective-permute-start | bytes 2752520 | tf_op jit(solution)/shard_map/ppermute | solution.py:19
  258.6 22.4 %collective-permute-start.29 = (bf16[256,1792]{1,0:T(8,128)(2,1)S(1)}, bf16[256,1792]{1,0:T(8,128)(2,1)S(1)}, u32[]{:S(2)}, u32[]{:S(2)}) collective-permute-start(bf16[256,1792]{1,0:T(8,128)(2,1)S(1)} %get-tuple-element.66.refs_6_), channel_id=1, source_target_pairs={{0,96},{32,0},{64,32},{96,64},{1,97},{33,1},{65,33},{97,65},{2,98}... | collective-permute-start | bytes 2752520 | tf_op jit(solution)/shard_map/ppermute | solution.py:19
  283.4 34.1 %all-to-all-start.4 = ((bf16[32,8,3584]{2,1,0:T(8,128)(2,1)}), bf16[32,8,3584]{2,1,0:T(8,128)(2,1)}, u32[]{:S(2)}, u32[]{:S(2)}) async-start(bf16[32,8,3584]{2,1,0:T(8,128)(2,1)} %bitcast.85), calls=%async_computation.4 | async-start | bytes 3670016 | tf_op jit(solution)/shard_map/all_to_all | solution.py:353
  293.7 25.4 %copy-start.48 = (f32[128]{0:T(128)S(1)}, f32[128]{0:T(128)}, u32[]{:S(2)}) copy-start(f32[128]{0:T(128)} %copy-done.47) | copy-start | bytes 1540
  293.7 25.4 %copy-start.50 = (f32[128]{0:T(128)S(1)}, f32[128]{0:T(128)}, u32[]{:S(2)}) copy-start(f32[128]{0:T(128)} %copy-done.49) | copy-start | bytes 1540
  298.7 23.3 %copy-start.37 = (bf16[128,7168]{1,0:T(8,128)(2,1)S(1)}, bf16[128,7168]{1,0:T(8,128)(2,1)}, u32[]{:S(2)}) copy-start(bf16[128,7168]{1,0:T(8,128)(2,1)} %param.10) | copy-start | bytes 5505028
  298.7 23.3 %copy-start.39 = (bf16[128,1792]{1,0:T(8,128)(2,1)S(1)}, bf16[128,1792]{1,0:T(8,128)(2,1)}, u32[]{:S(2)}) copy-start(bf16[128,1792]{1,0:T(8,128)(2,1)} %param.11) | copy-start | bytes 1376260
  319.2 13.4 %copy-start.46 = (f32[128]{0:T(128)S(1)}, f32[128]{0:T(128)}, u32[]{:S(2)}) copy-start(f32[128]{0:T(128)} %copy-done.45) | copy-start | bytes 1540
  319.2 13.4 %copy-start.52 = (f32[128]{0:T(128)S(1)}, f32[128]{0:T(128)}, u32[]{:S(2)}) copy-start(f32[128]{0:T(128)} %get-tuple-element.87) | copy-start | bytes 1540
  319.2 13.4 %copy-start.53 = (f32[128]{0:T(128)S(1)}, f32[128]{0:T(128)}, u32[]{:S(2)}) copy-start(f32[128]{0:T(128)} %get-tuple-element.91) | copy-start | bytes 1540
  323.8 4.4 %collective-permute-start.32 = (f32[4,128]{1,0:T(4,128)S(1)}, f32[4,128]{1,0:T(4,128)S(1)}, u32[]{:S(2)}, u32[]{:S(2)}) collective-permute-start(f32[4,128]{1,0:T(4,128)S(1)} %pad_maximum_fusion.3), channel_id=1, source_target_pairs={{0,96},{32,0},{64,32},{96,64},{1,97},{33,1},{65,33},{97,65},{2,98}... | collective-permute-start | bytes 6152 | tf_op jit(solution)/shard_map/ppermute | solution.py:19
  326.9 5.1 %collective-permute-start.31 = (f32[4,128]{1,0:T(4,128)S(1)}, f32[4,128]{1,0:T(4,128)S(1)}, u32[]{:S(2)}, u32[]{:S(2)}) collective-permute-start(f32[4,128]{1,0:T(4,128)S(1)} %pad_maximum_fusion.3), channel_id=1, source_target_pairs={{0,64},{32,96},{64,0},{96,32},{1,65},{33,97},{65,1},{97,33},{2,66}... | collective-permute-start | bytes 6152 | tf_op jit(solution)/shard_map/ppermute | solution.py:19
  327.1 4.9 %collective-permute-start.30 = (f32[4,128]{1,0:T(4,128)S(1)}, f32[4,128]{1,0:T(4,128)S(1)}, u32[]{:S(2)}, u32[]{:S(2)}) collective-permute-start(f32[4,128]{1,0:T(4,128)S(1)} %pad_maximum_fusion.3), channel_id=1, source_target_pairs={{0,32},{32,64},{64,96},{96,0},{1,33},{33,65},{65,97},{97,1},{2,34}... | collective-permute-start | bytes 6152 | tf_op jit(solution)/shard_map/ppermute | solution.py:19
  (29 other events, 71.4 us)

commit v2 on v1

--- a/solution.py
+++ b/solution.py
@@ -48,80 +48,100 @@
 
 
 def add_halves(up, down, from_below, from_above, *others):
-    rows, width = from_below.shape
+    rows, extended = from_below.shape
+    width = up.shape[1]
+    skip = extended - width
 
     def body(up_ref, down_ref, below_ref, above_ref, *refs):
         up_out, down_out = refs[-2:]
-        up_out[...] = (up_ref[...].astype(F32) + below_ref[...].astype(F32)).astype(BF)
-        down_out[...] = (down_ref[...].astype(F32) + above_ref[...].astype(F32)).astype(BF)
-
-    block = (rows, width // 2)
-    first = pl.BlockSpec(block, lambda i: (0, i))
-    last = pl.BlockSpec(block, lambda i: (1, i))
+        up_out[...] = (up_ref[...].astype(F32) + below_ref[:, skip:].astype(F32)).astype(BF)
+        down_out[...] = (down_ref[...].astype(F32) + above_ref[:, skip:].astype(F32)).astype(BF)
+
+    first = pl.BlockSpec((rows // 2, width), lambda i: (i, 0))
+    last = pl.BlockSpec((rows // 2, width), lambda i: (2 + i, 0))
+    arrived = pl.BlockSpec((rows // 2, extended), lambda i: (i, 0))
     return pl.pallas_call(
         body,
         grid=(2,),
         out_shape=[jax.ShapeDtypeStruct(up.shape, BF)] * 2,
-        in_specs=[first, last, first, first] + [ANYWHERE] * len(others),
+        in_specs=[first, last, arrived, arrived] + [ANYWHERE] * len(others),
         out_specs=[first, last],
         input_output_aliases={0: 0, 1: 1},
         compiler_params=params(),
     )(up, down, from_below, from_above, *others)
 
 
-def ring_scatter(far_low, far_high, rest, *others):
-    from_below = shift(far_low, 1)
-    from_above = shift(far_high, -1)
-    up, down, own = rest()
-    up, down = add_halves(up, down, from_below, from_above, *others)
-    parts = (own, shift(up, 1), shift(down, -1))
-    return parts, (up, down), (from_below, from_above)
+def add_and_carry(up, down, from_below, from_above):
+    count, width = up.shape
+    rows, extended = from_below.shape
+    units = (extended - width) // 2
+    half = units // 2
+
+    def body(up_ref, down_ref, below_ref, above_ref, up_out, down_out):
+        up_out[:, half:] = up_ref[...]
+        down_out[:, half:] = down_ref[...]
+        for i in range(2):
+            here = pl.ds(i * rows, rows)
+            up_out[here, :half] = below_ref[:, i * half : (i + 1) * half]
+            down_out[here, :half] = above_ref[:, units + i * half : units + (i + 1) * half]
+        top, bottom = pl.ds(0, rows), pl.ds(rows, rows)
+        below, above = below_ref[:, 2 * units :], above_ref[:, 2 * units :]
+        up_out[top, half:] = (up_ref[top, :].astype(F32) + below.astype(F32)).astype(BF)
+        down_out[bottom, half:] = (down_ref[bottom, :].astype(F32) + above.astype(F32)).astype(BF)
+
+    return pl.pallas_call(
+        body,
+        out_shape=[jax.ShapeDtypeStruct((count, half + width), BF)] * 2,
+        compiler_params=params(),
+    )(up, down, from_below, from_above)
+
+
+def ring_scatter(from_below, from_above, rest, *others, carry=False):
+    up, down, own = rest
+    if carry:
+        up, down = add_and_carry(up, down, from_below, from_above)
+    else:
+        up, down = add_halves(up, down, from_below, from_above, *others)
+    return (own, shift(up, 1), shift(down, -1)), (up, down)
 
 
 def sum_beside(left, parts, *others):
-    count, quarter = left.shape
-    blocks = 2
-    width = quarter // blocks
+    count, quarter = parts[0].shape
+    block = count // 2
 
     def body(left_ref, a_ref, b_ref, c_ref, *refs):
-        out = refs[-1]
-
-        @pl.when(pl.program_id(0) < blocks)
-        def _():
-            out[...] = left_ref[...]
-
-        @pl.when(pl.program_id(0) >= blocks)
-        def _():
-            total = a_ref[...].astype(F32) + b_ref[...].astype(F32) + c_ref[...].astype(F32)
-            out[...] = total.astype(BF)
-
-    copied = pl.BlockSpec((count, width), lambda i: (0, jnp.minimum(i, blocks - 1)))
-    added = pl.BlockSpec((count, width), lambda i: (0, jnp.maximum(i - blocks, 0)))
-    return pl.pallas_call(
-        body,
-        grid=(2 * blocks,),
-        out_shape=jax.ShapeDtypeStruct((count, 2 * quarter), BF),
-        in_specs=[copied, added, added, added] + [ANYWHERE] * len(others),
-        out_specs=pl.BlockSpec((count, width), lambda i: (0, i)),
+        total = a_ref[...].astype(F32)
+        for ref in (b_ref, c_ref):
+            total = total + ref[:, ref.shape[1] - quarter :].astype(F32)
+        refs[-1][...] = total.astype(BF)
+
+    return pl.pallas_call(
+        body,
+        grid=(2,),
+        out_shape=jax.ShapeDtypeStruct(left.shape, BF),
+        in_specs=[ANYWHERE]
+        + [pl.BlockSpec((block, p.shape[1]), lambda i: (i, 0)) for p in parts]
+        + [ANYWHERE] * len(others),
+        out_specs=pl.BlockSpec((block, quarter), lambda i: (i, 1)),
+        input_output_aliases={0: 0},
         compiler_params=params(),
     )(left, *parts, *others)
 
 
-def row_half(array, part, *others):
-    rows, width = array.shape
-
-    def body(array_ref, *refs):
-        refs[-1][...] = array_ref[...]
+def carried(extended, part, units, *others):
+    half = extended.shape[0]
+
+    def body(extended_ref, *refs):
+        refs[-1][...] = extended_ref[...]
 
     return pl.pallas_call(
         body,
         grid=(1,),
-        out_shape=jax.ShapeDtypeStruct((rows // 2, width), array.dtype),
-        in_specs=[pl.BlockSpec((rows // 2, width), lambda i: (part, 0))]
-        + [ANYWHERE] * len(others),
-        out_specs=pl.BlockSpec((rows // 2, width), lambda i: (0, 0)),
-        compiler_params=params(),
-    )(array, *others)
+        out_shape=jax.ShapeDtypeStruct((half, units), extended.dtype),
+        in_specs=[pl.BlockSpec((half, units), lambda i: (0, part))] + [ANYWHERE] * len(others),
+        out_specs=pl.BlockSpec((half, units), lambda i: (0, 0)),
+        compiler_params=params(),
+    )(extended, *others)
 
 
 def cut_columns(here, array, offset, part, *others):
@@ -220,14 +240,14 @@
     )(rows, gate_mat, up_mat, *others)
 
 
-def backward_far(here, h, gate_pre, up_proj, grad_inner, gate_mat, up_mat, *others):
+def backward_far(here, h, gate_pre, up_proj, act, grad_inner, gate_mat, up_mat, *others):
     count, units = gate_pre.shape
     experts, capacity, _ = grad_inner.shape
     quarter = gate_mat.shape[0] // 4
     block = quarter // 2
     half = count // 2
 
-    def body(here_ref, gate_pre_ref, up_ref, inner_ref, gate_w, up_w, *refs):
+    def body(here_ref, gate_pre_ref, up_ref, act_ref, inner_ref, gate_w, up_w, *refs):
         ggp, gup, low, high = refs[-4:]
 
         @pl.when(pl.program_id(0) == 0)
@@ -237,20 +257,29 @@
             sig = jax.nn.sigmoid(gate)
             ggp[...] = (inner * up_ref[...] * sig * (1.0 + gate * (1.0 - sig))).astype(BF)
             gup[...] = (inner * gate * sig).astype(BF)
+            for out in (low, high):
+                out[:, :units] = act_ref[:half]
+                out[:, units : 2 * units] = act_ref[half:]
 
         piece = dot(ggp[...], gate_w[...], ((1,), (1,))) + dot(gup[...], up_w[...], ((1,), (1,)))
-        low[...] = piece[:half].astype(BF)
-        high[...] = piece[half:].astype(BF)
+        for j in range(2):
+
+            @pl.when(pl.program_id(0) == j)
+            def _():
+                columns = slice(2 * units + j * block, 2 * units + (j + 1) * block)
+                low[:, columns] = piece[:half].astype(BF)
+                high[:, columns] = piece[half:].astype(BF)
 
     whole = pl.BlockSpec((count, units), lambda j, here: (0, 0))
     weight = pl.BlockSpec((block, units), lambda j, here: (((here[0] + 2) % 4) * 2 + j, 0))
-    out = pl.BlockSpec((half, block), lambda j, here: (0, j))
+    out = pl.BlockSpec((half, 2 * units + quarter), lambda j, here: (0, 0))
     return pl.pallas_call(
         body,
         grid_spec=pltpu.PrefetchScalarGridSpec(
             num_scalar_prefetch=1,
             grid=(2,),
             in_specs=[
+                whole,
                 whole,
                 whole,
                 pl.BlockSpec((experts, capacity // 2, units), lambda j, here: (0, h, 0)),
@@ -263,11 +292,11 @@
         out_shape=[
             jax.ShapeDtypeStruct((count, units), BF),
             jax.ShapeDtypeStruct((count, units), BF),
-            jax.ShapeDtypeStruct((half, quarter), BF),
-            jax.ShapeDtypeStruct((half, quarter), BF),
+            jax.ShapeDtypeStruct((half, 2 * units + quarter), BF),
+            jax.ShapeDtypeStruct((half, 2 * units + quarter), BF),
         ],
         compiler_params=params(),
-    )(here, gate_pre, up_proj, grad_inner, gate_mat, up_mat, *others)
+    )(here, gate_pre, up_proj, act, grad_inner, gate_mat, up_mat, *others)
 
 
 def backward_rest(here, grad_gate_pre, grad_up, gate_mat, up_mat):
@@ -315,16 +344,23 @@
     half_units = units // 2
 
     def body(a0, a1, a3, a2_low, a2_high, *refs):
-        down_refs, (out, far) = refs[: len(downs)], refs[-2:]
+        down_refs, (out, above, below, far) = refs[: len(downs)], refs[-4:]
 
         @pl.when(pl.program_id(0) == 0)
         def _():
-            far[: count // 2] = a2_low[...]
-            far[count // 2 :] = a2_high[...]
+            for act, rows in ((a2_low, pl.ds(0, count // 2)), (a2_high, pl.ds(count // 2, count // 2))):
+                if act.shape[0] == count:
+                    far[rows, :half_units] = act[: count // 2]
+                    far[rows, half_units:] = act[count // 2 :]
+                else:
+                    far[rows, :] = act[...]
+            for act, full in ((a1, above), (a3, below)):
+                full[: count // 2] = act[:, :units]
+                full[count // 2 :] = act[:, units : 2 * units]
 
         total = jnp.dot(a0[...], down_refs[0][...], preferred_element_type=F32)
-        total += jnp.dot(a1[...], down_refs[1][...], preferred_element_type=F32)
-        total += jnp.dot(a3[...], down_refs[2][...], preferred_element_type=F32)
+        total += jnp.dot(above[...], down_refs[1][...], preferred_element_type=F32)
+        total += jnp.dot(below[...], down_refs[2][...], preferred_element_type=F32)
         for part in range(2):
             left = far[:, part * half_units : (part + 1) * half_units]
             total += jnp.dot(left, down_refs[3 + part][...], preferred_element_type=F32)
@@ -339,12 +375,17 @@
     return pl.pallas_call(
         body,
         grid=(quarter // block,),
-        out_shape=jax.ShapeDtypeStruct((count, quarter), BF),
-        in_specs=[held(a) for a in acts]
+        out_shape=jax.ShapeDtypeStruct((count, 2 * quarter), BF),
+        in_specs=[held(acts[0])]
+        + [pl.BlockSpec((count // 2, 2 * units), lambda j: (0, 0))] * 2
+        + [
+            held(a) if a.shape[1] == units else pl.BlockSpec((count, half_units), lambda j: (0, 0))
+            for a in acts[3:]
+        ]
         + [streamed(d) for d in downs]
         + [ANYWHERE] * len(others),
         out_specs=pl.BlockSpec((count, block), lambda j: (0, j)),
-        scratch_shapes=[pltpu.VMEM((count, units), BF)],
+        scratch_shapes=[pltpu.VMEM((count, units), BF)] * 3,
         compiler_params=params(),
     )(*acts, *downs, *others)
 
@@ -431,8 +472,8 @@
     down_own = cut_columns(place, down_mat, 0, None, grad_slots)
     far = inner_share(grad_slots, (far_low, far_high))
     own = dot(grad_slots, down_own, ((1,), (1,)))
-    send_rows[0] = after(send_rows[0], far_low, far_high, down_up, down_back)
-    send_rows[1] = after(send_rows[1], down_above, down_below, *far, own)
+    send_rows[0] = after(send_rows[0], pass_low, pass_high, down_up, down_back)
+    send_rows[1] = after(send_rows[1], *far, own)
     arrived = [
         exchange(send_rows[h].reshape(experts, part, width)).reshape(experts * part, width)
         for h in range(2)
@@ -440,38 +481,35 @@
     downs = (down_own, down_above, down_below, far_low, far_high)
     up = jnp.concatenate(inner_share(grad_slots, (down_above,)), axis=0)
     down = jnp.concatenate(inner_share(grad_slots, (down_below,)), axis=0)
-    inner_shares, passed, _ = ring_scatter(*far, lambda: (up, down, own))
-
-    gate_pre, up_proj, act = forward(arrived[0], gate_mat, up_mat, *passed)
-    act_below, act_above = shift(act, 1), shift(act, -1)
-    inner_shares = (after(own, act), *inner_shares[1:])
-    grad_inner = sum(share.astype(F32) for share in inner_shares)
-    grad_inner = grad_inner.reshape(experts, capacity, hidden_units)
-    grad_gate_pre, grad_up, low, high = backward_far(
-        place, 0, gate_pre, up_proj, grad_inner, gate_mat, up_mat
-    )
-    rest = backward_rest(place, grad_gate_pre, grad_up, gate_mat, up_mat)
-    act_low = shift(row_half(act_below, 0, rest[0]), 1)
-    act_high = shift(row_half(act_above, 1, rest[0]), -1)
-    first_acts = (act, act_above, act_below, act_low, act_high)
-
-    gate_pre, up_proj, act = forward(arrived[1], gate_mat, up_mat, rest[0])
-    first, passed, _ = ring_scatter(low, high, lambda: rest, act_low, act_high, act)
-    act_below, act_above = shift(act, 1), shift(act, -1)
-    grad_gate_pre, grad_up, low, high = backward_far(
-        place, 1, gate_pre, up_proj, grad_inner, gate_mat, up_mat, *passed
-    )
-    first_output = down_product(first_acts, downs, low)
-    last = backward_rest(place, grad_gate_pre, grad_up, gate_mat, up_mat)
-    act_low = shift(row_half(act_below, 0, last[0]), 1)
-    act_high = shift(row_half(act_above, 1, last[0]), -1)
-    acts = (act, act_above, act_below, act_low, act_high)
-    second, passed, came = ring_scatter(low, high, lambda: last, act_low, act_high)
-    output = down_product(acts, downs, *passed)
-
+    came = shift(far[0], 1), shift(far[1], -1)
+    inner_shares, passed = ring_scatter(*came, (up, down, own))
+
+    for h in range(2):
+        gate_pre, up_proj, act = forward(arrived[h], gate_mat, up_mat, *passed)
+        if h == 0:
+            inner_shares = (after(own, act), *inner_shares[1:])
+            grad_inner = sum(share.astype(F32) for share in inner_shares)
+            grad_inner = grad_inner.reshape(experts, capacity, hidden_units)
+        grad_gate_pre, grad_up, low, high = backward_far(
+            place, h, gate_pre, up_proj, act, grad_inner, gate_mat, up_mat
+        )
+        below, above = shift(low, 1), shift(high, -1)
+        rest = backward_rest(place, grad_gate_pre, grad_up, gate_mat, up_mat)
+        if h == 0:
+            shares, passed = ring_scatter(below, above, rest, carry=True)
+            act_low, act_high = shares[1], shares[2]
+            first = (act, above, below, act_low, act_high), shares
+    first_output = down_product(first[0], downs, low)
+    act_low = shift(carried(below, 0, hidden_units, rest[0]), 1)
+    act_high = shift(carried(above, 1, hidden_units, rest[0]), -1)
+    second, passed = ring_scatter(below, above, rest, act_low, act_high)
+    output = down_product((act, above, below, act_low, act_high), downs, *passed)
     returned = [
         exchange(both.reshape(experts, part, 2 * quarter))
-        for both in (sum_beside(first_output, first, *came), sum_beside(output, second))
+        for both in (
+            sum_beside(first_output, first[1], below, above, rest[0]),
+            sum_beside(output, second),
+        )
     ]
     returned = [both.reshape(experts * part, 2 * quarter) for both in returned]
     back = [both[:, :quarter] for both in returned]

time: 336 us -> 309 us (0.920)
  waiting for transfers between devices: 107 us -> 90.3 us
  starting transfers between devices: 87.3 us -> 79.2 us
    ppermute x33 -> x27, waiting for transfers between devices: 85.9 us -> 53.7 us  [shift(): lax.ppermute(value, 'pp', [(i, (i + step) % ring) for i in range(ring)])]
    all_to_all x5, waiting for transfers between devices: 21 us -> 36.6 us  [exchange(): return lax.all_to_all(value, 'ep', split_axis=0, concat_axis=0, tiled=True)]
    ppermute x33 -> x27, starting transfers between devices: 50.6 us -> 42.8 us  [shift(): lax.ppermute(value, 'pp', [(i, (i + step) % ring) for i in range(ring)])]
    pallas_call x6 -> x5, Pallas kernels: 7.12 us -> 5.23 us  [the longest x2 3.61 us: sum_beside(): pl.pallas_call(body, grid=(2,), out_shape=jax.ShapeDtypeStruct(left.shape...]
    unnamed x116 -> x104, local copies, waits for them, and re-layouts: 16.5 us -> 15.5 us
  transfers between devices with their start and end apart: 38 -> 32, of which waited for: 14 -> 14; matrix products, arithmetic and copies ran while one was open for 10% -> 11% of each run, Pallas kernels for 23% -> 25%
where the time goes in v2:
time: 309 us; the launch traced here: 307 us
  waiting for transfers between devices  90.3 us (29%)
  Pallas kernels  80.6 us (26%)
  starting transfers between devices  79.2 us (26%)
  matrix products  24.4 us (8%)
  local copies, waits for them, and re-layouts  21.4 us (7%)
  other arithmetic  9.2 us (3%)
    ppermute x27, waiting for transfers between devices, shift(): lax.ppermute(value, 'pp', [(i, (i + step) % ring) for i in range(ring)])  53.7 us
    ppermute x27, starting transfers between devices, shift(): lax.ppermute(value, 'pp', [(i, (i + step) % ring) for i in range(ring)])  42.8 us
    all_to_all x5, waiting for transfers between devices, exchange(): return lax.all_to_all(value, 'ep', split_axis=0, concat_axis=0, tiled=True)  36.6 us
    all_to_all x5, starting transfers between devices, exchange(): return lax.all_to_all(value, 'ep', split_axis=0, concat_axis=0, tiled=True)  36.5 us
    dot_general x10, matrix products, dot(): lax.dot_general(left, right, (dims, ((), ())), preferred_element_type=F32)  24.4 us
    pallas_call x2, Pallas kernels, forward(): pl.pallas_call(body, grid=(width // depth,), out_shape=[jax.ShapeDtypeStr...  20 us
    pallas_call x2, Pallas kernels, backward_rest(): pl.pallas_call(body, grid_spec=pltpu.PrefetchScalarGridSpec(num_scalar_pr...  16.5 us
    unnamed x104, local copies, waits for them, and re-layouts  15.5 us
  transfers between devices with their start and end apart: 32, of which 14 were waited for; matrix products, arithmetic and copies ran while one was open for 11% of the time, Pallas kernels for 25%

profile of v2, /device:TPU:0, one launch (start us, length us, event | category | flops | bytes accessed | tf_op | source)
XLA Modules:
  0.0 306.5 jit_solution(15745468399115452044)
XLA Ops:
  0.6 1.6 collective-permute-start.1
  2.3 1.7 collective-permute-start
  3.9 1.2 shard_map.129.refs_1_
  5.7 2.2 shard_map.130.refs_2_
  7.9 2.8 collective-permute-start.5
  12.5 2.0 multiply_convert_fusion.refs_0_
  14.5 8.6 %all-to-all-start.1 = ((bf16[32,16,1792]{2,1,0:T(8,128)(2,1)}), bf16[32,16,1792]{2,1,0:T(8,128)(2,1)S(1)}, u32[]{:S(2)}, u32[]{:S(2)}) async-start(bf16[32,16,1792]{2,1,0:T(8,128)(2,1)} %bitcast.83), calls=%async_computation.1 | async-start | bytes 3670016 | tf_op jit(solution)/shard_map/all_to_all | solution.py:394
  23.1 1.9 fusion
  27.2 3.3 %collective-permute-start.3 = (bf16[64,1792]{1,0:T(8,128)(2,1)S(1)}, bf16[64,1792]{1,0:T(8,128)(2,1)S(1)}, u32[]{:S(2)}, u32[]{:S(2)}) collective-permute-start(bf16[64,1792]{1,0:T(8,128)(2,1)S(1)} %slice.74), channel_id=1, source_target_pairs={{0,96},{32,0},{64,32},{96,64},{1,97},{33,1},{65,33},{97,65},{2,98}... | collective-permute-start | bytes 688136 | tf_op jit(solution)/shard_map/ppermute | solution.py:19
  31.5 7.3 %collective-permute-done.2 = bf16[64,1792]{1,0:T(8,128)(2,1)S(1)} collective-permute-done((bf16[64,1792]{1,0:T(8,128)(2,1)S(1)}, bf16[64,1792]{1,0:T(8,128)(2,1)S(1)}, u32[]{:S(2)}, u32[]{:S(2)}) %collective-permute-start.2) | collective-permute-done | bytes 229408 | tf_op jit(solution)/shard_map/ppermute | solution.py:19
  45.7 3.0 convolution_convert_fusion.1.refs_0_
  48.7 1.5 shard_map.132.refs_4_
  50.3 1.3 copy-done.6
  51.5 1.5 shard_map.131.refs_3_
  54.3 8.5 %all-to-all-start = ((bf16[32,8,7168]{2,1,0:T(8,128)(2,1)}), bf16[32,8,7168]{2,1,0:T(8,128)(2,1)}, u32[]{:S(2)}, u32[]{:S(2)}) async-start(bf16[32,8,7168]{2,1,0:T(8,128)(2,1)} %bitcast.79), calls=%async_computation | async-start | bytes 7340032 | tf_op jit(solution)/shard_map/all_to_all | solution.py:394
  62.8 1.6 collective-permute-start.8
  64.4 1.7 collective-permute-start.9
  66.4 3.0 collective-permute-start.6
  69.4 4.5 %convolution_convert_fusion.refs_0_ = bf16[256,7168]{1,0:T(8,128)(2,1)} fusion(bf16[128,7168]{1,0:T(8,128)(2,1)} %copy-done.30, s32[256]{0:T(256)S(1)} %iota_add_fusion, s32[128]{0:T(128)S(1)} %get-tuple-element.84, s32[128]{0:T(128)S(1)} %get-tuple-element.83), kind=kOutput, calls=%fused_computation | convolution fusion | flops 471695360 | bytes 5507072 | tf_op jit(solution)/shard_map/dot_general | solution.py:14
  73.9 1.5 shard_map.140.refs_0_
  75.5 2.1 fusion.57.refs_0_.refs_3_
  77.6 9.9 %collective-permute-done.8.refs_0_.refs_3_ = bf16[256,1792]{1,0:T(8,128)(2,1)S(1)} collective-permute-done((bf16[256,1792]{1,0:T(8,128)(2,1)}, bf16[256,1792]{1,0:T(8,128)(2,1)S(1)}, u32[]{:S(2)}, u32[]{:S(2)}) %collective-permute-start.8) | collective-permute-done | bytes 917536 | tf_op jit(solution)/shard_map/ppermute | solution.py:19
  87.8 2.6 shard_map.137
  92.8 17.7 %all-to-all-done = bf16[32,8,7168]{2,1,0:T(8,128)(2,1)} async-done(((bf16[32,8,7168]{2,1,0:T(8,128)(2,1)}), bf16[32,8,7168]{2,1,0:T(8,128)(2,1)}, u32[]{:S(2)}, u32[]{:S(2)}) %all-to-all-start) | async-done | bytes 3670048 | tf_op jit(solution)/shard_map/all_to_all | solution.py:394
  110.5 5.0 %all-to-all-start.2 = ((bf16[32,8,7168]{2,1,0:T(8,128)(2,1)}), bf16[32,8,7168]{2,1,0:T(8,128)(2,1)}, u32[]{:S(2)}, u32[]{:S(2)}) async-start(bf16[32,8,7168]{2,1,0:T(8,128)(2,1)} %bitcast.80), calls=%async_computation.2 | async-start | bytes 7340032 | tf_op jit(solution)/shard_map/all_to_all | solution.py:394
  115.5 1.6 collective-permute-start.10
  117.1 1.7 collective-permute-start.11
  118.8 8.1 %collective-permute-done.7.refs_0_.refs_2_ = bf16[512,1792]{1,0:T(8,128)(2,1)} collective-permute-done((bf16[512,1792]{1,0:T(8,128)(2,1)}, bf16[512,1792]{1,0:T(8,128)(2,1)}, u32[]{:S(2)}, u32[]{:S(2)}) %collective-permute-start.7) | collective-permute-done | bytes 1835040 | tf_op jit(solution)/shard_map/ppermute | solution.py:19
  126.9 2.9 shard_map.136
  129.8 2.9 shard_map.135
  133.4 3.0 collective-permute-start.13
  136.4 10.0 %shard_map.139 = (f32[256,512]{1,0:T(8,128)S(1)}, f32[256,512]{1,0:T(8,128)S(1)}, bf16[256,512]{1,0:T(8,128)(2,1)S(1)}) custom-call(bf16[256,7168]{1,0:T(8,128)(2,1)} %bitcast.7.rows_ref, bf16[7168,512]{1,0:T(8,128)(2,1)} %bitcast.62, bf16[7168,512]{1,0:T(8,128)(2,1)} %bitcast.68, bf16[512,512]{1,0:T(8,128)(2,1)S(1)} %get-tuple-element.42.refs_0_, ...), custom_call_target="tpu_custom_call" | custom-call | tf_op jit(solution)/shard_map/pallas_call | solution.py:228
  147.1 2.7 convert_add_fusion
  149.8 3.5 %shard_map.142 = (bf16[256,512]{1,0:T(8,128)(2,1)S(1)}, bf16[256,512]{1,0:T(8,128)(2,1)S(1)}, bf16[128,2816]{1,0:T(8,128)(2,1)S(1)}, bf16[128,2816]{1,0:T(8,128)(2,1)S(1)}) custom-call(s32[1]{0:T(128)} %bitcast.4.here_ref, f32[256,512]{1,0:T(8,128)S(1)} %get-tuple-element.45.gate_pre_ref, f32[256,512]{1,0:T(8,128)S(1)} %get-tuple-element.46.up_ref, ...), custom_call_target="tpu_custom_call" | custom-call | tf_op jit(solution)/shard_map/pallas_call | solution.py:276
  153.3 2.9 collective-permute-start.14
  156.2 8.2 %shard_map.143 = (bf16[256,1792]{1,0:T(8,128)(2,1)S(1)}, bf16[256,1792]{1,0:T(8,128)(2,1)S(1)}, bf16[256,1792]{1,0:T(8,128)(2,1)S(1)}) custom-call(s32[1]{0:T(128)} %bitcast.4.here_ref, bf16[256,512]{1,0:T(8,128)(2,1)S(1)} %get-tuple-element.49.ggp, bf16[256,512]{1,0:T(8,128)(2,1)S(1)} %get-tuple-element.50.gup, bf16[7168,512]{1,0:T(8,128)(2,1)} %bitcast.64, ...), custom_call_target="tpu_custom_call" | custom-call | tf_op jit(solution)/shard_map/pallas_call | solution.py:327
  164.4 5.2 %collective-permute-done.14.above_ref.a1 = bf16[128,2816]{1,0:T(8,128)(2,1)S(1)} collective-permute-done((bf16[128,2816]{1,0:T(8,128)(2,1)S(1)}, bf16[128,2816]{1,0:T(8,128)(2,1)S(1)}, u32[]{:S(2)}, u32[]{:S(2)}) %collective-permute-start.14) | collective-permute-done | bytes 720928 | tf_op jit(solution)/shard_map/ppermute | solution.py:19
  169.5 3.1 %collective-permute-done.15.below_ref.a3 = bf16[128,2816]{1,0:T(8,128)(2,1)S(1)} collective-permute-done((bf16[128,2816]{1,0:T(8,128)(2,1)S(1)}, bf16[128,2816]{1,0:T(8,128)(2,1)S(1)}, u32[]{:S(2)}, u32[]{:S(2)}) %collective-permute-start.15) | collective-permute-done | bytes 720928 | tf_op jit(solution)/shard_map/ppermute | solution.py:19
  172.6 1.6 shard_map.144
  175.1 3.2 %collective-permute-start.17 = (bf16[256,2048]{1,0:T(8,128)(2,1)}, bf16[256,2048]{1,0:T(8,128)(2,1)}, u32[]{:S(2)}, u32[]{:S(2)}) collective-permute-start(bf16[256,2048]{1,0:T(8,128)(2,1)} %get-tuple-element.54.refs_1_), channel_id=1, source_target_pairs={{0,96},{32,0},{64,32},{96,64},{1,97},{33,1},{65,33},{97,65},{2,98}... | collective-permute-start | bytes 3145736 | tf_op jit(solution)/shard_map/ppermute | solution.py:19
  178.3 1.3 copy-done.20
  180.8 10.1 %shard_map.146 = (f32[256,512]{1,0:T(8,128)S(1)}, f32[256,512]{1,0:T(8,128)S(1)}, bf16[256,512]{1,0:T(8,128)(2,1)S(1)}) custom-call(bf16[256,7168]{1,0:T(8,128)(2,1)} %bitcast.17.rows_ref, bf16[7168,512]{1,0:T(8,128)(2,1)} %bitcast.65, bf16[7168,512]{1,0:T(8,128)(2,1)} %bitcast.71, bf16[256,2048]{1,0:T(8,128)(2,1)S(1)} %copy-done.21, ...), custom_call_target="tpu_custom_call" | custom-call | tf_op jit(solution)/shard_map/pallas_call | solution.py:228
  190.9 3.6 %shard_map.147 = (bf16[256,512]{1,0:T(8,128)(2,1)S(1)}, bf16[256,512]{1,0:T(8,128)(2,1)S(1)}, bf16[128,2816]{1,0:T(8,128)(2,1)S(1)}, bf16[128,2816]{1,0:T(8,128)(2,1)S(1)}) custom-call(s32[1]{0:T(128)} %bitcast.4.here_ref, f32[256,512]{1,0:T(8,128)S(1)} %get-tuple-element.55.gate_pre_ref, f32[256,512]{1,0:T(8,128)S(1)} %get-tuple-element.56.up_ref, ...), custom_call_target="tpu_custom_call" | custom-call | tf_op jit(solution)/shard_map/pallas_call | solution.py:276
  194.6 2.0 collective-permute-start.18
  196.6 8.3 %shard_map.149 = (bf16[256,1792]{1,0:T(8,128)(2,1)S(1)}, bf16[256,1792]{1,0:T(8,128)(2,1)S(1)}, bf16[256,1792]{1,0:T(8,128)(2,1)S(1)}) custom-call(s32[1]{0:T(128)} %bitcast.4.here_ref, bf16[256,512]{1,0:T(8,128)(2,1)S(1)} %get-tuple-element.61.ggp, bf16[256,512]{1,0:T(8,128)(2,1)S(1)} %get-tuple-element.62.gup, bf16[7168,512]{1,0:T(8,128)(2,1)} %bitcast.67, ...), custom_call_target="tpu_custom_call" | custom-call | tf_op jit(solution)/shard_map/pallas_call | solution.py:327
  206.9 7.6 %shard_map.148.left_ref = bf16[256,3584]{1,0:T(8,128)(2,1)} custom-call(bf16[256,512]{1,0:T(8,128)(2,1)S(1)} %copy-done.17, bf16[128,2816]{1,0:T(8,128)(2,1)S(1)} %copy-done.13, bf16[128,2816]{1,0:T(8,128)(2,1)S(1)} %copy-done.15, bf16[256,2048]{1,0:T(8,128)(2,1)} %collective-permute-done.16.a2_low.b_ref, ...), custom_call_target="tpu_custom_call" | custom-call | tf_op jit(solution)/shard_map/pallas_call | solution.py:375
  214.5 2.5 shard_map.150
  217.0 7.2 %all-to-all-start.3 = ((bf16[32,8,3584]{2,1,0:T(8,128)(2,1)}), bf16[32,8,3584]{2,1,0:T(8,128)(2,1)}, u32[]{:S(2)}, u32[]{:S(2)}) async-start(bf16[32,8,3584]{2,1,0:T(8,128)(2,1)} %bitcast.82), calls=%async_computation.3 | async-start | bytes 3670016 | tf_op jit(solution)/shard_map/all_to_all | solution.py:394
  224.3 3.3 %collective-permute-start.21 = (bf16[128,512]{1,0:T(8,128)(2,1)S(1)}, bf16[128,512]{1,0:T(8,128)(2,1)S(1)}, u32[]{:S(2)}, u32[]{:S(2)}) collective-permute-start(bf16[128,512]{1,0:T(8,128)(2,1)S(1)} %shard_map.152), channel_id=1, source_target_pairs={{0,96},{32,0},{64,32},{96,64},{1,97},{33,1},{65,33},{97,65},{2,98}... | collective-permute-start | bytes 393224 | tf_op jit(solution)/shard_map/ppermute | solution.py:19
  227.6 3.5 %collective-permute-done.20.refs_0_.a2_low = bf16[128,512]{1,0:T(8,128)(2,1)S(1)} collective-permute-done((bf16[128,512]{1,0:T(8,128)(2,1)S(1)}, bf16[128,512]{1,0:T(8,128)(2,1)S(1)}, u32[]{:S(2)}, u32[]{:S(2)}) %collective-permute-start.20) | collective-permute-done | bytes 131104 | tf_op jit(solution)/shard_map/ppermute | solution.py:19
  231.5 3.2 %collective-permute-start.23 = (bf16[256,1792]{1,0:T(8,128)(2,1)S(1)}, bf16[256,1792]{1,0:T(8,128)(2,1)S(1)}, u32[]{:S(2)}, u32[]{:S(2)}) collective-permute-start(bf16[256,1792]{1,0:T(8,128)(2,1)S(1)} %get-tuple-element.66.refs_6_), channel_id=1, source_target_pairs={{0,96},{32,0},{64,32},{96,64},{1,97},{33,1},{65,33},{97,65},{2,98}... | collective-permute-start | bytes 2752520 | tf_op jit(solution)/shard_map/ppermute | solution.py:19
  234.7 7.3 %shard_map.154.left_ref = bf16[256,3584]{1,0:T(8,128)(2,1)} custom-call(bf16[256,512]{1,0:T(8,128)(2,1)S(1)} %copy-done.19, bf16[128,2816]{1,0:T(8,128)(2,1)S(1)} %collective-permute-done.19.refs_1_.extended_ref.above_ref.a1, bf16[128,2816]{1,0:T(8,128)(2,1)S(1)} %collective-permute-done.18.refs_0_.extended_ref.below_ref.a3, ...), custom_call_target="tpu_custom_call" | custom-call | tf_op jit(solution)/shard_map/pallas_call | solution.py:375
  241.9 12.5 %collective-permute-done.22.b_ref = bf16[256,1792]{1,0:T(8,128)(2,1)S(1)} collective-permute-done((bf16[256,1792]{1,0:T(8,128)(2,1)S(1)}, bf16[256,1792]{1,0:T(8,128)(2,1)S(1)}, u32[]{:S(2)}, u32[]{:S(2)}) %collective-permute-start.22) | collective-permute-done | bytes 917536 | tf_op jit(solution)/shard_map/ppermute | solution.py:19
  255.5 7.3 %all-to-all-start.4 = ((bf16[32,8,3584]{2,1,0:T(8,128)(2,1)}), bf16[32,8,3584]{2,1,0:T(8,128)(2,1)}, u32[]{:S(2)}, u32[]{:S(2)}) async-start(bf16[32,8,3584]{2,1,0:T(8,128)(2,1)} %bitcast.81), calls=%async_computation.4 | async-start | bytes 3670016 | tf_op jit(solution)/shard_map/all_to_all | solution.py:394
  264.4 1.5 fusion.21
  266.0 2.4 fusion.23
  268.4 2.5 fusion.17
  270.9 18.8 %all-to-all-done.4 = bf16[32,8,3584]{2,1,0:T(8,128)(2,1)} async-done(((bf16[32,8,3584]{2,1,0:T(8,128)(2,1)}), bf16[32,8,3584]{2,1,0:T(8,128)(2,1)}, u32[]{:S(2)}, u32[]{:S(2)}) %all-to-all-start.4) | async-done | bytes 1835040 | tf_op jit(solution)/shard_map/all_to_all | solution.py:394
  289.8 1.6 convolution_add_fusion.1
  291.4 2.8 fusion.6
  294.3 1.8 fusion.8
  296.0 2.8 collective-permute-start.25
  302.4 2.1 collective-permute-done.24
  305.1 1.4 fusion.15
  (177 shorter events, 29.1 us)
Async XLA Ops:
  0.6 24.5 %collective-permute-start.1 = (bf16[128,1792]{1,0:T(8,128)(2,1)}, bf16[128,1792]{1,0:T(8,128)(2,1)}, u32[]{:S(2)}, u32[]{:S(2)}) collective-permute-start(bf16[128,1792]{1,0:T(8,128)(2,1)} %param.11), channel_id=1, source_target_pairs={{0,32},{32,64},{64,96},{96,0},{1,33},{33,65},{65,97},{97,1},{2,34}... | collective-permute-start | bytes 1376264 | tf_op jit(solution)/shard_map/ppermute | solution.py:19
  2.3 23.9 %collective-permute-start = (bf16[128,1792]{1,0:T(8,128)(2,1)}, bf16[128,1792]{1,0:T(8,128)(2,1)}, u32[]{:S(2)}, u32[]{:S(2)}) collective-permute-start(bf16[128,1792]{1,0:T(8,128)(2,1)} %param.11), channel_id=1, source_target_pairs={{0,96},{32,0},{64,32},{96,64},{1,97},{33,1},{65,33},{97,65},{2,98}... | collective-permute-start | bytes 1376264 | tf_op jit(solution)/shard_map/ppermute | solution.py:19
  5.2 5.5 %copy-start.45 = (s32[128,2]{0,1:T(2,128)S(1)}, s32[128,2]{0,1:T(2,128)}, u32[]{:S(2)}) copy-start(s32[128,2]{0,1:T(2,128)} %param.12) | copy-start | bytes 3076
  5.2 5.9 %copy-start.48 = (f32[128,2]{0,1:T(2,128)S(1)}, f32[128,2]{0,1:T(2,128)}, u32[]{:S(2)}) copy-start(f32[128,2]{0,1:T(2,128)} %param.13) | copy-start | bytes 3076
  5.2 7.3 %copy-start.36 = (bf16[128,1792]{1,0:T(8,128)(2,1)S(1)}, bf16[128,1792]{1,0:T(8,128)(2,1)}, u32[]{:S(2)}) copy-start(bf16[128,1792]{1,0:T(8,128)(2,1)} %param.19) | copy-start | bytes 1376260
  5.2 49.1 %collective-permute-start.4 = (bf16[256,1792]{1,0:T(8,128)(2,1)S(1)}, bf16[256,1792]{1,0:T(8,128)(2,1)}, u32[]{:S(2)}, u32[]{:S(2)}) collective-permute-start(bf16[256,1792]{1,0:T(8,128)(2,1)S(1)} %shard_map.129.refs_1_), channel_id=1, source_target_pairs={{0,32},{32,64},{64,96},{96,0},{1,33},{33,65},{65,97},{97,1},{2,34}... | collective-permute-start | bytes 2752520 | tf_op jit(solution)/shard_map/ppermute | solution.py:19
  7.9 46.5 %collective-permute-start.5 = (bf16[256,1792]{1,0:T(8,128)(2,1)}, bf16[256,1792]{1,0:T(8,128)(2,1)}, u32[]{:S(2)}, u32[]{:S(2)}) collective-permute-start(bf16[256,1792]{1,0:T(8,128)(2,1)} %shard_map.130.refs_2_), channel_id=1, source_target_pairs={{0,96},{32,0},{64,32},{96,64},{1,97},{33,1},{65,33},{97,65},{2,98}... | collective-permute-start | bytes 2752520 | tf_op jit(solution)/shard_map/ppermute | solution.py:19
  11.1 3.4 %copy-start.41 = (f32[128]{0:T(128)}, f32[128]{0:T(128)S(1)}, u32[]{:S(2)}) copy-start(f32[128]{0:T(128)S(1)} %get-tuple-element.81) | copy-start | bytes 1540
  11.1 3.4 %copy-start.43 = (f32[128]{0:T(128)}, f32[128]{0:T(128)S(1)}, u32[]{:S(2)}) copy-start(f32[128]{0:T(128)S(1)} %get-tuple-element.82) | copy-start | bytes 1540
  14.5 10.5 %copy-start.33 = (bf16[128,1792]{1,0:T(8,128)(2,1)S(1)}, bf16[128,1792]{1,0:T(8,128)(2,1)}, u32[]{:S(2)}) copy-start(bf16[128,1792]{1,0:T(8,128)(2,1)} %param.11) | copy-start | bytes 1376260
  14.5 39.8 %all-to-all-start.1 = ((bf16[32,16,1792]{2,1,0:T(8,128)(2,1)}), bf16[32,16,1792]{2,1,0:T(8,128)(2,1)S(1)}, u32[]{:S(2)}, u32[]{:S(2)}) async-start(bf16[32,16,1792]{2,1,0:T(8,128)(2,1)} %bitcast.83), calls=%async_computation.1 | async-start | bytes 3670016 | tf_op jit(solution)/shard_map/all_to_all | solution.py:394
  26.1 12.7 %collective-permute-start.2 = (bf16[64,1792]{1,0:T(8,128)(2,1)S(1)}, bf16[64,1792]{1,0:T(8,128)(2,1)S(1)}, u32[]{:S(2)}, u32[]{:S(2)}) collective-permute-start(bf16[64,1792]{1,0:T(8,128)(2,1)S(1)} %slice.73), channel_id=1, source_target_pairs={{0,32},{32,64},{64,96},{96,0},{1,33},{33,65},{65,97},{97,1},{2,34}... | collective-permute-start | bytes 688136 | tf_op jit(solution)/shard_map/ppermute | solution.py:19
  27.2 11.9 %collective-permute-start.3 = (bf16[64,1792]{1,0:T(8,128)(2,1)S(1)}, bf16[64,1792]{1,0:T(8,128)(2,1)S(1)}, u32[]{:S(2)}, u32[]{:S(2)}) collective-permute-start(bf16[64,1792]{1,0:T(8,128)(2,1)S(1)} %slice.74), channel_id=1, source_target_pairs={{0,96},{32,0},{64,32},{96,64},{1,97},{33,1},{65,33},{97,65},{2,98}... | collective-permute-start | bytes 688136 | tf_op jit(solution)/shard_map/ppermute | solution.py:19
  31.5 11.9 %copy-start.31 = (bf16[128,7168]{1,0:T(8,128)(2,1)S(1)}, bf16[128,7168]{1,0:T(8,128)(2,1)}, u32[]{:S(2)}) copy-start(bf16[128,7168]{1,0:T(8,128)(2,1)} %param.10) | copy-start | bytes 5505028
  31.5 11.9 %copy-start.37 = (f32[7168]{0:T(1024)S(1)}, f32[7168]{0:T(1024)}, u32[]{:S(2)}) copy-start(f32[7168]{0:T(1024)} %param.14) | copy-start | bytes 86020
  31.5 11.9 %copy-start.38 = (f32[7168]{0:T(1024)S(1)}, f32[7168]{0:T(1024)}, u32[]{:S(2)}) copy-start(f32[7168]{0:T(1024)} %param.15) | copy-start | bytes 86020
  43.4 5.3 %copy-start.39 = (f32[128]{0:T(128)}, f32[128]{0:T(128)S(1)}, u32[]{:S(2)}) copy-start(f32[128]{0:T(128)S(1)} %get-tuple-element.90) | copy-start | bytes 1540
  54.3 21.1 %copy-start = (bf16[32,16,1792]{2,1,0:T(8,128)(2,1)}, bf16[32,16,1792]{2,1,0:T(8,128)(2,1)S(1)}, u32[]{:S(2)}) copy-start(bf16[32,16,1792]{2,1,0:T(8,128)(2,1)S(1)} %all-to-all-done.1) | copy-start | bytes 5505028
  54.3 56.1 %all-to-all-start = ((bf16[32,8,7168]{2,1,0:T(8,128)(2,1)}), bf16[32,8,7168]{2,1,0:T(8,128)(2,1)}, u32[]{:S(2)}, u32[]{:S(2)}) async-start(bf16[32,8,7168]{2,1,0:T(8,128)(2,1)} %bitcast.79), calls=%async_computation | async-start | bytes 7340032 | tf_op jit(solution)/shard_map/all_to_all | solution.py:394
  62.8 24.7 %collective-permute-start.8 = (bf16[256,1792]{1,0:T(8,128)(2,1)}, bf16[256,1792]{1,0:T(8,128)(2,1)S(1)}, u32[]{:S(2)}, u32[]{:S(2)}) collective-permute-start(bf16[256,1792]{1,0:T(8,128)(2,1)} %collective-permute-done.4.refs_1_), channel_id=1, source_target_pairs={{0,32},{32,64},{64,96},{96,0},{1,33},{33,65},{65,97},{97,1},{2,34}... | collective-permute-start | bytes 2752520 | tf_op jit(solution)/shard_map/ppermute | solution.py:19
  64.4 23.4 %collective-permute-start.9 = (bf16[256,1792]{1,0:T(8,128)(2,1)}, bf16[256,1792]{1,0:T(8,128)(2,1)S(1)}, u32[]{:S(2)}, u32[]{:S(2)}) collective-permute-start(bf16[256,1792]{1,0:T(8,128)(2,1)} %collective-permute-done.5.refs_2_), channel_id=1, source_target_pairs={{0,96},{32,0},{64,32},{96,64},{1,97},{33,1},{65,33},{97,65},{2,98}... | collective-permute-start | bytes 2752520 | tf_op jit(solution)/shard_map/ppermute | solution.py:19
  66.1 60.8 %collective-permute-start.7 = (bf16[512,1792]{1,0:T(8,128)(2,1)}, bf16[512,1792]{1,0:T(8,128)(2,1)}, u32[]{:S(2)}, u32[]{:S(2)}) collective-permute-start(bf16[512,1792]{1,0:T(8,128)(2,1)} %copy-done.7), channel_id=1, source_target_pairs={{0,32},{32,64},{64,96},{96,0},{1,33},{33,65},{65,97},{97,1},{2,34}... | collective-permute-start | bytes 5505032 | tf_op jit(solution)/shard_map/ppermute | solution.py:19
  66.4 63.4 %collective-permute-start.6 = (bf16[512,1792]{1,0:T(8,128)(2,1)}, bf16[512,1792]{1,0:T(8,128)(2,1)}, u32[]{:S(2)}, u32[]{:S(2)}) collective-permute-start(bf16[512,1792]{1,0:T(8,128)(2,1)} %copy-done.6), channel_id=1, source_target_pairs={{0,96},{32,0},{64,32},{96,64},{1,97},{33,1},{65,33},{97,65},{2,98}... | collective-permute-start | bytes 5505032 | tf_op jit(solution)/shard_map/ppermute | solution.py:19
  110.5 5.0 %copy-start.29 = (bf16[256,512]{1,0:T(8,128)(2,1)S(1)}, bf16[256,512]{1,0:T(8,128)(2,1)}, u32[]{:S(2)}) copy-start(bf16[256,512]{1,0:T(8,128)(2,1)} %copy-done.28) | copy-start | bytes 786436
  110.5 6.6 %copy-start.27 = (bf16[256,512]{1,0:T(8,128)(2,1)S(1)}, bf16[256,512]{1,0:T(8,128)(2,1)}, u32[]{:S(2)}) copy-start(bf16[256,512]{1,0:T(8,128)(2,1)} %copy-done.26) | copy-start | bytes 786436
  110.5 16.4 %copy-start.1 = (bf16[32,16,1792]{2,1,0:T(8,128)(2,1)S(1)}, bf16[32,16,1792]{2,1,0:T(8,128)(2,1)}, u32[]{:S(2)}) copy-start(bf16[32,16,1792]{2,1,0:T(8,128)(2,1)} %copy-done) | copy-start | bytes 5505028
  110.5 67.8 %all-to-all-start.2 = ((bf16[32,8,7168]{2,1,0:T(8,128)(2,1)}), bf16[32,8,7168]{2,1,0:T(8,128)(2,1)}, u32[]{:S(2)}, u32[]{:S(2)}) async-start(bf16[32,8,7168]{2,1,0:T(8,128)(2,1)} %bitcast.80), calls=%async_computation.2 | async-start | bytes 7340032 | tf_op jit(solution)/shard_map/all_to_all | solution.py:394
  115.5 17.4 %collective-permute-start.10 = (bf16[256,512]{1,0:T(8,128)(2,1)S(1)}, bf16[256,512]{1,0:T(8,128)(2,1)S(1)}, u32[]{:S(2)}, u32[]{:S(2)}) collective-permute-start(bf16[256,512]{1,0:T(8,128)(2,1)S(1)} %copy-done.29), channel_id=1, source_target_pairs={{0,32},{32,64},{64,96},{96,0},{1,33},{33,65},{65,97},{97,1},{2,34}... | collective-permute-start | bytes 786440 | tf_op jit(solution)/shard_map/ppermute | solution.py:19
  117.1 15.8 %collective-permute-start.11 = (bf16[256,512]{1,0:T(8,128)(2,1)S(1)}, bf16[256,512]{1,0:T(8,128)(2,1)S(1)}, u32[]{:S(2)}, u32[]{:S(2)}) collective-permute-start(bf16[256,512]{1,0:T(8,128)(2,1)S(1)} %copy-done.27), channel_id=1, source_target_pairs={{0,96},{32,0},{64,32},{96,64},{1,97},{33,1},{65,33},{97,65},{2,98}... | collective-permute-start | bytes 786440 | tf_op jit(solution)/shard_map/ppermute | solution.py:19
  133.1 14.0 %collective-permute-start.12 = (bf16[512,512]{1,0:T(8,128)(2,1)S(1)}, bf16[512,512]{1,0:T(8,128)(2,1)}, u32[]{:S(2)}, u32[]{:S(2)}) collective-permute-start(bf16[512,512]{1,0:T(8,128)(2,1)S(1)} %get-tuple-element.42.refs_0_), channel_id=1, source_target_pairs={{0,32},{32,64},{64,96},{96,0},{1,33},{33,65},{65,97},{97,1},{2,34}... | collective-permute-start | bytes 1572872 | tf_op jit(solution)/shard_map/ppermute | solution.py:19
  133.4 13.6 %collective-permute-start.13 = (bf16[512,512]{1,0:T(8,128)(2,1)S(1)}, bf16[512,512]{1,0:T(8,128)(2,1)}, u32[]{:S(2)}, u32[]{:S(2)}) collective-permute-start(bf16[512,512]{1,0:T(8,128)(2,1)S(1)} %get-tuple-element.43.refs_1_), channel_id=1, source_target_pairs={{0,96},{32,0},{64,32},{96,64},{1,97},{33,1},{65,33},{97,65},{2,98}... | collective-permute-start | bytes 1572872 | tf_op jit(solution)/shard_map/ppermute | solution.py:19
  153.3 16.2 %collective-permute-start.14 = (bf16[128,2816]{1,0:T(8,128)(2,1)S(1)}, bf16[128,2816]{1,0:T(8,128)(2,1)S(1)}, u32[]{:S(2)}, u32[]{:S(2)}) collective-permute-start(bf16[128,2816]{1,0:T(8,128)(2,1)S(1)} %get-tuple-element.47), channel_id=1, source_target_pairs={{0,96},{32,0},{64,32},{96,64},{1,97},{33,1},{65,33},{97,65},{2,98}... | collective-permute-start | bytes 2162696 | tf_op jit(solution)/shard_map/ppermute | solution.py:19
  156.2 16.4 %collective-permute-start.15 = (bf16[128,2816]{1,0:T(8,128)(2,1)S(1)}, bf16[128,2816]{1,0:T(8,128)(2,1)S(1)}, u32[]{:S(2)}, u32[]{:S(2)}) collective-permute-start(bf16[128,2816]{1,0:T(8,128)(2,1)S(1)} %get-tuple-element.48), channel_id=1, source_target_pairs={{0,32},{32,64},{64,96},{96,0},{1,33},{33,65},{65,97},{97,1},{2,34}... | collective-permute-start | bytes 2162696 | tf_op jit(solution)/shard_map/ppermute | solution.py:19
  164.3 10.7 %copy-start.22 = (bf16[256,1792]{1,0:T(8,128)(2,1)}, bf16[256,1792]{1,0:T(8,128)(2,1)S(1)}, u32[]{:S(2)}) copy-start(bf16[256,1792]{1,0:T(8,128)(2,1)S(1)} %get-tuple-element.59.a_ref) | copy-start | bytes 2752516
  175.1 31.8 %collective-permute-start.16 = (bf16[256,2048]{1,0:T(8,128)(2,1)}, bf16[256,2048]{1,0:T(8,128)(2,1)}, u32[]{:S(2)}, u32[]{:S(2)}) collective-permute-start(bf16[256,2048]{1,0:T(8,128)(2,1)} %get-tuple-element.53.refs_0_), channel_id=1, source_target_pairs={{0,32},{32,64},{64,96},{96,0},{1,33},{33,65},{65,97},{97,1},{2,34}... | collective-permute-start | bytes 3145736 | tf_op jit(solution)/shard_map/ppermute | solution.py:19
  175.1 31.8 %collective-permute-start.17 = (bf16[256,2048]{1,0:T(8,128)(2,1)}, bf16[256,2048]{1,0:T(8,128)(2,1)}, u32[]{:S(2)}, u32[]{:S(2)}) collective-permute-start(bf16[256,2048]{1,0:T(8,128)(2,1)} %get-tuple-element.54.refs_1_), channel_id=1, source_target_pairs={{0,96},{32,0},{64,32},{96,64},{1,97},{33,1},{65,33},{97,65},{2,98}... | collective-permute-start | bytes 3145736 | tf_op jit(solution)/shard_map/ppermute | solution.py:19
  190.9 3.6 %copy-start.18 = (bf16[256,512]{1,0:T(8,128)(2,1)}, bf16[256,512]{1,0:T(8,128)(2,1)S(1)}, u32[]{:S(2)}) copy-start(bf16[256,512]{1,0:T(8,128)(2,1)S(1)} %get-tuple-element.57.act_ref.a0) | copy-start | bytes 786436
  194.5 20.0 %collective-permute-start.19 = (bf16[128,2816]{1,0:T(8,128)(2,1)S(1)}, bf16[128,2816]{1,0:T(8,128)(2,1)S(1)}, u32[]{:S(2)}, u32[]{:S(2)}) collective-permute-start(bf16[128,2816]{1,0:T(8,128)(2,1)S(1)} %get-tuple-element.60), channel_id=1, source_target_pairs={{0,96},{32,0},{64,32},{96,64},{1,97},{33,1},{65,33},{97,65},{2,98}... | collective-permute-start | bytes 2162696 | tf_op jit(solution)/shard_map/ppermute | solution.py:19
  194.6 19.9 %collective-permute-start.18 = (bf16[128,2816]{1,0:T(8,128)(2,1)S(1)}, bf16[128,2816]{1,0:T(8,128)(2,1)S(1)}, u32[]{:S(2)}, u32[]{:S(2)}) collective-permute-start(bf16[128,2816]{1,0:T(8,128)(2,1)S(1)} %get-tuple-element.58.refs_5_), channel_id=1, source_target_pairs={{0,32},{32,64},{64,96},{96,0},{1,33},{33,65},{65,97},{97,1},{2,34}... | collective-permute-start | bytes 2162696 | tf_op jit(solution)/shard_map/ppermute | solution.py:19
  196.6 10.2 %copy-start.13 = (bf16[128,2816]{1,0:T(8,128)(2,1)S(1)}, bf16[128,2816]{1,0:T(8,128)(2,1)}, u32[]{:S(2)}) copy-start(bf16[128,2816]{1,0:T(8,128)(2,1)} %copy-done.12) | copy-start | bytes 2162692
  196.6 10.2 %copy-start.15 = (bf16[128,2816]{1,0:T(8,128)(2,1)S(1)}, bf16[128,2816]{1,0:T(8,128)(2,1)}, u32[]{:S(2)}) copy-start(bf16[128,2816]{1,0:T(8,128)(2,1)} %copy-done.14) | copy-start | bytes 2162692
  206.8 7.6 %copy-start.23 = (bf16[256,1792]{1,0:T(8,128)(2,1)S(1)}, bf16[256,1792]{1,0:T(8,128)(2,1)}, u32[]{:S(2)}) copy-start(bf16[256,1792]{1,0:T(8,128)(2,1)} %copy-done.22) | copy-start | bytes 2752516
  217.0 38.6 %all-to-all-start.3 = ((bf16[32,8,3584]{2,1,0:T(8,128)(2,1)}), bf16[32,8,3584]{2,1,0:T(8,128)(2,1)}, u32[]{:S(2)}, u32[]{:S(2)}) async-start(bf16[32,8,3584]{2,1,0:T(8,128)(2,1)} %bitcast.82), calls=%async_computation.3 | async-start | bytes 3670016 | tf_op jit(solution)/shard_map/all_to_all | solution.py:394
  224.1 6.9 %copy-start.9 = (bf16[256,1792]{1,0:T(8,128)(2,1)S(1)}, bf16[256,1792]{1,0:T(8,128)(2,1)}, u32[]{:S(2)}) copy-start(bf16[256,1792]{1,0:T(8,128)(2,1)} %copy-done.8) | copy-start | bytes 2752516
  224.1 10.5 %copy-start.5 = (bf16[256,1792]{1,0:T(8,128)(2,1)S(1)}, bf16[256,1792]{1,0:T(8,128)(2,1)}, u32[]{:S(2)}) copy-start(bf16[256,1792]{1,0:T(8,128)(2,1)} %copy-done.4) | copy-start | bytes 2752516
  224.1 10.5 %copy-start.19 = (bf16[256,512]{1,0:T(8,128)(2,1)S(1)}, bf16[256,512]{1,0:T(8,128)(2,1)}, u32[]{:S(2)}) copy-start(bf16[256,512]{1,0:T(8,128)(2,1)} %copy-done.18) | copy-start | bytes 786436
  224.2 6.9 %collective-permute-start.20 = (bf16[128,512]{1,0:T(8,128)(2,1)S(1)}, bf16[128,512]{1,0:T(8,128)(2,1)S(1)}, u32[]{:S(2)}, u32[]{:S(2)}) collective-permute-start(bf16[128,512]{1,0:T(8,128)(2,1)S(1)} %shard_map.151), channel_id=1, source_target_pairs={{0,32},{32,64},{64,96},{96,0},{1,33},{33,65},{65,97},{97,1},{2,34}... | collective-permute-start | bytes 393224 | tf_op jit(solution)/shard_map/ppermute | solution.py:19
  224.3 6.8 %collective-permute-start.21 = (bf16[128,512]{1,0:T(8,128)(2,1)S(1)}, bf16[128,512]{1,0:T(8,128)(2,1)S(1)}, u32[]{:S(2)}, u32[]{:S(2)}) collective-permute-start(bf16[128,512]{1,0:T(8,128)(2,1)S(1)} %shard_map.152), channel_id=1, source_target_pairs={{0,96},{32,0},{64,32},{96,64},{1,97},{33,1},{65,33},{97,65},{2,98}... | collective-permute-start | bytes 393224 | tf_op jit(solution)/shard_map/ppermute | solution.py:19
  231.3 3.3 %copy-start.2 = (bf16[256,1792]{1,0:T(8,128)(2,1)}, bf16[256,1792]{1,0:T(8,128)(2,1)S(1)}, u32[]{:S(2)}) copy-start(bf16[256,1792]{1,0:T(8,128)(2,1)S(1)} %get-tuple-element.65.refs_5_) | copy-start | bytes 2752516
  231.4 23.0 %collective-permute-start.22 = (bf16[256,1792]{1,0:T(8,128)(2,1)S(1)}, bf16[256,1792]{1,0:T(8,128)(2,1)S(1)}, u32[]{:S(2)}, u32[]{:S(2)}) collective-permute-start(bf16[256,1792]{1,0:T(8,128)(2,1)S(1)} %get-tuple-element.65.refs_5_), channel_id=1, source_target_pairs={{0,32},{32,64},{64,96},{96,0},{1,33},{33,65},{65,97},{97,1},{2,34}... | collective-permute-start | bytes 2752520 | tf_op jit(solution)/shard_map/ppermute | solution.py:19
  231.4 23.0 %copy-start.25 = (bf16[256,1792]{1,0:T(8,128)(2,1)S(1)}, bf16[256,1792]{1,0:T(8,128)(2,1)}, u32[]{:S(2)}) copy-start(bf16[256,1792]{1,0:T(8,128)(2,1)} %copy-done.24) | copy-start | bytes 2752516
  231.5 22.9 %collective-permute-start.23 = (bf16[256,1792]{1,0:T(8,128)(2,1)S(1)}, bf16[256,1792]{1,0:T(8,128)(2,1)S(1)}, u32[]{:S(2)}, u32[]{:S(2)}) collective-permute-start(bf16[256,1792]{1,0:T(8,128)(2,1)S(1)} %get-tuple-element.66.refs_6_), channel_id=1, source_target_pairs={{0,96},{32,0},{64,32},{96,64},{1,97},{33,1},{65,33},{97,65},{2,98}... | collective-permute-start | bytes 2752520 | tf_op jit(solution)/shard_map/ppermute | solution.py:19
  255.5 34.2 %all-to-all-start.4 = ((bf16[32,8,3584]{2,1,0:T(8,128)(2,1)}), bf16[32,8,3584]{2,1,0:T(8,128)(2,1)}, u32[]{:S(2)}, u32[]{:S(2)}) async-start(bf16[32,8,3584]{2,1,0:T(8,128)(2,1)} %bitcast.81), calls=%async_computation.4 | async-start | bytes 3670016 | tf_op jit(solution)/shard_map/all_to_all | solution.py:394
  265.9 25.4 %copy-start.42 = (f32[128]{0:T(128)S(1)}, f32[128]{0:T(128)}, u32[]{:S(2)}) copy-start(f32[128]{0:T(128)} %copy-done.41) | copy-start | bytes 1540
  266.0 25.4 %copy-start.44 = (f32[128]{0:T(128)S(1)}, f32[128]{0:T(128)}, u32[]{:S(2)}) copy-start(f32[128]{0:T(128)} %copy-done.43) | copy-start | bytes 1540
  270.9 23.3 %copy-start.32 = (bf16[128,7168]{1,0:T(8,128)(2,1)S(1)}, bf16[128,7168]{1,0:T(8,128)(2,1)}, u32[]{:S(2)}) copy-start(bf16[128,7168]{1,0:T(8,128)(2,1)} %param.10) | copy-start | bytes 5505028
  270.9 23.3 %copy-start.34 = (bf16[128,1792]{1,0:T(8,128)(2,1)S(1)}, bf16[128,1792]{1,0:T(8,128)(2,1)}, u32[]{:S(2)}) copy-start(bf16[128,1792]{1,0:T(8,128)(2,1)} %param.11) | copy-start | bytes 1376260
  289.8 4.5 %copy-start.35 = (f32[128,1792]{1,0:T(8,128)S(1)}, f32[128,1792]{1,0:T(8,128)}, u32[]{:S(2)}) copy-start(f32[128,1792]{1,0:T(8,128)} %fusion.17) | copy-start | bytes 2752516
  291.4 13.7 %copy-start.40 = (f32[128]{0:T(128)S(1)}, f32[128]{0:T(128)}, u32[]{:S(2)}) copy-start(f32[128]{0:T(128)} %copy-done.39) | copy-start | bytes 1540
  291.4 13.7 %copy-start.46 = (f32[128]{0:T(128)S(1)}, f32[128]{0:T(128)}, u32[]{:S(2)}) copy-start(f32[128]{0:T(128)} %get-tuple-element.87) | copy-start | bytes 1540
  291.4 13.7 %copy-start.47 = (f32[128]{0:T(128)S(1)}, f32[128]{0:T(128)}, u32[]{:S(2)}) copy-start(f32[128]{0:T(128)} %get-tuple-element.91) | copy-start | bytes 1540
  296.0 5.2 %collective-permute-start.25 = (f32[4,128]{1,0:T(4,128)S(1)}, f32[4,128]{1,0:T(4,128)S(1)}, u32[]{:S(2)}, u32[]{:S(2)}) collective-permute-start(f32[4,128]{1,0:T(4,128)S(1)} %pad_maximum_fusion.3), channel_id=1, source_target_pairs={{0,64},{32,96},{64,0},{96,32},{1,65},{33,97},{65,1},{97,33},{2,66}... | collective-permute-start | bytes 6152 | tf_op jit(solution)/shard_map/ppermute | solution.py:19
  298.8 3.6 %collective-permute-start.26 = (f32[4,128]{1,0:T(4,128)S(1)}, f32[4,128]{1,0:T(4,128)S(1)}, u32[]{:S(2)}, u32[]{:S(2)}) collective-permute-start(f32[4,128]{1,0:T(4,128)S(1)} %pad_maximum_fusion.3), channel_id=1, source_target_pairs={{0,96},{32,0},{64,32},{96,64},{1,97},{33,1},{65,33},{97,65},{2,98}... | collective-permute-start | bytes 6152 | tf_op jit(solution)/shard_map/ppermute | solution.py:19
  299.7 4.8 %collective-permute-start.24 = (f32[4,128]{1,0:T(4,128)S(1)}, f32[4,128]{1,0:T(4,128)S(1)}, u32[]{:S(2)}, u32[]{:S(2)}) collective-permute-start(f32[4,128]{1,0:T(4,128)S(1)} %pad_maximum_fusion.3), channel_id=1, source_target_pairs={{0,32},{32,64},{64,96},{96,0},{1,33},{33,65},{65,97},{97,1},{2,34}... | collective-permute-start | bytes 6152 | tf_op jit(solution)/shard_map/ppermute | solution.py:19
  (17 other events, 24.6 us)

commit v3 on v2

--- a/solution.py
+++ b/solution.py
@@ -388,6 +388,71 @@
         scratch_shapes=[pltpu.VMEM((count, units), BF)] * 3,
         compiler_params=params(),
     )(*acts, *downs, *others)
+
+
+def token_sums(returned, bases, selectors, scores, grads, hidden, emb, gain_hidden, gain_emb):
+    tokens, quarter = grads.shape
+    rows = returned.shape[0]
+    block = quarter // 2
+
+    def body(y, z, b0, b1, b2, s0, s1, score, grad, hid, em, gh, ge, moe, ig, sums):
+        first = b0[...] + jnp.dot(s0[...], y[...], preferred_element_type=F32)
+        second = b1[...] + jnp.dot(s1[...], y[...], preferred_element_type=F32)
+        both = s0[...] + s1[...]
+        inputs = b2[...] + jnp.dot(both, z[...], preferred_element_type=F32)
+        moe[...] = (score[:, 0:1] * first + score[:, 1:2] * second).astype(BF)
+        ig[...] = inputs
+        grad_f = grad[...].astype(F32)
+        terms = (
+            grad_f * first,
+            grad_f * second,
+            inputs * gh[...] * hid[...].astype(F32),
+            inputs * ge[...] * em[...].astype(F32),
+        )
+        lane = lax.broadcasted_iota(jnp.int32, (tokens, 128), 1)
+        total = jnp.zeros((tokens, 128), F32)
+        for k, term in enumerate(terms):
+            total = jnp.where(lane == k, jnp.sum(term, axis=1, keepdims=True), total)
+
+        @pl.when(pl.program_id(0) == 0)
+        def _():
+            sums[...] = total
+
+        @pl.when(pl.program_id(0) == 1)
+        def _():
+            sums[...] += total
+
+    columns = pl.BlockSpec((tokens, block), lambda j: (0, j))
+    gain = pl.BlockSpec((1, block), lambda j: (0, j))
+    held = pl.BlockSpec((tokens, rows), lambda j: (0, 0))
+    return pl.pallas_call(
+        body,
+        grid=(2,),
+        out_shape=[
+            jax.ShapeDtypeStruct((tokens, quarter), BF),
+            jax.ShapeDtypeStruct((tokens, quarter), F32),
+            jax.ShapeDtypeStruct((tokens, 128), F32),
+        ],
+        in_specs=[
+            pl.BlockSpec((rows, block), lambda j: (0, j)),
+            pl.BlockSpec((rows, block), lambda j: (0, 2 + j)),
+            columns,
+            columns,
+            columns,
+            held,
+            held,
+            pl.BlockSpec(scores.shape, lambda j: (0, 0)),
+            columns,
+            columns,
+            columns,
+            gain,
+            gain,
+        ],
+        out_specs=[columns, columns, pl.BlockSpec((tokens, 128), lambda j: (0, 0))],
+        compiler_params=params(),
+    )(
+        returned, returned, *bases, *selectors, scores, grads, hidden, emb, gain_hidden, gain_emb
+    )
 
 
 def exchange(value):
@@ -512,32 +577,29 @@
         )
     ]
     returned = [both.reshape(experts * part, 2 * quarter) for both in returned]
-    back = [both[:, :quarter] for both in returned]
-    grads_back = [both[:, quarter:] for both in returned]
-
-    route_outputs = [
-        sum(dot(part_selectors[h][k].astype(BF), back[h], ((1,), (0,))) for h in range(2))
-        for k in range(routes)
+    outputs_back, grads_back = returned[0][:, :quarter], returned[0][:, quarter:]
+    bases = [
+        dot(part_selectors[0][k].astype(BF), outputs_back, ((1,), (0,))) for k in range(routes)
     ]
-    moe_out = sum(gate_scores[:, k : k + 1] * route_outputs[k] for k in range(routes)).astype(BF)
-    input_grad = sum(dot(part_placement[h], grads_back[h], ((1,), (0,))) for h in range(2))
-
-    grad_f = output_grad.astype(F32)
-    hidden_cols = columns(hidden_rows, 0).astype(F32)
-    emb_cols = emb_rows.astype(F32)
-    gain_hidden_cols = lax.dynamic_slice_in_dim(gain_hidden, here * quarter, quarter, 0)
-    gain_emb_cols = lax.dynamic_slice_in_dim(gain_emb, here * quarter, quarter, 0)
-    partial = jnp.stack(
-        [jnp.sum(grad_f * route_outputs[k], axis=1) for k in range(routes)]
-        + [
-            jnp.sum(input_grad * gain_hidden_cols * hidden_cols, axis=1),
-            jnp.sum(input_grad * gain_emb_cols * emb_cols, axis=1),
-        ],
-        axis=0,
+    bases.append(dot(part_placement[0], grads_back, ((1,), (0,))))
+    hidden_cols = columns(hidden_rows, 0)
+    gain_hidden_cols = lax.dynamic_slice_in_dim(gain_hidden, here * quarter, quarter, 0)[None]
+    gain_emb_cols = lax.dynamic_slice_in_dim(gain_emb, here * quarter, quarter, 0)[None]
+    moe_out, input_grad, partial = token_sums(
+        returned[1],
+        bases,
+        [part_selectors[1][k].astype(BF) for k in range(routes)],
+        gate_scores,
+        output_grad,
+        hidden_cols,
+        emb_rows,
+        gain_hidden_cols,
+        gain_emb_cols,
     )
     total = partial + shift(partial, 1) + shift(partial, 2) + shift(partial, 3)
-    grad_gate = total[:routes].T
-    hidden_dot, emb_dot = total[routes][:, None], total[routes + 1][:, None]
+    grad_gate = total[:, :routes]
+    hidden_dot, emb_dot = total[:, routes : routes + 1], total[:, routes + 1 : routes + 2]
+    hidden_cols, emb_cols = hidden_cols.astype(F32), emb_rows.astype(F32)
     hidden_cube = hidden_scale * hidden_scale * hidden_scale
     emb_cube = emb_scale * emb_scale * emb_scale
     grad_hidden = gain_hidden_cols * input_grad / hidden_scale - hidden_cols * hidden_dot / (

time: 309 us -> 309 us (level)
  waiting for transfers between devices: 90.3 us -> 98.5 us
  matrix products: 24.4 us -> 18.2 us
  local copies, waits for them, and re-layouts: 21.4 us -> 16.8 us
  Pallas kernels: 80.6 us -> 84.9 us
    ppermute x27, waiting for transfers between devices: 53.7 us -> 63 us  [shift(): lax.ppermute(value, 'pp', [(i, (i + step) % ring) for i in range(ring)])]
    dot_general x10 -> x7, matrix products: 24.4 us -> 18.2 us  [dot(): lax.dot_general(left, right, (dims, ((), ())), preferred_element_type=F32)]
    pallas_call x0 -> x1, Pallas kernels: none -> 3.43 us  [token_sums(): pl.pallas_call(body, grid=(2,), out_shape=[jax.ShapeDtypeStruct((tokens,...]
    unnamed x104 -> x96, local copies, waits for them, and re-layouts: 15.5 us -> 13.2 us
  transfers between devices with their start and end apart: 32 -> 32, of which waited for: 14 -> 14; matrix products, arithmetic and copies ran while one was open for 11% -> 10% of each run, Pallas kernels for 25% -> 26%
where the time goes in v3:
time: 309 us; the launch traced here: 307 us
  waiting for transfers between devices  98.5 us (32%)
  Pallas kernels  84.9 us (27%)
  starting transfers between devices  76.6 us (25%)
  matrix products  18.2 us (6%)
  local copies, waits for them, and re-layouts  16.8 us (5%)
  other arithmetic  10.3 us (3%)
    ppermute x27, waiting for transfers between devices, shift(): lax.ppermute(value, 'pp', [(i, (i + step) % ring) for i in range(ring)])  63 us
    ppermute x27, starting transfers between devices, shift(): lax.ppermute(value, 'pp', [(i, (i + step) % ring) for i in range(ring)])  40.1 us
    all_to_all x5, starting transfers between devices, exchange(): return lax.all_to_all(value, 'ep', split_axis=0, concat_axis=0, tiled=True)  36.5 us
    all_to_all x5, waiting for transfers between devices, exchange(): return lax.all_to_all(value, 'ep', split_axis=0, concat_axis=0, tiled=True)  35.5 us
    pallas_call x2, Pallas kernels, forward(): pl.pallas_call(body, grid=(width // depth,), out_shape=[jax.ShapeDtypeStr...  20 us
    dot_general x7, matrix products, dot(): lax.dot_general(left, right, (dims, ((), ())), preferred_element_type=F32)  18.2 us
    pallas_call x2, Pallas kernels, backward_rest(): pl.pallas_call(body, grid_spec=pltpu.PrefetchScalarGridSpec(num_scalar_pr...  16.5 us
    pallas_call x2, Pallas kernels, down_product(): pl.pallas_call(body, grid=(quarter // block,), out_shape=jax.ShapeDtypeSt...  14.8 us
  transfers between devices with their start and end apart: 32, of which 14 were waited for; matrix products, arithmetic and copies ran while one was open for 10% of the time, Pallas kernels for 26%

profile of v3, /device:TPU:0, one launch (start us, length us, event | category | flops | bytes accessed | tf_op | source)
XLA Modules:
  0.0 306.8 jit_solution(6762591921791729026)
XLA Ops:
  0.6 2.9 collective-permute-start
  3.5 2.2 shard_map.129.refs_1_
  6.5 2.2 shard_map.130.refs_2_
  8.6 2.6 collective-permute-start.6
  13.0 2.0 multiply_convert_fusion.refs_0_
  15.0 8.5 %all-to-all-start = ((bf16[32,16,1792]{2,1,0:T(8,128)(2,1)}), bf16[32,16,1792]{2,1,0:T(8,128)(2,1)S(1)}, u32[]{:S(2)}, u32[]{:S(2)}) async-start(bf16[32,16,1792]{2,1,0:T(8,128)(2,1)} %bitcast.74), calls=%async_computation | async-start | bytes 3670016 | tf_op jit(solution)/shard_map/all_to_all | solution.py:459
  23.5 1.9 fusion
  25.5 2.0 collective-permute-start.3
  27.8 10.3 %collective-permute-done.3 = bf16[64,1792]{1,0:T(8,128)(2,1)S(1)} collective-permute-done((bf16[64,1792]{1,0:T(8,128)(2,1)S(1)}, bf16[64,1792]{1,0:T(8,128)(2,1)S(1)}, u32[]{:S(2)}, u32[]{:S(2)}) %collective-permute-start.3) | collective-permute-done | bytes 229408 | tf_op jit(solution)/shard_map/ppermute | solution.py:19
  38.1 3.4 %collective-permute-done.2 = bf16[64,1792]{1,0:T(8,128)(2,1)S(1)} collective-permute-done((bf16[64,1792]{1,0:T(8,128)(2,1)S(1)}, bf16[64,1792]{1,0:T(8,128)(2,1)S(1)}, u32[]{:S(2)}, u32[]{:S(2)}) %collective-permute-start.2) | collective-permute-done | bytes 229408 | tf_op jit(solution)/shard_map/ppermute | solution.py:19
  43.9 1.2 copy-done.33
  45.1 3.0 convolution_convert_fusion.refs_0_
  48.1 1.5 shard_map.135.refs_3_
  49.7 1.3 copy-done.6
  51.0 1.5 shard_map.136.refs_4_
  52.5 1.2 copy-done.7
  53.8 8.5 %all-to-all-start.2 = ((bf16[32,8,7168]{2,1,0:T(8,128)(2,1)}), bf16[32,8,7168]{2,1,0:T(8,128)(2,1)}, u32[]{:S(2)}, u32[]{:S(2)}) async-start(bf16[32,8,7168]{2,1,0:T(8,128)(2,1)} %bitcast.70), calls=%async_computation.2 | async-start | bytes 7340032 | tf_op jit(solution)/shard_map/all_to_all | solution.py:459
  62.3 3.2 %collective-permute-start.7 = (bf16[256,1792]{1,0:T(8,128)(2,1)}, bf16[256,1792]{1,0:T(8,128)(2,1)S(1)}, u32[]{:S(2)}, u32[]{:S(2)}) collective-permute-start(bf16[256,1792]{1,0:T(8,128)(2,1)} %collective-permute-done.6.refs_2_), channel_id=1, source_target_pairs={{0,96},{32,0},{64,32},{96,64},{1,97},{33,1},{65,33},{97,65},{2,98}... | collective-permute-start | bytes 2752520 | tf_op jit(solution)/shard_map/ppermute | solution.py:19
  65.6 2.0 collective-permute-start.9
  67.6 4.5 %convolution_convert_fusion.1.refs_0_ = bf16[256,7168]{1,0:T(8,128)(2,1)} fusion(bf16[128,7168]{1,0:T(8,128)(2,1)} %copy-done.33, s32[256]{0:T(256)S(1)} %iota_add_fusion, s32[128]{0:T(128)S(1)} %get-tuple-element.107, s32[128]{0:T(128)S(1)} %get-tuple-element.106), kind=kOutput, calls=%fused_computation.1 | convolution fusion | flops 471695360 | bytes 5507072 | tf_op jit(solution)/shard_map/dot_general | solution.py:14
  72.1 1.5 shard_map.133.refs_0_
  73.7 2.1 fusion.35.refs_3_.refs_0_
  75.8 11.1 %collective-permute-done.5.refs_0_.refs_3_ = bf16[256,1792]{1,0:T(8,128)(2,1)S(1)} collective-permute-done((bf16[256,1792]{1,0:T(8,128)(2,1)}, bf16[256,1792]{1,0:T(8,128)(2,1)S(1)}, u32[]{:S(2)}, u32[]{:S(2)}) %collective-permute-start.5) | collective-permute-done | bytes 917536 | tf_op jit(solution)/shard_map/ppermute | solution.py:19
  86.9 2.6 shard_map.132
  91.9 18.0 %all-to-all-done.2 = bf16[32,8,7168]{2,1,0:T(8,128)(2,1)} async-done(((bf16[32,8,7168]{2,1,0:T(8,128)(2,1)}), bf16[32,8,7168]{2,1,0:T(8,128)(2,1)}, u32[]{:S(2)}, u32[]{:S(2)}) %all-to-all-start.2) | async-done | bytes 3670048 | tf_op jit(solution)/shard_map/all_to_all | solution.py:459
  109.9 5.0 %all-to-all-start.1 = ((bf16[32,8,7168]{2,1,0:T(8,128)(2,1)}), bf16[32,8,7168]{2,1,0:T(8,128)(2,1)}, u32[]{:S(2)}, u32[]{:S(2)}) async-start(bf16[32,8,7168]{2,1,0:T(8,128)(2,1)} %bitcast.71), calls=%async_computation.1 | async-start | bytes 7340032 | tf_op jit(solution)/shard_map/all_to_all | solution.py:459
  115.0 3.2 %collective-permute-start.11 = (bf16[256,512]{1,0:T(8,128)(2,1)S(1)}, bf16[256,512]{1,0:T(8,128)(2,1)S(1)}, u32[]{:S(2)}, u32[]{:S(2)}) collective-permute-start(bf16[256,512]{1,0:T(8,128)(2,1)S(1)} %copy-done.30), channel_id=1, source_target_pairs={{0,96},{32,0},{64,32},{96,64},{1,97},{33,1},{65,33},{97,65},{2,98}... | collective-permute-start | bytes 786440 | tf_op jit(solution)/shard_map/ppermute | solution.py:19
  118.2 7.7 %collective-permute-done.8.refs_0_.refs_1_ = bf16[512,1792]{1,0:T(8,128)(2,1)} collective-permute-done((bf16[512,1792]{1,0:T(8,128)(2,1)}, bf16[512,1792]{1,0:T(8,128)(2,1)}, u32[]{:S(2)}, u32[]{:S(2)}) %collective-permute-start.8) | collective-permute-done | bytes 1835040 | tf_op jit(solution)/shard_map/ppermute | solution.py:19
  125.9 2.9 shard_map.138
  128.8 2.9 shard_map.139
  132.1 3.8 %collective-permute-start.13 = (bf16[512,512]{1,0:T(8,128)(2,1)S(1)}, bf16[512,512]{1,0:T(8,128)(2,1)}, u32[]{:S(2)}, u32[]{:S(2)}) collective-permute-start(bf16[512,512]{1,0:T(8,128)(2,1)S(1)} %get-tuple-element.46.refs_1_), channel_id=1, source_target_pairs={{0,96},{32,0},{64,32},{96,64},{1,97},{33,1},{65,33},{97,65},{2,98}... | collective-permute-start | bytes 1572872 | tf_op jit(solution)/shard_map/ppermute | solution.py:19
  135.8 10.0 %shard_map.141 = (f32[256,512]{1,0:T(8,128)S(1)}, f32[256,512]{1,0:T(8,128)S(1)}, bf16[256,512]{1,0:T(8,128)(2,1)S(1)}) custom-call(bf16[256,7168]{1,0:T(8,128)(2,1)} %bitcast.16.rows_ref, bf16[7168,512]{1,0:T(8,128)(2,1)} %bitcast.53, bf16[7168,512]{1,0:T(8,128)(2,1)} %bitcast.59, bf16[512,512]{1,0:T(8,128)(2,1)S(1)} %get-tuple-element.45.refs_0_, ...), custom_call_target="tpu_custom_call" | custom-call | tf_op jit(solution)/shard_map/pallas_call | solution.py:228
  146.5 2.2 collective-permute-done.12
  148.7 2.7 convert_add_fusion
  151.4 3.5 %shard_map.143 = (bf16[256,512]{1,0:T(8,128)(2,1)S(1)}, bf16[256,512]{1,0:T(8,128)(2,1)S(1)}, bf16[128,2816]{1,0:T(8,128)(2,1)S(1)}, bf16[128,2816]{1,0:T(8,128)(2,1)S(1)}) custom-call(s32[1]{0:T(128)} %bitcast.7.here_ref, f32[256,512]{1,0:T(8,128)S(1)} %get-tuple-element.47.gate_pre_ref, f32[256,512]{1,0:T(8,128)S(1)} %get-tuple-element.48.up_ref, ...), custom_call_target="tpu_custom_call" | custom-call | tf_op jit(solution)/shard_map/pallas_call | solution.py:276
  157.0 8.2 %shard_map.144 = (bf16[256,1792]{1,0:T(8,128)(2,1)S(1)}, bf16[256,1792]{1,0:T(8,128)(2,1)S(1)}, bf16[256,1792]{1,0:T(8,128)(2,1)S(1)}) custom-call(s32[1]{0:T(128)} %bitcast.7.here_ref, bf16[256,512]{1,0:T(8,128)(2,1)S(1)} %get-tuple-element.50.ggp, bf16[256,512]{1,0:T(8,128)(2,1)S(1)} %get-tuple-element.51.gup, bf16[7168,512]{1,0:T(8,128)(2,1)} %bitcast.55, ...), custom_call_target="tpu_custom_call" | custom-call | tf_op jit(solution)/shard_map/pallas_call | solution.py:327
  165.2 4.6 %collective-permute-done.15.above_ref.a1 = bf16[128,2816]{1,0:T(8,128)(2,1)S(1)} collective-permute-done((bf16[128,2816]{1,0:T(8,128)(2,1)S(1)}, bf16[128,2816]{1,0:T(8,128)(2,1)S(1)}, u32[]{:S(2)}, u32[]{:S(2)}) %collective-permute-start.15) | collective-permute-done | bytes 720928 | tf_op jit(solution)/shard_map/ppermute | solution.py:19
  169.8 2.7 collective-permute-done.14.below_ref.a3
  172.5 1.5 shard_map.145
  175.0 3.2 %collective-permute-start.23 = (bf16[256,2048]{1,0:T(8,128)(2,1)}, bf16[256,2048]{1,0:T(8,128)(2,1)}, u32[]{:S(2)}, u32[]{:S(2)}) collective-permute-start(bf16[256,2048]{1,0:T(8,128)(2,1)} %get-tuple-element.57.refs_1_), channel_id=1, source_target_pairs={{0,96},{32,0},{64,32},{96,64},{1,97},{33,1},{65,33},{97,65},{2,98}... | collective-permute-start | bytes 3145736 | tf_op jit(solution)/shard_map/ppermute | solution.py:19
  178.2 1.3 copy-done.23
  179.5 1.2 copy-done.24
  180.7 10.1 %shard_map.146 = (f32[256,512]{1,0:T(8,128)S(1)}, f32[256,512]{1,0:T(8,128)S(1)}, bf16[256,512]{1,0:T(8,128)(2,1)S(1)}) custom-call(bf16[256,7168]{1,0:T(8,128)(2,1)} %bitcast.12.rows_ref, bf16[7168,512]{1,0:T(8,128)(2,1)} %bitcast.56, bf16[7168,512]{1,0:T(8,128)(2,1)} %bitcast.62, bf16[256,2048]{1,0:T(8,128)(2,1)S(1)} %copy-done.24, ...), custom_call_target="tpu_custom_call" | custom-call | tf_op jit(solution)/shard_map/pallas_call | solution.py:228
  190.8 3.6 %shard_map.147 = (bf16[256,512]{1,0:T(8,128)(2,1)S(1)}, bf16[256,512]{1,0:T(8,128)(2,1)S(1)}, bf16[128,2816]{1,0:T(8,128)(2,1)S(1)}, bf16[128,2816]{1,0:T(8,128)(2,1)S(1)}) custom-call(s32[1]{0:T(128)} %bitcast.7.here_ref, f32[256,512]{1,0:T(8,128)S(1)} %get-tuple-element.59.gate_pre_ref, f32[256,512]{1,0:T(8,128)S(1)} %get-tuple-element.60.up_ref, ...), custom_call_target="tpu_custom_call" | custom-call | tf_op jit(solution)/shard_map/pallas_call | solution.py:276
  194.5 3.2 %collective-permute-start.16 = (bf16[128,2816]{1,0:T(8,128)(2,1)S(1)}, bf16[128,2816]{1,0:T(8,128)(2,1)S(1)}, u32[]{:S(2)}, u32[]{:S(2)}) collective-permute-start(bf16[128,2816]{1,0:T(8,128)(2,1)S(1)} %get-tuple-element.61), channel_id=1, source_target_pairs={{0,96},{32,0},{64,32},{96,64},{1,97},{33,1},{65,33},{97,65},{2,98}... | collective-permute-start | bytes 2162696 | tf_op jit(solution)/shard_map/ppermute | solution.py:19
  197.7 8.3 %shard_map.148 = (bf16[256,1792]{1,0:T(8,128)(2,1)S(1)}, bf16[256,1792]{1,0:T(8,128)(2,1)S(1)}, bf16[256,1792]{1,0:T(8,128)(2,1)S(1)}) custom-call(s32[1]{0:T(128)} %bitcast.7.here_ref, bf16[256,512]{1,0:T(8,128)(2,1)S(1)} %get-tuple-element.63.ggp, bf16[256,512]{1,0:T(8,128)(2,1)S(1)} %get-tuple-element.64.gup, bf16[7168,512]{1,0:T(8,128)(2,1)} %bitcast.58, ...), custom_call_target="tpu_custom_call" | custom-call | tf_op jit(solution)/shard_map/pallas_call | solution.py:327
  207.9 7.5 %shard_map.154.left_ref = bf16[256,3584]{1,0:T(8,128)(2,1)} custom-call(bf16[256,512]{1,0:T(8,128)(2,1)S(1)} %copy-done.18, bf16[128,2816]{1,0:T(8,128)(2,1)S(1)} %copy-done.14, bf16[128,2816]{1,0:T(8,128)(2,1)S(1)} %copy-done.16, bf16[256,2048]{1,0:T(8,128)(2,1)} %collective-permute-done.22.a2_low.b_ref, ...), custom_call_target="tpu_custom_call" | custom-call | tf_op jit(solution)/shard_map/pallas_call | solution.py:375
  215.5 2.5 shard_map.155
  217.9 7.3 %all-to-all-start.4 = ((bf16[32,8,3584]{2,1,0:T(8,128)(2,1)}), bf16[32,8,3584]{2,1,0:T(8,128)(2,1)}, u32[]{:S(2)}, u32[]{:S(2)}) async-start(bf16[32,8,3584]{2,1,0:T(8,128)(2,1)} %bitcast.73), calls=%async_computation.4 | async-start | bytes 3670016 | tf_op jit(solution)/shard_map/all_to_all | solution.py:459
  225.4 3.3 %collective-permute-start.19 = (bf16[128,512]{1,0:T(8,128)(2,1)S(1)}, bf16[128,512]{1,0:T(8,128)(2,1)S(1)}, u32[]{:S(2)}, u32[]{:S(2)}) collective-permute-start(bf16[128,512]{1,0:T(8,128)(2,1)S(1)} %shard_map.150), channel_id=1, source_target_pairs={{0,96},{32,0},{64,32},{96,64},{1,97},{33,1},{65,33},{97,65},{2,98}... | collective-permute-start | bytes 393224 | tf_op jit(solution)/shard_map/ppermute | solution.py:19
  228.7 3.5 %collective-permute-done.18.refs_0_.a2_low = bf16[128,512]{1,0:T(8,128)(2,1)S(1)} collective-permute-done((bf16[128,512]{1,0:T(8,128)(2,1)S(1)}, bf16[128,512]{1,0:T(8,128)(2,1)S(1)}, u32[]{:S(2)}, u32[]{:S(2)}) %collective-permute-start.18) | collective-permute-done | bytes 131104 | tf_op jit(solution)/shard_map/ppermute | solution.py:19
  232.6 3.2 %collective-permute-start.21 = (bf16[256,1792]{1,0:T(8,128)(2,1)S(1)}, bf16[256,1792]{1,0:T(8,128)(2,1)S(1)}, u32[]{:S(2)}, u32[]{:S(2)}) collective-permute-start(bf16[256,1792]{1,0:T(8,128)(2,1)S(1)} %get-tuple-element.68.refs_6_), channel_id=1, source_target_pairs={{0,96},{32,0},{64,32},{96,64},{1,97},{33,1},{65,33},{97,65},{2,98}... | collective-permute-start | bytes 2752520 | tf_op jit(solution)/shard_map/ppermute | solution.py:19
  235.8 7.3 %shard_map.152.left_ref = bf16[256,3584]{1,0:T(8,128)(2,1)} custom-call(bf16[256,512]{1,0:T(8,128)(2,1)S(1)} %copy-done.22, bf16[128,2816]{1,0:T(8,128)(2,1)S(1)} %collective-permute-done.16.extended_ref.above_ref.a1.refs_1_, bf16[128,2816]{1,0:T(8,128)(2,1)S(1)} %collective-permute-done.17.extended_ref.below_ref.a3.refs_0_, ...), custom_call_target="tpu_custom_call" | custom-call | tf_op jit(solution)/shard_map/pallas_call | solution.py:375
  243.1 12.4 %collective-permute-done.20.b_ref = bf16[256,1792]{1,0:T(8,128)(2,1)S(1)} collective-permute-done((bf16[256,1792]{1,0:T(8,128)(2,1)S(1)}, bf16[256,1792]{1,0:T(8,128)(2,1)S(1)}, u32[]{:S(2)}, u32[]{:S(2)}) %collective-permute-start.20) | collective-permute-done | bytes 917536 | tf_op jit(solution)/shard_map/ppermute | solution.py:19
  255.5 1.2 shard_map.153
  256.7 7.3 %all-to-all-start.3 = ((bf16[32,8,3584]{2,1,0:T(8,128)(2,1)}), bf16[32,8,3584]{2,1,0:T(8,128)(2,1)}, u32[]{:S(2)}, u32[]{:S(2)}) async-start(bf16[32,8,3584]{2,1,0:T(8,128)(2,1)} %bitcast.72), calls=%async_computation.3 | async-start | bytes 3670016 | tf_op jit(solution)/shard_map/all_to_all | solution.py:459
  267.0 1.5 fusion.10.b0
  268.5 2.4 fusion.8.b1
  271.0 2.5 fusion.6.b2
  273.5 17.5 %all-to-all-done.3 = bf16[32,8,3584]{2,1,0:T(8,128)(2,1)} async-done(((bf16[32,8,3584]{2,1,0:T(8,128)(2,1)}), bf16[32,8,3584]{2,1,0:T(8,128)(2,1)}, u32[]{:S(2)}, u32[]{:S(2)}) %all-to-all-start.3) | async-done | bytes 1835040 | tf_op jit(solution)/shard_map/all_to_all | solution.py:459
  291.0 3.4 %shard_map.156 = (bf16[128,1792]{1,0:T(8,128)(2,1)}, f32[128,1792]{1,0:T(8,128)S(1)}, f32[128,128]{1,0:T(8,128)S(1)}) custom-call(bf16[256,3584]{1,0:T(8,128)(2,1)} %bitcast.19.y.z, bf16[256,3584]{1,0:T(8,128)(2,1)} %bitcast.19.y.z, f32[128,1792]{1,0:T(8,128)S(1)} %fusion.10.b0, f32[128,1792]{1,0:T(8,128)} %fusion.8.b1, f32[128,1792]{1,0:T(8,128)} %fusion.6.b2, ...), custom_call_target="tpu_custom_call" | custom-call | tf_op jit(solution)/shard_map/pallas_call | solution.py:428
  294.4 2.9 collective-permute-start.26
  299.2 4.0 %collective-permute-done.25 = f32[128,128]{1,0:T(8,128)S(1)} collective-permute-done((f32[128,128]{1,0:T(8,128)S(1)}, f32[128,128]{1,0:T(8,128)S(1)}, u32[]{:S(2)}, u32[]{:S(2)}) %collective-permute-start.25) | collective-permute-done | bytes 65568 | tf_op jit(solution)/shard_map/ppermute | solution.py:19
  304.4 2.4 subtract_convert_fusion
  (169 shorter events, 20.0 us)
Async XLA Ops:
  0.6 24.9 %collective-permute-start = (bf16[128,1792]{1,0:T(8,128)(2,1)}, bf16[128,1792]{1,0:T(8,128)(2,1)S(1)}, u32[]{:S(2)}, u32[]{:S(2)}) collective-permute-start(bf16[128,1792]{1,0:T(8,128)(2,1)} %em.1), channel_id=1, source_target_pairs={{0,96},{32,0},{64,32},{96,64},{1,97},{33,1},{65,33},{97,65},{2,98}... | collective-permute-start | bytes 1376264 | tf_op jit(solution)/shard_map/ppermute | solution.py:19
  3.5 24.0 %collective-permute-start.1 = (bf16[128,1792]{1,0:T(8,128)(2,1)}, bf16[128,1792]{1,0:T(8,128)(2,1)S(1)}, u32[]{:S(2)}, u32[]{:S(2)}) collective-permute-start(bf16[128,1792]{1,0:T(8,128)(2,1)} %em.1), channel_id=1, source_target_pairs={{0,32},{32,64},{64,96},{96,0},{1,33},{33,65},{65,97},{97,1},{2,34}... | collective-permute-start | bytes 1376264 | tf_op jit(solution)/shard_map/ppermute | solution.py:19
  5.7 5.5 %copy-start.41 = (s32[128,2]{0,1:T(2,128)S(1)}, s32[128,2]{0,1:T(2,128)}, u32[]{:S(2)}) copy-start(s32[128,2]{0,1:T(2,128)} %param.12) | copy-start | bytes 3076
  5.7 7.1 %copy-start.39 = (f32[128,2]{0,1:T(2,128)S(1)}, f32[128,2]{0,1:T(2,128)}, u32[]{:S(2)}) copy-start(f32[128,2]{0,1:T(2,128)} %param.13) | copy-start | bytes 3076
  5.7 7.2 %copy-start.19 = (bf16[128,1792]{1,0:T(8,128)(2,1)S(1)}, bf16[128,1792]{1,0:T(8,128)(2,1)}, u32[]{:S(2)}) copy-start(bf16[128,1792]{1,0:T(8,128)(2,1)} %grad.1) | copy-start | bytes 1376260
  5.7 48.0 %collective-permute-start.4 = (bf16[256,1792]{1,0:T(8,128)(2,1)}, bf16[256,1792]{1,0:T(8,128)(2,1)}, u32[]{:S(2)}, u32[]{:S(2)}) collective-permute-start(bf16[256,1792]{1,0:T(8,128)(2,1)} %shard_map.129.refs_1_), channel_id=1, source_target_pairs={{0,32},{32,64},{64,96},{96,0},{1,33},{33,65},{65,97},{97,1},{2,34}... | collective-permute-start | bytes 2752520 | tf_op jit(solution)/shard_map/ppermute | solution.py:19
  8.6 45.1 %collective-permute-start.6 = (bf16[256,1792]{1,0:T(8,128)(2,1)}, bf16[256,1792]{1,0:T(8,128)(2,1)}, u32[]{:S(2)}, u32[]{:S(2)}) collective-permute-start(bf16[256,1792]{1,0:T(8,128)(2,1)} %shard_map.130.refs_2_), channel_id=1, source_target_pairs={{0,96},{32,0},{64,32},{96,64},{1,97},{33,1},{65,33},{97,65},{2,98}... | collective-permute-start | bytes 2752520 | tf_op jit(solution)/shard_map/ppermute | solution.py:19
  15.0 10.4 %copy-start.8 = (bf16[128,1792]{1,0:T(8,128)(2,1)S(1)}, bf16[128,1792]{1,0:T(8,128)(2,1)}, u32[]{:S(2)}) copy-start(bf16[128,1792]{1,0:T(8,128)(2,1)} %em.1) | copy-start | bytes 1376260
  15.0 38.7 %all-to-all-start = ((bf16[32,16,1792]{2,1,0:T(8,128)(2,1)}), bf16[32,16,1792]{2,1,0:T(8,128)(2,1)S(1)}, u32[]{:S(2)}, u32[]{:S(2)}) async-start(bf16[32,16,1792]{2,1,0:T(8,128)(2,1)} %bitcast.74), calls=%async_computation | async-start | bytes 3670016 | tf_op jit(solution)/shard_map/all_to_all | solution.py:459
  25.5 12.6 %collective-permute-start.3 = (bf16[64,1792]{1,0:T(8,128)(2,1)S(1)}, bf16[64,1792]{1,0:T(8,128)(2,1)S(1)}, u32[]{:S(2)}, u32[]{:S(2)}) collective-permute-start(bf16[64,1792]{1,0:T(8,128)(2,1)S(1)} %slice.64), channel_id=1, source_target_pairs={{0,96},{32,0},{64,32},{96,64},{1,97},{33,1},{65,33},{97,65},{2,98}... | collective-permute-start | bytes 688136 | tf_op jit(solution)/shard_map/ppermute | solution.py:19
  27.6 13.9 %collective-permute-start.2 = (bf16[64,1792]{1,0:T(8,128)(2,1)S(1)}, bf16[64,1792]{1,0:T(8,128)(2,1)S(1)}, u32[]{:S(2)}, u32[]{:S(2)}) collective-permute-start(bf16[64,1792]{1,0:T(8,128)(2,1)S(1)} %slice.63), channel_id=1, source_target_pairs={{0,32},{32,64},{64,96},{96,0},{1,33},{33,65},{65,97},{97,1},{2,34}... | collective-permute-start | bytes 688136 | tf_op jit(solution)/shard_map/ppermute | solution.py:19
  27.8 15.1 %copy-start.34 = (bf16[128,7168]{1,0:T(8,128)(2,1)S(1)}, bf16[128,7168]{1,0:T(8,128)(2,1)}, u32[]{:S(2)}) copy-start(bf16[128,7168]{1,0:T(8,128)(2,1)} %param.10) | copy-start | bytes 5505028
  27.8 15.1 %copy-start.35 = (f32[7168]{0:T(1024)S(1)}, f32[7168]{0:T(1024)}, u32[]{:S(2)}) copy-start(f32[7168]{0:T(1024)} %param.14) | copy-start | bytes 86020
  27.8 15.1 %copy-start.36 = (f32[7168]{0:T(1024)S(1)}, f32[7168]{0:T(1024)}, u32[]{:S(2)}) copy-start(f32[7168]{0:T(1024)} %param.15) | copy-start | bytes 86020
  42.9 5.3 %copy-start.37 = (f32[128]{0:T(128)}, f32[128]{0:T(128)S(1)}, u32[]{:S(2)}) copy-start(f32[128]{0:T(128)S(1)} %get-tuple-element.112) | copy-start | bytes 1540
  53.7 19.9 %copy-start = (bf16[32,16,1792]{2,1,0:T(8,128)(2,1)}, bf16[32,16,1792]{2,1,0:T(8,128)(2,1)S(1)}, u32[]{:S(2)}) copy-start(bf16[32,16,1792]{2,1,0:T(8,128)(2,1)S(1)} %all-to-all-done) | copy-start | bytes 5505028
  53.8 56.1 %all-to-all-start.2 = ((bf16[32,8,7168]{2,1,0:T(8,128)(2,1)}), bf16[32,8,7168]{2,1,0:T(8,128)(2,1)}, u32[]{:S(2)}, u32[]{:S(2)}) async-start(bf16[32,8,7168]{2,1,0:T(8,128)(2,1)} %bitcast.70), calls=%async_computation.2 | async-start | bytes 7340032 | tf_op jit(solution)/shard_map/all_to_all | solution.py:459
  62.2 24.7 %collective-permute-start.5 = (bf16[256,1792]{1,0:T(8,128)(2,1)}, bf16[256,1792]{1,0:T(8,128)(2,1)S(1)}, u32[]{:S(2)}, u32[]{:S(2)}) collective-permute-start(bf16[256,1792]{1,0:T(8,128)(2,1)} %collective-permute-done.4.refs_1_), channel_id=1, source_target_pairs={{0,32},{32,64},{64,96},{96,0},{1,33},{33,65},{65,97},{97,1},{2,34}... | collective-permute-start | bytes 2752520 | tf_op jit(solution)/shard_map/ppermute | solution.py:19
  62.3 24.6 %collective-permute-start.7 = (bf16[256,1792]{1,0:T(8,128)(2,1)}, bf16[256,1792]{1,0:T(8,128)(2,1)S(1)}, u32[]{:S(2)}, u32[]{:S(2)}) collective-permute-start(bf16[256,1792]{1,0:T(8,128)(2,1)} %collective-permute-done.6.refs_2_), channel_id=1, source_target_pairs={{0,96},{32,0},{64,32},{96,64},{1,97},{33,1},{65,33},{97,65},{2,98}... | collective-permute-start | bytes 2752520 | tf_op jit(solution)/shard_map/ppermute | solution.py:19
  65.5 60.4 %collective-permute-start.8 = (bf16[512,1792]{1,0:T(8,128)(2,1)}, bf16[512,1792]{1,0:T(8,128)(2,1)}, u32[]{:S(2)}, u32[]{:S(2)}) collective-permute-start(bf16[512,1792]{1,0:T(8,128)(2,1)} %copy-done.7), channel_id=1, source_target_pairs={{0,96},{32,0},{64,32},{96,64},{1,97},{33,1},{65,33},{97,65},{2,98}... | collective-permute-start | bytes 5505032 | tf_op jit(solution)/shard_map/ppermute | solution.py:19
  65.6 63.3 %collective-permute-start.9 = (bf16[512,1792]{1,0:T(8,128)(2,1)}, bf16[512,1792]{1,0:T(8,128)(2,1)}, u32[]{:S(2)}, u32[]{:S(2)}) collective-permute-start(bf16[512,1792]{1,0:T(8,128)(2,1)} %copy-done.6), channel_id=1, source_target_pairs={{0,32},{32,64},{64,96},{96,0},{1,33},{33,65},{65,97},{97,1},{2,34}... | collective-permute-start | bytes 5505032 | tf_op jit(solution)/shard_map/ppermute | solution.py:19
  73.6 2.2 copy-start.3
  109.9 5.0 %copy-start.32 = (bf16[256,512]{1,0:T(8,128)(2,1)S(1)}, bf16[256,512]{1,0:T(8,128)(2,1)}, u32[]{:S(2)}) copy-start(bf16[256,512]{1,0:T(8,128)(2,1)} %copy-done.31) | copy-start | bytes 786436
  109.9 5.1 %copy-start.30 = (bf16[256,512]{1,0:T(8,128)(2,1)S(1)}, bf16[256,512]{1,0:T(8,128)(2,1)}, u32[]{:S(2)}) copy-start(bf16[256,512]{1,0:T(8,128)(2,1)} %copy-done.29) | copy-start | bytes 786436
  109.9 16.0 %copy-start.1 = (bf16[32,16,1792]{2,1,0:T(8,128)(2,1)S(1)}, bf16[32,16,1792]{2,1,0:T(8,128)(2,1)}, u32[]{:S(2)}) copy-start(bf16[32,16,1792]{2,1,0:T(8,128)(2,1)} %copy-done) | copy-start | bytes 5505028
  109.9 68.3 %all-to-all-start.1 = ((bf16[32,8,7168]{2,1,0:T(8,128)(2,1)}), bf16[32,8,7168]{2,1,0:T(8,128)(2,1)}, u32[]{:S(2)}, u32[]{:S(2)}) async-start(bf16[32,8,7168]{2,1,0:T(8,128)(2,1)} %bitcast.71), calls=%async_computation.1 | async-start | bytes 7340032 | tf_op jit(solution)/shard_map/all_to_all | solution.py:459
  114.9 17.0 %collective-permute-start.10 = (bf16[256,512]{1,0:T(8,128)(2,1)S(1)}, bf16[256,512]{1,0:T(8,128)(2,1)S(1)}, u32[]{:S(2)}, u32[]{:S(2)}) collective-permute-start(bf16[256,512]{1,0:T(8,128)(2,1)S(1)} %copy-done.32), channel_id=1, source_target_pairs={{0,32},{32,64},{64,96},{96,0},{1,33},{33,65},{65,97},{97,1},{2,34}... | collective-permute-start | bytes 786440 | tf_op jit(solution)/shard_map/ppermute | solution.py:19
  115.0 16.9 %collective-permute-start.11 = (bf16[256,512]{1,0:T(8,128)(2,1)S(1)}, bf16[256,512]{1,0:T(8,128)(2,1)S(1)}, u32[]{:S(2)}, u32[]{:S(2)}) collective-permute-start(bf16[256,512]{1,0:T(8,128)(2,1)S(1)} %copy-done.30), channel_id=1, source_target_pairs={{0,96},{32,0},{64,32},{96,64},{1,97},{33,1},{65,33},{97,65},{2,98}... | collective-permute-start | bytes 786440 | tf_op jit(solution)/shard_map/ppermute | solution.py:19
  132.1 14.5 %collective-permute-start.13 = (bf16[512,512]{1,0:T(8,128)(2,1)S(1)}, bf16[512,512]{1,0:T(8,128)(2,1)}, u32[]{:S(2)}, u32[]{:S(2)}) collective-permute-start(bf16[512,512]{1,0:T(8,128)(2,1)S(1)} %get-tuple-element.46.refs_1_), channel_id=1, source_target_pairs={{0,96},{32,0},{64,32},{96,64},{1,97},{33,1},{65,33},{97,65},{2,98}... | collective-permute-start | bytes 1572872 | tf_op jit(solution)/shard_map/ppermute | solution.py:19
  135.8 12.9 %collective-permute-start.12 = (bf16[512,512]{1,0:T(8,128)(2,1)S(1)}, bf16[512,512]{1,0:T(8,128)(2,1)}, u32[]{:S(2)}, u32[]{:S(2)}) collective-permute-start(bf16[512,512]{1,0:T(8,128)(2,1)S(1)} %get-tuple-element.45.refs_0_), channel_id=1, source_target_pairs={{0,32},{32,64},{64,96},{96,0},{1,33},{33,65},{65,97},{97,1},{2,34}... | collective-permute-start | bytes 1572872 | tf_op jit(solution)/shard_map/ppermute | solution.py:19
  146.5 4.9 %copy-start.18 = (bf16[256,512]{1,0:T(8,128)(2,1)S(1)}, bf16[256,512]{1,0:T(8,128)(2,1)}, u32[]{:S(2)}) copy-start(bf16[256,512]{1,0:T(8,128)(2,1)} %copy-done.17) | copy-start | bytes 786436
  154.9 14.9 %collective-permute-start.15 = (bf16[128,2816]{1,0:T(8,128)(2,1)S(1)}, bf16[128,2816]{1,0:T(8,128)(2,1)S(1)}, u32[]{:S(2)}, u32[]{:S(2)}) collective-permute-start(bf16[128,2816]{1,0:T(8,128)(2,1)S(1)} %get-tuple-element.55), channel_id=1, source_target_pairs={{0,96},{32,0},{64,32},{96,64},{1,97},{33,1},{65,33},{97,65},{2,98}... | collective-permute-start | bytes 2162696 | tf_op jit(solution)/shard_map/ppermute | solution.py:19
  156.1 16.4 %collective-permute-start.14 = (bf16[128,2816]{1,0:T(8,128)(2,1)S(1)}, bf16[128,2816]{1,0:T(8,128)(2,1)S(1)}, u32[]{:S(2)}, u32[]{:S(2)}) collective-permute-start(bf16[128,2816]{1,0:T(8,128)(2,1)S(1)} %get-tuple-element.54), channel_id=1, source_target_pairs={{0,32},{32,64},{64,96},{96,0},{1,33},{33,65},{65,97},{97,1},{2,34}... | collective-permute-start | bytes 2162696 | tf_op jit(solution)/shard_map/ppermute | solution.py:19
  165.2 9.8 %copy-start.25 = (bf16[256,1792]{1,0:T(8,128)(2,1)}, bf16[256,1792]{1,0:T(8,128)(2,1)S(1)}, u32[]{:S(2)}) copy-start(bf16[256,1792]{1,0:T(8,128)(2,1)S(1)} %get-tuple-element.70.a_ref) | copy-start | bytes 2752516
  172.5 1.6 copy-start.15
  175.0 32.9 %collective-permute-start.22 = (bf16[256,2048]{1,0:T(8,128)(2,1)}, bf16[256,2048]{1,0:T(8,128)(2,1)}, u32[]{:S(2)}, u32[]{:S(2)}) collective-permute-start(bf16[256,2048]{1,0:T(8,128)(2,1)} %get-tuple-element.56.refs_0_), channel_id=1, source_target_pairs={{0,32},{32,64},{64,96},{96,0},{1,33},{33,65},{65,97},{97,1},{2,34}... | collective-permute-start | bytes 3145736 | tf_op jit(solution)/shard_map/ppermute | solution.py:19
  175.0 32.9 %collective-permute-start.23 = (bf16[256,2048]{1,0:T(8,128)(2,1)}, bf16[256,2048]{1,0:T(8,128)(2,1)}, u32[]{:S(2)}, u32[]{:S(2)}) collective-permute-start(bf16[256,2048]{1,0:T(8,128)(2,1)} %get-tuple-element.57.refs_1_), channel_id=1, source_target_pairs={{0,96},{32,0},{64,32},{96,64},{1,97},{33,1},{65,33},{97,65},{2,98}... | collective-permute-start | bytes 3145736 | tf_op jit(solution)/shard_map/ppermute | solution.py:19
  190.7 3.6 %copy-start.21 = (bf16[256,512]{1,0:T(8,128)(2,1)}, bf16[256,512]{1,0:T(8,128)(2,1)S(1)}, u32[]{:S(2)}) copy-start(bf16[256,512]{1,0:T(8,128)(2,1)S(1)} %get-tuple-element.58.act_ref.a0) | copy-start | bytes 786436
  194.4 21.1 %collective-permute-start.17 = (bf16[128,2816]{1,0:T(8,128)(2,1)S(1)}, bf16[128,2816]{1,0:T(8,128)(2,1)S(1)}, u32[]{:S(2)}, u32[]{:S(2)}) collective-permute-start(bf16[128,2816]{1,0:T(8,128)(2,1)S(1)} %get-tuple-element.62.refs_5_), channel_id=1, source_target_pairs={{0,32},{32,64},{64,96},{96,0},{1,33},{33,65},{65,97},{97,1},{2,34}... | collective-permute-start | bytes 2162696 | tf_op jit(solution)/shard_map/ppermute | solution.py:19
  194.5 21.0 %collective-permute-start.16 = (bf16[128,2816]{1,0:T(8,128)(2,1)S(1)}, bf16[128,2816]{1,0:T(8,128)(2,1)S(1)}, u32[]{:S(2)}, u32[]{:S(2)}) collective-permute-start(bf16[128,2816]{1,0:T(8,128)(2,1)S(1)} %get-tuple-element.61), channel_id=1, source_target_pairs={{0,96},{32,0},{64,32},{96,64},{1,97},{33,1},{65,33},{97,65},{2,98}... | collective-permute-start | bytes 2162696 | tf_op jit(solution)/shard_map/ppermute | solution.py:19
  197.7 10.2 %copy-start.14 = (bf16[128,2816]{1,0:T(8,128)(2,1)S(1)}, bf16[128,2816]{1,0:T(8,128)(2,1)}, u32[]{:S(2)}) copy-start(bf16[128,2816]{1,0:T(8,128)(2,1)} %copy-done.13) | copy-start | bytes 2162692
  197.7 10.2 %copy-start.16 = (bf16[128,2816]{1,0:T(8,128)(2,1)S(1)}, bf16[128,2816]{1,0:T(8,128)(2,1)}, u32[]{:S(2)}) copy-start(bf16[128,2816]{1,0:T(8,128)(2,1)} %copy-done.15) | copy-start | bytes 2162692
  207.9 7.6 %copy-start.26 = (bf16[256,1792]{1,0:T(8,128)(2,1)S(1)}, bf16[256,1792]{1,0:T(8,128)(2,1)}, u32[]{:S(2)}) copy-start(bf16[256,1792]{1,0:T(8,128)(2,1)} %copy-done.25) | copy-start | bytes 2752516
  217.9 38.8 %all-to-all-start.4 = ((bf16[32,8,3584]{2,1,0:T(8,128)(2,1)}), bf16[32,8,3584]{2,1,0:T(8,128)(2,1)}, u32[]{:S(2)}, u32[]{:S(2)}) async-start(bf16[32,8,3584]{2,1,0:T(8,128)(2,1)} %bitcast.73), calls=%async_computation.4 | async-start | bytes 3670016 | tf_op jit(solution)/shard_map/all_to_all | solution.py:459
  225.3 6.9 %copy-start.11 = (bf16[256,1792]{1,0:T(8,128)(2,1)S(1)}, bf16[256,1792]{1,0:T(8,128)(2,1)}, u32[]{:S(2)}) copy-start(bf16[256,1792]{1,0:T(8,128)(2,1)} %copy-done.10) | copy-start | bytes 2752516
  225.3 10.5 %copy-start.5 = (bf16[256,1792]{1,0:T(8,128)(2,1)S(1)}, bf16[256,1792]{1,0:T(8,128)(2,1)}, u32[]{:S(2)}) copy-start(bf16[256,1792]{1,0:T(8,128)(2,1)} %copy-done.4) | copy-start | bytes 2752516
  225.3 10.5 %copy-start.22 = (bf16[256,512]{1,0:T(8,128)(2,1)S(1)}, bf16[256,512]{1,0:T(8,128)(2,1)}, u32[]{:S(2)}) copy-start(bf16[256,512]{1,0:T(8,128)(2,1)} %copy-done.21) | copy-start | bytes 786436
  225.3 6.9 %collective-permute-start.18 = (bf16[128,512]{1,0:T(8,128)(2,1)S(1)}, bf16[128,512]{1,0:T(8,128)(2,1)S(1)}, u32[]{:S(2)}, u32[]{:S(2)}) collective-permute-start(bf16[128,512]{1,0:T(8,128)(2,1)S(1)} %shard_map.149), channel_id=1, source_target_pairs={{0,32},{32,64},{64,96},{96,0},{1,33},{33,65},{65,97},{97,1},{2,34}... | collective-permute-start | bytes 393224 | tf_op jit(solution)/shard_map/ppermute | solution.py:19
  225.4 6.8 %collective-permute-start.19 = (bf16[128,512]{1,0:T(8,128)(2,1)S(1)}, bf16[128,512]{1,0:T(8,128)(2,1)S(1)}, u32[]{:S(2)}, u32[]{:S(2)}) collective-permute-start(bf16[128,512]{1,0:T(8,128)(2,1)S(1)} %shard_map.150), channel_id=1, source_target_pairs={{0,96},{32,0},{64,32},{96,64},{1,97},{33,1},{65,33},{97,65},{2,98}... | collective-permute-start | bytes 393224 | tf_op jit(solution)/shard_map/ppermute | solution.py:19
  232.5 3.3 %copy-start.2 = (bf16[256,1792]{1,0:T(8,128)(2,1)}, bf16[256,1792]{1,0:T(8,128)(2,1)S(1)}, u32[]{:S(2)}) copy-start(bf16[256,1792]{1,0:T(8,128)(2,1)S(1)} %get-tuple-element.67.refs_5_) | copy-start | bytes 2752516
  232.5 3.3 %copy-start.12 = (bf16[256,1792]{1,0:T(8,128)(2,1)}, bf16[256,1792]{1,0:T(8,128)(2,1)S(1)}, u32[]{:S(2)}) copy-start(bf16[256,1792]{1,0:T(8,128)(2,1)S(1)} %get-tuple-element.68.refs_6_) | copy-start | bytes 2752516
  232.5 23.0 %collective-permute-start.20 = (bf16[256,1792]{1,0:T(8,128)(2,1)S(1)}, bf16[256,1792]{1,0:T(8,128)(2,1)S(1)}, u32[]{:S(2)}, u32[]{:S(2)}) collective-permute-start(bf16[256,1792]{1,0:T(8,128)(2,1)S(1)} %get-tuple-element.67.refs_5_), channel_id=1, source_target_pairs={{0,32},{32,64},{64,96},{96,0},{1,33},{33,65},{65,97},{97,1},{2,34}... | collective-permute-start | bytes 2752520 | tf_op jit(solution)/shard_map/ppermute | solution.py:19
  232.6 23.0 %copy-start.28 = (bf16[256,1792]{1,0:T(8,128)(2,1)S(1)}, bf16[256,1792]{1,0:T(8,128)(2,1)}, u32[]{:S(2)}) copy-start(bf16[256,1792]{1,0:T(8,128)(2,1)} %copy-done.27) | copy-start | bytes 2752516
  232.6 22.9 %collective-permute-start.21 = (bf16[256,1792]{1,0:T(8,128)(2,1)S(1)}, bf16[256,1792]{1,0:T(8,128)(2,1)S(1)}, u32[]{:S(2)}, u32[]{:S(2)}) collective-permute-start(bf16[256,1792]{1,0:T(8,128)(2,1)S(1)} %get-tuple-element.68.refs_6_), channel_id=1, source_target_pairs={{0,96},{32,0},{64,32},{96,64},{1,97},{33,1},{65,33},{97,65},{2,98}... | collective-permute-start | bytes 2752520 | tf_op jit(solution)/shard_map/ppermute | solution.py:19
  255.5 8.5 %copy-start.40 = (f32[128,2]{0,1:T(2,128)S(1)}, f32[128,2]{0,1:T(2,128)}, u32[]{:S(2)}) copy-start(f32[128,2]{0,1:T(2,128)} %param.13) | copy-start | bytes 3076
  256.7 34.2 %all-to-all-start.3 = ((bf16[32,8,3584]{2,1,0:T(8,128)(2,1)}), bf16[32,8,3584]{2,1,0:T(8,128)(2,1)}, u32[]{:S(2)}, u32[]{:S(2)}) async-start(bf16[32,8,3584]{2,1,0:T(8,128)(2,1)} %bitcast.72), calls=%async_computation.3 | async-start | bytes 3670016 | tf_op jit(solution)/shard_map/all_to_all | solution.py:459
  264.0 26.9 %copy-start.9 = (bf16[128,1792]{1,0:T(8,128)(2,1)S(1)}, bf16[128,1792]{1,0:T(8,128)(2,1)}, u32[]{:S(2)}) copy-start(bf16[128,1792]{1,0:T(8,128)(2,1)} %em.1) | copy-start | bytes 1376260
  264.0 26.9 %copy-start.20 = (bf16[128,1792]{1,0:T(8,128)(2,1)S(1)}, bf16[128,1792]{1,0:T(8,128)(2,1)}, u32[]{:S(2)}) copy-start(bf16[128,1792]{1,0:T(8,128)(2,1)} %grad.1) | copy-start | bytes 1376260
  290.9 13.4 %copy-start.38 = (f32[128]{0:T(128)S(1)}, f32[128]{0:T(128)}, u32[]{:S(2)}) copy-start(f32[128]{0:T(128)} %copy-done.37) | copy-start | bytes 1540
  290.9 13.4 %copy-start.42 = (f32[128]{0:T(128)S(1)}, f32[128]{0:T(128)}, u32[]{:S(2)}) copy-start(f32[128]{0:T(128)} %get-tuple-element.110) | copy-start | bytes 1540
  291.0 13.4 %copy-start.43 = (f32[128]{0:T(128)S(1)}, f32[128]{0:T(128)}, u32[]{:S(2)}) copy-start(f32[128]{0:T(128)} %get-tuple-element.113) | copy-start | bytes 1540
  294.4 4.8 %collective-permute-start.26 = (f32[128,128]{1,0:T(8,128)S(1)}, f32[128,128]{1,0:T(8,128)S(1)}, u32[]{:S(2)}, u32[]{:S(2)}) collective-permute-start(f32[128,128]{1,0:T(8,128)S(1)} %get-tuple-element.72), channel_id=1, source_target_pairs={{0,96},{32,0},{64,32},{96,64},{1,97},{33,1},{65,33},{97,65},{2,98}... | collective-permute-start | bytes 196616 | tf_op jit(solution)/shard_map/ppermute | solution.py:19
  297.3 5.9 %collective-permute-start.25 = (f32[128,128]{1,0:T(8,128)S(1)}, f32[128,128]{1,0:T(8,128)S(1)}, u32[]{:S(2)}, u32[]{:S(2)}) collective-permute-start(f32[128,128]{1,0:T(8,128)S(1)} %get-tuple-element.72), channel_id=1, source_target_pairs={{0,64},{32,96},{64,0},{96,32},{1,65},{33,97},{65,1},{97,33},{2,66}... | collective-permute-start | bytes 196616 | tf_op jit(solution)/shard_map/ppermute | solution.py:19
  297.3 6.2 %collective-permute-start.24 = (f32[128,128]{1,0:T(8,128)S(1)}, f32[128,128]{1,0:T(8,128)S(1)}, u32[]{:S(2)}, u32[]{:S(2)}) collective-permute-start(f32[128,128]{1,0:T(8,128)S(1)} %get-tuple-element.72), channel_id=1, source_target_pairs={{0,32},{32,64},{64,96},{96,0},{1,33},{33,65},{65,97},{97,1},{2,34}... | collective-permute-start | bytes 196616 | tf_op jit(solution)/shard_map/ppermute | solution.py:19
  (12 other events, 12.0 us)

commit v4 on v2

--- a/solution.py
+++ b/solution.py
@@ -144,12 +144,9 @@
     )(extended, *others)
 
 
-def cut_columns(here, array, offset, part, *others):
-    rows, width = array.shape
-    quarter = width // 4
-    steps = 2 if part is None else 1
-    first = 0 if part is None else part
-    block = rows // 2
+def cut_columns(here, array, offset, first, rows, *others):
+    quarter = array.shape[1] // 4
+    block = 128
 
     def body(here_ref, array_ref, *refs):
         refs[-1][...] = array_ref[...]
@@ -158,14 +155,16 @@
         body,
         grid_spec=pltpu.PrefetchScalarGridSpec(
             num_scalar_prefetch=1,
-            grid=(steps,),
+            grid=(rows // block,),
             in_specs=[
-                pl.BlockSpec((block, quarter), lambda i, here: (i + first, (here[0] + offset) % 4))
+                pl.BlockSpec(
+                    (block, quarter), lambda i, here: (i + first // block, (here[0] + offset) % 4)
+                )
             ]
             + [ANYWHERE] * len(others),
             out_specs=pl.BlockSpec((block, quarter), lambda i, here: (i, 0)),
         ),
-        out_shape=jax.ShapeDtypeStruct((block * steps, quarter), array.dtype),
+        out_shape=jax.ShapeDtypeStruct((rows, quarter), array.dtype),
         compiler_params=params(),
     )(here, array, *others)
 
@@ -361,9 +360,11 @@
         total = jnp.dot(a0[...], down_refs[0][...], preferred_element_type=F32)
         total += jnp.dot(above[...], down_refs[1][...], preferred_element_type=F32)
         total += jnp.dot(below[...], down_refs[2][...], preferred_element_type=F32)
-        for part in range(2):
-            left = far[:, part * half_units : (part + 1) * half_units]
-            total += jnp.dot(left, down_refs[3 + part][...], preferred_element_type=F32)
+        start = 0
+        for piece, ref in zip(downs[3:], down_refs[3:]):
+            left = far[:, start : start + piece.shape[0]]
+            total += jnp.dot(left, ref[...], preferred_element_type=F32)
+            start += piece.shape[0]
         out[...] = total.astype(BF)
 
     def held(array):
@@ -447,12 +448,16 @@
     emb_pieces = [emb_own, emb_above, jnp.concatenate([emb_low, emb_high], axis=0), emb_below]
 
     place = here.reshape(1)
-    down_low, down_high = (cut_columns(place, down_mat, 2, i) for i in range(2))
-    pass_low, pass_high = shift(down_low, 1), shift(down_high, -1)
-    far_low, far_high = shift(pass_low, 1), shift(pass_high, -1)
+    fourth = hidden_units // 4
+    down_far = [cut_columns(place, down_mat, 2, i * fourth, fourth) for i in range(4)]
+    ways = (1, 1, -1, -1)
+    passing = [None] * 4
+    for i in (0, 2, 1, 3):
+        passing[i] = shift(down_far[i], ways[i])
+    far_pieces = [shift(passing[i], ways[i]) for i in range(4)]
 
     grad_send = (dot(placement, output_grad, ((0,), (0,))) * slot_score[:, None]).astype(BF)
-    grad_send = after(grad_send, down_low, down_high)
+    grad_send = after(grad_send, *down_far)
     grad_slots = exchange(grad_send.reshape(experts, capacity, quarter))
     grad_slots = grad_slots.reshape(experts * capacity, quarter)
 
@@ -466,19 +471,21 @@
     send_rows = [
         dot(part_placement[h], mixed_input, ((0,), (0,))).astype(BF) for h in range(2)
     ]
-    down_up = cut_columns(place, down_mat, 1, None, send_rows[0])
-    down_back = cut_columns(place, down_mat, 3, None, send_rows[0])
+    down_up = cut_columns(place, down_mat, 1, 0, hidden_units, passing[0])
+    down_back = cut_columns(place, down_mat, 3, 0, hidden_units, passing[0])
     down_below, down_above = shift(down_up, 1), shift(down_back, -1)
-    down_own = cut_columns(place, down_mat, 0, None, grad_slots)
-    far = inner_share(grad_slots, (far_low, far_high))
+    down_own = cut_columns(place, down_mat, 0, 0, hidden_units, grad_slots)
+    far = inner_share(grad_slots, far_pieces)
     own = dot(grad_slots, down_own, ((1,), (1,)))
-    send_rows[0] = after(send_rows[0], pass_low, pass_high, down_up, down_back)
+    send_rows[0] = after(
+        send_rows[0], *passing, far_pieces[0], far_pieces[2], down_up, down_back
+    )
     send_rows[1] = after(send_rows[1], *far, own)
     arrived = [
         exchange(send_rows[h].reshape(experts, part, width)).reshape(experts * part, width)
         for h in range(2)
     ]
-    downs = (down_own, down_above, down_below, far_low, far_high)
+    downs = (down_own, down_above, down_below, *far_pieces)
     up = jnp.concatenate(inner_share(grad_slots, (down_above,)), axis=0)
     down = jnp.concatenate(inner_share(grad_slots, (down_below,)), axis=0)
     came = shift(far[0], 1), shift(far[1], -1)

time: 309 us -> 309 us (level)
  Pallas kernels: 80.6 us -> 87.1 us
  waiting for transfers between devices: 90.3 us -> 84 us
    ppermute x27 -> x31, waiting for transfers between devices: 53.7 us -> 38.4 us  [shift(): lax.ppermute(value, 'pp', [(i, (i + step) % ring) for i in range(ring)])]
    all_to_all x5, waiting for transfers between devices: 36.6 us -> 45.6 us  [exchange(): return lax.all_to_all(value, 'ep', split_axis=0, concat_axis=0, tiled=True)]
    pallas_call x5 -> x7, Pallas kernels: 8.07 us -> 12.8 us  [cut_columns(): pl.pallas_call(body, grid_spec=pltpu.PrefetchScalarGridSpec(num_scalar_pr...]
    unnamed x104 -> x130, local copies, waits for them, and re-layouts: 15.5 us -> 13.1 us
    ppermute x27 -> x31, starting transfers between devices: 42.8 us -> 45.2 us  [shift(): lax.ppermute(value, 'pp', [(i, (i + step) % ring) for i in range(ring)])]
  transfers between devices with their start and end apart: 32 -> 36, of which waited for: 14 -> 13; matrix products, arithmetic and copies ran while one was open for 11% -> 12% of each run, Pallas kernels for 25% -> 28%
where the time goes in v4:
time: 309 us; the launch traced here: 306 us
  Pallas kernels  87.1 us (28%)
  waiting for transfers between devices  84 us (27%)
  starting transfers between devices  80.9 us (26%)
  matrix products  24.5 us (8%)
  local copies, waits for them, and re-layouts  18.9 us (6%)
  other arithmetic  9.12 us (3%)
    all_to_all x5, waiting for transfers between devices, exchange(): return lax.all_to_all(value, 'ep', split_axis=0, concat_axis=0, tiled=True)  45.6 us
    ppermute x31, starting transfers between devices, shift(): lax.ppermute(value, 'pp', [(i, (i + step) % ring) for i in range(ring)])  45.2 us
    ppermute x31, waiting for transfers between devices, shift(): lax.ppermute(value, 'pp', [(i, (i + step) % ring) for i in range(ring)])  38.4 us
    all_to_all x5, starting transfers between devices, exchange(): return lax.all_to_all(value, 'ep', split_axis=0, concat_axis=0, tiled=True)  35.7 us
    dot_general x10, matrix products, dot(): lax.dot_general(left, right, (dims, ((), ())), preferred_element_type=F32)  24.5 us
    pallas_call x2, Pallas kernels, forward(): pl.pallas_call(body, grid=(width // depth,), out_shape=[jax.ShapeDtypeStr...  19.9 us
    pallas_call x2, Pallas kernels, backward_rest(): pl.pallas_call(body, grid_spec=pltpu.PrefetchScalarGridSpec(num_scalar_pr...  16.6 us
    pallas_call x2, Pallas kernels, down_product(): pl.pallas_call(body, grid=(quarter // block,), out_shape=jax.ShapeDtypeSt...  15.5 us
  transfers between devices with their start and end apart: 36, of which 13 were waited for; matrix products, arithmetic and copies ran while one was open for 12% of the time, Pallas kernels for 28%

profile of v4, /device:TPU:0, one launch (start us, length us, event | category | flops | bytes accessed | tf_op | source)
XLA Modules:
  0.0 306.2 jit_solution(3363726435156064078)
XLA Ops:
  0.6 2.9 collective-permute-start
  5.4 1.8 shard_map.130.refs_2_
  7.3 1.5 collective-permute-start.5
  9.8 1.8 collective-permute-start.6
  12.0 1.9 shard_map.132.refs_4_
  15.3 2.1 multiply_convert_fusion.refs_0_
  17.4 8.3 %all-to-all-start.1 = ((bf16[32,16,1792]{2,1,0:T(8,128)(2,1)}), bf16[32,16,1792]{2,1,0:T(8,128)(2,1)S(1)}, u32[]{:S(2)}, u32[]{:S(2)}) async-start(bf16[32,16,1792]{2,1,0:T(8,128)(2,1)} %bitcast.85), calls=%async_computation.1 | async-start | bytes 3670016 | tf_op jit(solution)/shard_map/all_to_all | solution.py:395
  25.7 1.9 fusion
  28.8 1.4 collective-permute-start.7
  31.2 2.0 collective-permute-start.3
  34.3 2.3 shard_map.133.refs_7_
  37.9 2.4 shard_map.134.refs_8_
  40.3 1.4 constant_dynamic-update-slice_fusion.4
  42.4 4.2 %collective-permute-done.3 = bf16[64,1792]{1,0:T(8,128)(2,1)S(1)} collective-permute-done((bf16[64,1792]{1,0:T(8,128)(2,1)S(1)}, bf16[64,1792]{1,0:T(8,128)(2,1)S(1)}, u32[]{:S(2)}, u32[]{:S(2)}) %collective-permute-start.3) | collective-permute-done | bytes 229408 | tf_op jit(solution)/shard_map/ppermute | solution.py:19
  46.7 2.6 collective-permute-start.9
  54.6 3.1 %convolution_convert_fusion.1.refs_0_ = bf16[256,7168]{1,0:T(8,128)(2,1)} fusion(bf16[128,7168]{1,0:T(8,128)(2,1)S(1)} %fusion.3, s32[128]{0:T(128)S(1)} %get-tuple-element.84, s32[128]{0:T(128)S(1)} %get-tuple-element.83), kind=kOutput, calls=%fused_computation.1 | convolution fusion | flops 471695360 | bytes 5506048 | tf_op jit(solution)/shard_map/dot_general | solution.py:14
  60.1 7.5 %all-to-all-start = ((bf16[32,8,7168]{2,1,0:T(8,128)(2,1)}), bf16[32,8,7168]{2,1,0:T(8,128)(2,1)}, u32[]{:S(2)}, u32[]{:S(2)}) async-start(bf16[32,8,7168]{2,1,0:T(8,128)(2,1)} %bitcast.82), calls=%async_computation | async-start | bytes 7340032 | tf_op jit(solution)/shard_map/all_to_all | solution.py:395
  68.3 2.6 collective-permute-start.13
  70.9 1.9 collective-permute-start.10
  72.9 4.5 %convolution_convert_fusion.refs_0_ = bf16[256,7168]{1,0:T(8,128)(2,1)} fusion(bf16[128,7168]{1,0:T(8,128)(2,1)} %copy-done.41, s32[256]{0:T(256)S(1)} %iota_add_fusion, s32[128]{0:T(128)S(1)} %get-tuple-element.84, s32[128]{0:T(128)S(1)} %get-tuple-element.83), kind=kOutput, calls=%fused_computation | convolution fusion | flops 471695360 | bytes 5507072 | tf_op jit(solution)/shard_map/dot_general | solution.py:14
  77.5 2.4 shard_map.142.refs_0_
  79.9 2.5 collective-permute-done.12.refs_1_.refs_4_
  82.4 3.8 %shard_map.139 = (bf16[256,512]{1,0:T(8,128)(2,1)S(1)}, bf16[256,512]{1,0:T(8,128)(2,1)S(1)}) custom-call(bf16[512,1792]{1,0:T(8,128)(2,1)} %bitcast.58, bf16[128,1792]{1,0:T(8,128)(2,1)S(1)} %copy-done.7, bf16[128,1792]{1,0:T(8,128)(2,1)S(1)} %collective-permute-done.12.refs_1_.refs_4_, bf16[128,1792]{1,0:T(8,128)(2,1)S(1)} %copy-done.9, ...), custom_call_target="tpu_custom_call" | custom-call | tf_op jit(solution)/shard_map/pallas_call | solution.py:191
  86.3 2.1 fusion.57.refs_0_.refs_3_
  88.5 26.8 %all-to-all-done = bf16[32,8,7168]{2,1,0:T(8,128)(2,1)} async-done(((bf16[32,8,7168]{2,1,0:T(8,128)(2,1)}), bf16[32,8,7168]{2,1,0:T(8,128)(2,1)}, u32[]{:S(2)}, u32[]{:S(2)}) %all-to-all-start) | async-done | bytes 3670048 | tf_op jit(solution)/shard_map/all_to_all | solution.py:395
  115.3 5.0 %all-to-all-start.2 = ((bf16[32,8,7168]{2,1,0:T(8,128)(2,1)}), bf16[32,8,7168]{2,1,0:T(8,128)(2,1)}, u32[]{:S(2)}, u32[]{:S(2)}) async-start(bf16[32,8,7168]{2,1,0:T(8,128)(2,1)} %bitcast.81), calls=%async_computation.2 | async-start | bytes 7340032 | tf_op jit(solution)/shard_map/all_to_all | solution.py:395
  120.9 2.6 collective-permute-start.15
  123.6 2.9 shard_map.137
  126.5 2.9 shard_map.138
  130.2 3.1 %collective-permute-start.17 = (bf16[512,512]{1,0:T(8,128)(2,1)S(1)}, bf16[512,512]{1,0:T(8,128)(2,1)}, u32[]{:S(2)}, u32[]{:S(2)}) collective-permute-start(bf16[512,512]{1,0:T(8,128)(2,1)S(1)} %get-tuple-element.43.refs_1_), channel_id=1, source_target_pairs={{0,96},{32,0},{64,32},{96,64},{1,97},{33,1},{65,33},{97,65},{2,98}... | collective-permute-start | bytes 1572872 | tf_op jit(solution)/shard_map/ppermute | solution.py:19
  133.3 10.0 %shard_map.141 = (f32[256,512]{1,0:T(8,128)S(1)}, f32[256,512]{1,0:T(8,128)S(1)}, bf16[256,512]{1,0:T(8,128)(2,1)S(1)}) custom-call(bf16[256,7168]{1,0:T(8,128)(2,1)} %bitcast.7.rows_ref, bf16[7168,512]{1,0:T(8,128)(2,1)} %bitcast.69, bf16[7168,512]{1,0:T(8,128)(2,1)} %bitcast.75, bf16[512,512]{1,0:T(8,128)(2,1)S(1)} %get-tuple-element.42.refs_0_, ...), custom_call_target="tpu_custom_call" | custom-call | tf_op jit(solution)/shard_map/pallas_call | solution.py:227
  144.0 3.5 %collective-permute-done.16 = bf16[512,512]{1,0:T(8,128)(2,1)} collective-permute-done((bf16[512,512]{1,0:T(8,128)(2,1)S(1)}, bf16[512,512]{1,0:T(8,128)(2,1)}, u32[]{:S(2)}, u32[]{:S(2)}) %collective-permute-start.16) | collective-permute-done | bytes 524320 | tf_op jit(solution)/shard_map/ppermute | solution.py:19
  147.5 2.7 convert_add_fusion
  150.2 3.5 %shard_map.144 = (bf16[256,512]{1,0:T(8,128)(2,1)S(1)}, bf16[256,512]{1,0:T(8,128)(2,1)S(1)}, bf16[128,2816]{1,0:T(8,128)(2,1)S(1)}, bf16[128,2816]{1,0:T(8,128)(2,1)S(1)}) custom-call(s32[1]{0:T(128)} %bitcast.4.here_ref, f32[256,512]{1,0:T(8,128)S(1)} %get-tuple-element.45.gate_pre_ref, f32[256,512]{1,0:T(8,128)S(1)} %get-tuple-element.46.up_ref, ...), custom_call_target="tpu_custom_call" | custom-call | tf_op jit(solution)/shard_map/pallas_call | solution.py:275
  154.1 1.7 collective-permute-start.19
  155.8 8.2 %shard_map.145 = (bf16[256,1792]{1,0:T(8,128)(2,1)S(1)}, bf16[256,1792]{1,0:T(8,128)(2,1)S(1)}, bf16[256,1792]{1,0:T(8,128)(2,1)S(1)}) custom-call(s32[1]{0:T(128)} %bitcast.4.here_ref, bf16[256,512]{1,0:T(8,128)(2,1)S(1)} %get-tuple-element.49.ggp, bf16[256,512]{1,0:T(8,128)(2,1)S(1)} %get-tuple-element.50.gup, bf16[7168,512]{1,0:T(8,128)(2,1)} %bitcast.71, ...), custom_call_target="tpu_custom_call" | custom-call | tf_op jit(solution)/shard_map/pallas_call | solution.py:326
  164.0 6.0 %collective-permute-done.18.above_ref.a1 = bf16[128,2816]{1,0:T(8,128)(2,1)S(1)} collective-permute-done((bf16[128,2816]{1,0:T(8,128)(2,1)S(1)}, bf16[128,2816]{1,0:T(8,128)(2,1)S(1)}, u32[]{:S(2)}, u32[]{:S(2)}) %collective-permute-start.18) | collective-permute-done | bytes 720928 | tf_op jit(solution)/shard_map/ppermute | solution.py:19
  170.0 1.5 collective-permute-done.19.below_ref.a3
  171.5 1.6 shard_map.146
  174.2 3.0 collective-permute-start.21
  177.2 1.3 copy-done.30
  179.7 10.0 %shard_map.148 = (f32[256,512]{1,0:T(8,128)S(1)}, f32[256,512]{1,0:T(8,128)S(1)}, bf16[256,512]{1,0:T(8,128)(2,1)S(1)}) custom-call(bf16[256,7168]{1,0:T(8,128)(2,1)} %bitcast.17.rows_ref, bf16[7168,512]{1,0:T(8,128)(2,1)} %bitcast.72, bf16[7168,512]{1,0:T(8,128)(2,1)} %bitcast.78, bf16[256,2048]{1,0:T(8,128)(2,1)S(1)} %copy-done.31, ...), custom_call_target="tpu_custom_call" | custom-call | tf_op jit(solution)/shard_map/pallas_call | solution.py:227
  189.7 3.6 %shard_map.149 = (bf16[256,512]{1,0:T(8,128)(2,1)S(1)}, bf16[256,512]{1,0:T(8,128)(2,1)S(1)}, bf16[128,2816]{1,0:T(8,128)(2,1)S(1)}, bf16[128,2816]{1,0:T(8,128)(2,1)S(1)}) custom-call(s32[1]{0:T(128)} %bitcast.4.here_ref, f32[256,512]{1,0:T(8,128)S(1)} %get-tuple-element.55.gate_pre_ref, f32[256,512]{1,0:T(8,128)S(1)} %get-tuple-element.56.up_ref, ...), custom_call_target="tpu_custom_call" | custom-call | tf_op jit(solution)/shard_map/pallas_call | solution.py:275
  193.3 3.2 %collective-permute-start.23 = (bf16[128,2816]{1,0:T(8,128)(2,1)S(1)}, bf16[128,2816]{1,0:T(8,128)(2,1)S(1)}, u32[]{:S(2)}, u32[]{:S(2)}) collective-permute-start(bf16[128,2816]{1,0:T(8,128)(2,1)S(1)} %get-tuple-element.60), channel_id=1, source_target_pairs={{0,96},{32,0},{64,32},{96,64},{1,97},{33,1},{65,33},{97,65},{2,98}... | collective-permute-start | bytes 2162696 | tf_op jit(solution)/shard_map/ppermute | solution.py:19
  196.6 8.4 %shard_map.151 = (bf16[256,1792]{1,0:T(8,128)(2,1)S(1)}, bf16[256,1792]{1,0:T(8,128)(2,1)S(1)}, bf16[256,1792]{1,0:T(8,128)(2,1)S(1)}) custom-call(s32[1]{0:T(128)} %bitcast.4.here_ref, bf16[256,512]{1,0:T(8,128)(2,1)S(1)} %get-tuple-element.61.ggp, bf16[256,512]{1,0:T(8,128)(2,1)S(1)} %get-tuple-element.62.gup, bf16[7168,512]{1,0:T(8,128)(2,1)} %bitcast.74, ...), custom_call_target="tpu_custom_call" | custom-call | tf_op jit(solution)/shard_map/pallas_call | solution.py:326
  206.0 8.0 %shard_map.150.left_ref = bf16[256,3584]{1,0:T(8,128)(2,1)} custom-call(bf16[256,512]{1,0:T(8,128)(2,1)S(1)} %copy-done.25, bf16[128,2816]{1,0:T(8,128)(2,1)S(1)} %copy-done.21, bf16[128,2816]{1,0:T(8,128)(2,1)S(1)} %copy-done.23, bf16[256,2048]{1,0:T(8,128)(2,1)} %collective-permute-done.20.a2_low.b_ref, ...), custom_call_target="tpu_custom_call" | custom-call | tf_op jit(solution)/shard_map/pallas_call | solution.py:376
  214.0 2.5 shard_map.152
  216.5 7.6 %all-to-all-start.3 = ((bf16[32,8,3584]{2,1,0:T(8,128)(2,1)}), bf16[32,8,3584]{2,1,0:T(8,128)(2,1)}, u32[]{:S(2)}, u32[]{:S(2)}) async-start(bf16[32,8,3584]{2,1,0:T(8,128)(2,1)} %bitcast.84), calls=%async_computation.3 | async-start | bytes 3670016 | tf_op jit(solution)/shard_map/all_to_all | solution.py:395
  224.3 3.3 %collective-permute-start.25 = (bf16[128,512]{1,0:T(8,128)(2,1)S(1)}, bf16[128,512]{1,0:T(8,128)(2,1)S(1)}, u32[]{:S(2)}, u32[]{:S(2)}) collective-permute-start(bf16[128,512]{1,0:T(8,128)(2,1)S(1)} %shard_map.154), channel_id=1, source_target_pairs={{0,96},{32,0},{64,32},{96,64},{1,97},{33,1},{65,33},{97,65},{2,98}... | collective-permute-start | bytes 393224 | tf_op jit(solution)/shard_map/ppermute | solution.py:19
  227.6 3.5 %collective-permute-done.24.refs_0_.a2_low = bf16[128,512]{1,0:T(8,128)(2,1)S(1)} collective-permute-done((bf16[128,512]{1,0:T(8,128)(2,1)S(1)}, bf16[128,512]{1,0:T(8,128)(2,1)S(1)}, u32[]{:S(2)}, u32[]{:S(2)}) %collective-permute-start.24) | collective-permute-done | bytes 131104 | tf_op jit(solution)/shard_map/ppermute | solution.py:19
  231.8 2.9 collective-permute-start.27
  234.7 7.5 %shard_map.156.left_ref = bf16[256,3584]{1,0:T(8,128)(2,1)} custom-call(bf16[256,512]{1,0:T(8,128)(2,1)S(1)} %copy-done.29, bf16[128,2816]{1,0:T(8,128)(2,1)S(1)} %collective-permute-done.23.refs_1_.extended_ref.above_ref.a1, bf16[128,2816]{1,0:T(8,128)(2,1)S(1)} %collective-permute-done.22.refs_0_.extended_ref.below_ref.a3, ...), custom_call_target="tpu_custom_call" | custom-call | tf_op jit(solution)/shard_map/pallas_call | solution.py:376
  242.2 12.2 %collective-permute-done.26.b_ref = bf16[256,1792]{1,0:T(8,128)(2,1)S(1)} collective-permute-done((bf16[256,1792]{1,0:T(8,128)(2,1)S(1)}, bf16[256,1792]{1,0:T(8,128)(2,1)S(1)}, u32[]{:S(2)}, u32[]{:S(2)}) %collective-permute-start.26) | collective-permute-done | bytes 917536 | tf_op jit(solution)/shard_map/ppermute | solution.py:19
  255.5 7.3 %all-to-all-start.4 = ((bf16[32,8,3584]{2,1,0:T(8,128)(2,1)}), bf16[32,8,3584]{2,1,0:T(8,128)(2,1)}, u32[]{:S(2)}, u32[]{:S(2)}) async-start(bf16[32,8,3584]{2,1,0:T(8,128)(2,1)} %bitcast.83), calls=%async_computation.4 | async-start | bytes 3670016 | tf_op jit(solution)/shard_map/all_to_all | solution.py:395
  264.4 1.5 fusion.21
  266.0 2.4 fusion.23
  268.4 2.6 fusion.17
  271.0 18.8 %all-to-all-done.4 = bf16[32,8,3584]{2,1,0:T(8,128)(2,1)} async-done(((bf16[32,8,3584]{2,1,0:T(8,128)(2,1)}), bf16[32,8,3584]{2,1,0:T(8,128)(2,1)}, u32[]{:S(2)}, u32[]{:S(2)}) %all-to-all-start.4) | async-done | bytes 1835040 | tf_op jit(solution)/shard_map/all_to_all | solution.py:395
  289.8 1.6 convolution_add_fusion.1
  291.4 2.8 fusion.6
  294.2 1.8 fusion.8
  296.0 3.0 collective-permute-start.30
  300.4 3.8 %collective-permute-done.29 = f32[4,128]{1,0:T(4,128)S(1)} collective-permute-done((f32[4,128]{1,0:T(4,128)S(1)}, f32[4,128]{1,0:T(4,128)S(1)}, u32[]{:S(2)}, u32[]{:S(2)}) %collective-permute-start.29) | collective-permute-done | bytes 2080 | tf_op jit(solution)/shard_map/ppermute | solution.py:19
  304.8 1.4 fusion.15
  (212 shorter events, 29.7 us)
Async XLA Ops:
  0.6 28.1 %collective-permute-start = (bf16[128,1792]{1,0:T(8,128)(2,1)}, bf16[128,1792]{1,0:T(8,128)(2,1)}, u32[]{:S(2)}, u32[]{:S(2)}) collective-permute-start(bf16[128,1792]{1,0:T(8,128)(2,1)} %param.11), channel_id=1, source_target_pairs={{0,96},{32,0},{64,32},{96,64},{1,97},{33,1},{65,33},{97,65},{2,98}... | collective-permute-start | bytes 1376264 | tf_op jit(solution)/shard_map/ppermute | solution.py:19
  3.5 27.6 %collective-permute-start.1 = (bf16[128,1792]{1,0:T(8,128)(2,1)}, bf16[128,1792]{1,0:T(8,128)(2,1)}, u32[]{:S(2)}, u32[]{:S(2)}) collective-permute-start(bf16[128,1792]{1,0:T(8,128)(2,1)} %param.11), channel_id=1, source_target_pairs={{0,32},{32,64},{64,96},{96,0},{1,33},{33,65},{65,97},{97,1},{2,34}... | collective-permute-start | bytes 1376264 | tf_op jit(solution)/shard_map/ppermute | solution.py:19
  4.6 29.5 %collective-permute-start.4 = (bf16[128,1792]{1,0:T(8,128)(2,1)S(1)}, bf16[128,1792]{1,0:T(8,128)(2,1)S(1)}, u32[]{:S(2)}, u32[]{:S(2)}) collective-permute-start(bf16[128,1792]{1,0:T(8,128)(2,1)S(1)} %shard_map.129.refs_1_), channel_id=1, source_target_pairs={{0,32},{32,64},{64,96},{96,0},{1,33},{33,65},{65,97},{97,1},{2,34}... | collective-permute-start | bytes 1376264 | tf_op jit(solution)/shard_map/ppermute | solution.py:19
  7.3 50.5 %collective-permute-start.5 = (bf16[128,1792]{1,0:T(8,128)(2,1)}, bf16[128,1792]{1,0:T(8,128)(2,1)}, u32[]{:S(2)}, u32[]{:S(2)}) collective-permute-start(bf16[128,1792]{1,0:T(8,128)(2,1)} %shard_map.130.refs_2_), channel_id=1, source_target_pairs={{0,32},{32,64},{64,96},{96,0},{1,33},{33,65},{65,97},{97,1},{2,34}... | collective-permute-start | bytes 1376264 | tf_op jit(solution)/shard_map/ppermute | solution.py:19
  9.8 31.9 %collective-permute-start.6 = (bf16[128,1792]{1,0:T(8,128)(2,1)S(1)}, bf16[128,1792]{1,0:T(8,128)(2,1)}, u32[]{:S(2)}, u32[]{:S(2)}) collective-permute-start(bf16[128,1792]{1,0:T(8,128)(2,1)S(1)} %shard_map.131.refs_3_), channel_id=1, source_target_pairs={{0,96},{32,0},{64,32},{96,64},{1,97},{33,1},{65,33},{97,65},{2,98}... | collective-permute-start | bytes 1376264 | tf_op jit(solution)/shard_map/ppermute | solution.py:19
  17.4 42.7 %all-to-all-start.1 = ((bf16[32,16,1792]{2,1,0:T(8,128)(2,1)}), bf16[32,16,1792]{2,1,0:T(8,128)(2,1)S(1)}, u32[]{:S(2)}, u32[]{:S(2)}) async-start(bf16[32,16,1792]{2,1,0:T(8,128)(2,1)} %bitcast.85), calls=%async_computation.1 | async-start | bytes 3670016 | tf_op jit(solution)/shard_map/all_to_all | solution.py:395
  28.8 29.0 %collective-permute-start.7 = (bf16[128,1792]{1,0:T(8,128)(2,1)}, bf16[128,1792]{1,0:T(8,128)(2,1)S(1)}, u32[]{:S(2)}, u32[]{:S(2)}) collective-permute-start(bf16[128,1792]{1,0:T(8,128)(2,1)} %shard_map.132.refs_4_), channel_id=1, source_target_pairs={{0,96},{32,0},{64,32},{96,64},{1,97},{33,1},{65,33},{97,65},{2,98}... | collective-permute-start | bytes 1376264 | tf_op jit(solution)/shard_map/ppermute | solution.py:19
  31.2 15.5 %collective-permute-start.3 = (bf16[64,1792]{1,0:T(8,128)(2,1)S(1)}, bf16[64,1792]{1,0:T(8,128)(2,1)S(1)}, u32[]{:S(2)}, u32[]{:S(2)}) collective-permute-start(bf16[64,1792]{1,0:T(8,128)(2,1)S(1)} %slice.74), channel_id=1, source_target_pairs={{0,96},{32,0},{64,32},{96,64},{1,97},{33,1},{65,33},{97,65},{2,98}... | collective-permute-start | bytes 688136 | tf_op jit(solution)/shard_map/ppermute | solution.py:19
  34.1 7.6 %copy-start.16 = (bf16[128,1792]{1,0:T(8,128)(2,1)}, bf16[128,1792]{1,0:T(8,128)(2,1)S(1)}, u32[]{:S(2)}) copy-start(bf16[128,1792]{1,0:T(8,128)(2,1)S(1)} %collective-permute-done.4.refs_0_.refs_1_) | copy-start | bytes 1376260
  34.1 15.1 %collective-permute-start.2 = (bf16[64,1792]{1,0:T(8,128)(2,1)S(1)}, bf16[64,1792]{1,0:T(8,128)(2,1)S(1)}, u32[]{:S(2)}, u32[]{:S(2)}) collective-permute-start(bf16[64,1792]{1,0:T(8,128)(2,1)S(1)} %slice.73), channel_id=1, source_target_pairs={{0,32},{32,64},{64,96},{96,0},{1,33},{33,65},{65,97},{97,1},{2,34}... | collective-permute-start | bytes 688136 | tf_op jit(solution)/shard_map/ppermute | solution.py:19
  37.9 12.5 %copy-start.44 = (bf16[128,1792]{1,0:T(8,128)(2,1)S(1)}, bf16[128,1792]{1,0:T(8,128)(2,1)}, u32[]{:S(2)}) copy-start(bf16[128,1792]{1,0:T(8,128)(2,1)} %param.11) | copy-start | bytes 1376260
  40.2 12.8 %copy-start.5 = (bf16[512,1792]{1,0:T(8,128)(2,1)}, bf16[512,1792]{1,0:T(8,128)(2,1)S(1)}, u32[]{:S(2)}) copy-start(bf16[512,1792]{1,0:T(8,128)(2,1)S(1)} %shard_map.134.refs_8_) | copy-start | bytes 5505028
  41.7 12.0 %copy-start.42 = (bf16[128,7168]{1,0:T(8,128)(2,1)S(1)}, bf16[128,7168]{1,0:T(8,128)(2,1)}, u32[]{:S(2)}) copy-start(bf16[128,7168]{1,0:T(8,128)(2,1)} %param.10) | copy-start | bytes 5505028
  41.7 12.0 %copy-start.50 = (f32[7168]{0:T(1024)S(1)}, f32[7168]{0:T(1024)}, u32[]{:S(2)}) copy-start(f32[7168]{0:T(1024)} %param.14) | copy-start | bytes 86020
  41.7 12.0 %copy-start.51 = (f32[7168]{0:T(1024)S(1)}, f32[7168]{0:T(1024)}, u32[]{:S(2)}) copy-start(f32[7168]{0:T(1024)} %param.15) | copy-start | bytes 86020
  41.7 16.0 %collective-permute-start.8 = (bf16[128,1792]{1,0:T(8,128)(2,1)S(1)}, bf16[128,1792]{1,0:T(8,128)(2,1)S(1)}, u32[]{:S(2)}, u32[]{:S(2)}) collective-permute-start(bf16[128,1792]{1,0:T(8,128)(2,1)S(1)} %collective-permute-done.4.refs_0_.refs_1_), channel_id=1, source_target_pairs={{0,32},{32,64},{64,96},{96,0},{1,33},{33,65},{65,97},{97,1},{2,34}... | collective-permute-start | bytes 1376264 | tf_op jit(solution)/shard_map/ppermute | solution.py:19
  46.7 12.3 %collective-permute-start.9 = (bf16[128,1792]{1,0:T(8,128)(2,1)}, bf16[128,1792]{1,0:T(8,128)(2,1)S(1)}, u32[]{:S(2)}, u32[]{:S(2)}) collective-permute-start(bf16[128,1792]{1,0:T(8,128)(2,1)} %collective-permute-done.6.refs_3_), channel_id=1, source_target_pairs={{0,96},{32,0},{64,32},{96,64},{1,97},{33,1},{65,33},{97,65},{2,98}... | collective-permute-start | bytes 1376264 | tf_op jit(solution)/shard_map/ppermute | solution.py:19
  60.1 17.4 %copy-start = (bf16[32,16,1792]{2,1,0:T(8,128)(2,1)}, bf16[32,16,1792]{2,1,0:T(8,128)(2,1)S(1)}, u32[]{:S(2)}) copy-start(bf16[32,16,1792]{2,1,0:T(8,128)(2,1)S(1)} %all-to-all-done.1) | copy-start | bytes 5505028
  60.1 8.2 %copy-start.49 = (bf16[128,1792]{1,0:T(8,128)(2,1)S(1)}, bf16[128,1792]{1,0:T(8,128)(2,1)}, u32[]{:S(2)}) copy-start(bf16[128,1792]{1,0:T(8,128)(2,1)} %copy-done.48) | copy-start | bytes 1376260
  60.1 55.2 %all-to-all-start = ((bf16[32,8,7168]{2,1,0:T(8,128)(2,1)}), bf16[32,8,7168]{2,1,0:T(8,128)(2,1)}, u32[]{:S(2)}, u32[]{:S(2)}) async-start(bf16[32,8,7168]{2,1,0:T(8,128)(2,1)} %bitcast.82), calls=%async_computation | async-start | bytes 7340032 | tf_op jit(solution)/shard_map/all_to_all | solution.py:395
  67.6 14.8 %collective-permute-start.12 = (bf16[128,1792]{1,0:T(8,128)(2,1)}, bf16[128,1792]{1,0:T(8,128)(2,1)S(1)}, u32[]{:S(2)}, u32[]{:S(2)}) collective-permute-start(bf16[128,1792]{1,0:T(8,128)(2,1)} %collective-permute-done.5.refs_2_), channel_id=1, source_target_pairs={{0,32},{32,64},{64,96},{96,0},{1,33},{33,65},{65,97},{97,1},{2,34}... | collective-permute-start | bytes 1376264 | tf_op jit(solution)/shard_map/ppermute | solution.py:19
  68.3 14.2 %collective-permute-start.13 = (bf16[128,1792]{1,0:T(8,128)(2,1)S(1)}, bf16[128,1792]{1,0:T(8,128)(2,1)S(1)}, u32[]{:S(2)}, u32[]{:S(2)}) collective-permute-start(bf16[128,1792]{1,0:T(8,128)(2,1)S(1)} %copy-done.49), channel_id=1, source_target_pairs={{0,96},{32,0},{64,32},{96,64},{1,97},{33,1},{65,33},{97,65},{2,98}... | collective-permute-start | bytes 1376264 | tf_op jit(solution)/shard_map/ppermute | solution.py:19
  70.9 52.7 %collective-permute-start.10 = (bf16[512,1792]{1,0:T(8,128)(2,1)}, bf16[512,1792]{1,0:T(8,128)(2,1)}, u32[]{:S(2)}, u32[]{:S(2)}) collective-permute-start(bf16[512,1792]{1,0:T(8,128)(2,1)} %copy-done.5), channel_id=1, source_target_pairs={{0,96},{32,0},{64,32},{96,64},{1,97},{33,1},{65,33},{97,65},{2,98}... | collective-permute-start | bytes 5505032 | tf_op jit(solution)/shard_map/ppermute | solution.py:19
  72.8 53.6 %collective-permute-start.11 = (bf16[512,1792]{1,0:T(8,128)(2,1)}, bf16[512,1792]{1,0:T(8,128)(2,1)}, u32[]{:S(2)}, u32[]{:S(2)}) collective-permute-start(bf16[512,1792]{1,0:T(8,128)(2,1)} %copy-done.4), channel_id=1, source_target_pairs={{0,32},{32,64},{64,96},{96,0},{1,33},{33,65},{65,97},{97,1},{2,34}... | collective-permute-start | bytes 5505032 | tf_op jit(solution)/shard_map/ppermute | solution.py:19
  79.8 8.6 %copy-start.3 = (bf16[512,1792]{1,0:T(8,128)(2,1)}, bf16[512,1792]{1,0:T(8,128)(2,1)S(1)}, u32[]{:S(2)}) copy-start(bf16[512,1792]{1,0:T(8,128)(2,1)S(1)} %shard_map.142.refs_0_) | copy-start | bytes 5505028
  115.3 61.9 %all-to-all-start.2 = ((bf16[32,8,7168]{2,1,0:T(8,128)(2,1)}), bf16[32,8,7168]{2,1,0:T(8,128)(2,1)}, u32[]{:S(2)}, u32[]{:S(2)}) async-start(bf16[32,8,7168]{2,1,0:T(8,128)(2,1)} %bitcast.81), calls=%async_computation.2 | async-start | bytes 7340032 | tf_op jit(solution)/shard_map/all_to_all | solution.py:395
  120.3 9.8 %collective-permute-start.14 = (bf16[256,512]{1,0:T(8,128)(2,1)S(1)}, bf16[256,512]{1,0:T(8,128)(2,1)S(1)}, u32[]{:S(2)}, u32[]{:S(2)}) collective-permute-start(bf16[256,512]{1,0:T(8,128)(2,1)S(1)} %copy-done.40), channel_id=1, source_target_pairs={{0,32},{32,64},{64,96},{96,0},{1,33},{33,65},{65,97},{97,1},{2,34}... | collective-permute-start | bytes 786440 | tf_op jit(solution)/shard_map/ppermute | solution.py:19
  120.9 9.1 %collective-permute-start.15 = (bf16[256,512]{1,0:T(8,128)(2,1)S(1)}, bf16[256,512]{1,0:T(8,128)(2,1)S(1)}, u32[]{:S(2)}, u32[]{:S(2)}) collective-permute-start(bf16[256,512]{1,0:T(8,128)(2,1)S(1)} %copy-done.38), channel_id=1, source_target_pairs={{0,96},{32,0},{64,32},{96,64},{1,97},{33,1},{65,33},{97,65},{2,98}... | collective-permute-start | bytes 786440 | tf_op jit(solution)/shard_map/ppermute | solution.py:19
  130.2 13.8 %collective-permute-start.17 = (bf16[512,512]{1,0:T(8,128)(2,1)S(1)}, bf16[512,512]{1,0:T(8,128)(2,1)}, u32[]{:S(2)}, u32[]{:S(2)}) collective-permute-start(bf16[512,512]{1,0:T(8,128)(2,1)S(1)} %get-tuple-element.43.refs_1_), channel_id=1, source_target_pairs={{0,96},{32,0},{64,32},{96,64},{1,97},{33,1},{65,33},{97,65},{2,98}... | collective-permute-start | bytes 1572872 | tf_op jit(solution)/shard_map/ppermute | solution.py:19
  133.3 14.2 %collective-permute-start.16 = (bf16[512,512]{1,0:T(8,128)(2,1)S(1)}, bf16[512,512]{1,0:T(8,128)(2,1)}, u32[]{:S(2)}, u32[]{:S(2)}) collective-permute-start(bf16[512,512]{1,0:T(8,128)(2,1)S(1)} %get-tuple-element.42.refs_0_), channel_id=1, source_target_pairs={{0,32},{32,64},{64,96},{96,0},{1,33},{33,65},{65,97},{97,1},{2,34}... | collective-permute-start | bytes 1572872 | tf_op jit(solution)/shard_map/ppermute | solution.py:19
  153.7 16.3 %collective-permute-start.18 = (bf16[128,2816]{1,0:T(8,128)(2,1)S(1)}, bf16[128,2816]{1,0:T(8,128)(2,1)S(1)}, u32[]{:S(2)}, u32[]{:S(2)}) collective-permute-start(bf16[128,2816]{1,0:T(8,128)(2,1)S(1)} %get-tuple-element.47), channel_id=1, source_target_pairs={{0,96},{32,0},{64,32},{96,64},{1,97},{33,1},{65,33},{97,65},{2,98}... | collective-permute-start | bytes 2162696 | tf_op jit(solution)/shard_map/ppermute | solution.py:19
  154.1 17.4 %collective-permute-start.19 = (bf16[128,2816]{1,0:T(8,128)(2,1)S(1)}, bf16[128,2816]{1,0:T(8,128)(2,1)S(1)}, u32[]{:S(2)}, u32[]{:S(2)}) collective-permute-start(bf16[128,2816]{1,0:T(8,128)(2,1)S(1)} %get-tuple-element.48), channel_id=1, source_target_pairs={{0,32},{32,64},{64,96},{96,0},{1,33},{33,65},{65,97},{97,1},{2,34}... | collective-permute-start | bytes 2162696 | tf_op jit(solution)/shard_map/ppermute | solution.py:19
  164.0 9.9 %copy-start.32 = (bf16[256,1792]{1,0:T(8,128)(2,1)}, bf16[256,1792]{1,0:T(8,128)(2,1)S(1)}, u32[]{:S(2)}) copy-start(bf16[256,1792]{1,0:T(8,128)(2,1)S(1)} %get-tuple-element.59.a_ref) | copy-start | bytes 2752516
  173.9 32.0 %collective-permute-start.20 = (bf16[256,2048]{1,0:T(8,128)(2,1)}, bf16[256,2048]{1,0:T(8,128)(2,1)}, u32[]{:S(2)}, u32[]{:S(2)}) collective-permute-start(bf16[256,2048]{1,0:T(8,128)(2,1)} %get-tuple-element.53.refs_0_), channel_id=1, source_target_pairs={{0,32},{32,64},{64,96},{96,0},{1,33},{33,65},{65,97},{97,1},{2,34}... | collective-permute-start | bytes 3145736 | tf_op jit(solution)/shard_map/ppermute | solution.py:19
  174.2 31.8 %collective-permute-start.21 = (bf16[256,2048]{1,0:T(8,128)(2,1)}, bf16[256,2048]{1,0:T(8,128)(2,1)}, u32[]{:S(2)}, u32[]{:S(2)}) collective-permute-start(bf16[256,2048]{1,0:T(8,128)(2,1)} %get-tuple-element.54.refs_1_), channel_id=1, source_target_pairs={{0,96},{32,0},{64,32},{96,64},{1,97},{33,1},{65,33},{97,65},{2,98}... | collective-permute-start | bytes 3145736 | tf_op jit(solution)/shard_map/ppermute | solution.py:19
  193.2 11.7 %copy-start.36 = (bf16[128,2816]{1,0:T(8,128)(2,1)}, bf16[128,2816]{1,0:T(8,128)(2,1)S(1)}, u32[]{:S(2)}) copy-start(bf16[128,2816]{1,0:T(8,128)(2,1)S(1)} %get-tuple-element.58.refs_7_) | copy-start | bytes 2162692
  193.3 20.7 %collective-permute-start.22 = (bf16[128,2816]{1,0:T(8,128)(2,1)S(1)}, bf16[128,2816]{1,0:T(8,128)(2,1)S(1)}, u32[]{:S(2)}, u32[]{:S(2)}) collective-permute-start(bf16[128,2816]{1,0:T(8,128)(2,1)S(1)} %get-tuple-element.58.refs_7_), channel_id=1, source_target_pairs={{0,32},{32,64},{64,96},{96,0},{1,33},{33,65},{65,97},{97,1},{2,34}... | collective-permute-start | bytes 2162696 | tf_op jit(solution)/shard_map/ppermute | solution.py:19
  193.3 20.7 %collective-permute-start.23 = (bf16[128,2816]{1,0:T(8,128)(2,1)S(1)}, bf16[128,2816]{1,0:T(8,128)(2,1)S(1)}, u32[]{:S(2)}, u32[]{:S(2)}) collective-permute-start(bf16[128,2816]{1,0:T(8,128)(2,1)S(1)} %get-tuple-element.60), channel_id=1, source_target_pairs={{0,96},{32,0},{64,32},{96,64},{1,97},{33,1},{65,33},{97,65},{2,98}... | collective-permute-start | bytes 2162696 | tf_op jit(solution)/shard_map/ppermute | solution.py:19
  196.6 9.4 %copy-start.11 = (bf16[128,1792]{1,0:T(8,128)(2,1)S(1)}, bf16[128,1792]{1,0:T(8,128)(2,1)}, u32[]{:S(2)}) copy-start(bf16[128,1792]{1,0:T(8,128)(2,1)} %copy-done.10) | copy-start | bytes 1376260
  196.6 9.4 %copy-start.14 = (bf16[128,1792]{1,0:T(8,128)(2,1)S(1)}, bf16[128,1792]{1,0:T(8,128)(2,1)}, u32[]{:S(2)}) copy-start(bf16[128,1792]{1,0:T(8,128)(2,1)} %copy-done.13) | copy-start | bytes 1376260
  196.6 9.4 %copy-start.21 = (bf16[128,2816]{1,0:T(8,128)(2,1)S(1)}, bf16[128,2816]{1,0:T(8,128)(2,1)}, u32[]{:S(2)}) copy-start(bf16[128,2816]{1,0:T(8,128)(2,1)} %copy-done.20) | copy-start | bytes 2162692
  196.6 9.4 %copy-start.23 = (bf16[128,2816]{1,0:T(8,128)(2,1)S(1)}, bf16[128,2816]{1,0:T(8,128)(2,1)}, u32[]{:S(2)}) copy-start(bf16[128,2816]{1,0:T(8,128)(2,1)} %copy-done.22) | copy-start | bytes 2162692
  206.0 8.0 %copy-start.34 = (bf16[256,1792]{1,0:T(8,128)(2,1)}, bf16[256,1792]{1,0:T(8,128)(2,1)S(1)}, u32[]{:S(2)}) copy-start(bf16[256,1792]{1,0:T(8,128)(2,1)S(1)} %get-tuple-element.67.a_ref) | copy-start | bytes 2752516
  206.0 8.0 %copy-start.33 = (bf16[256,1792]{1,0:T(8,128)(2,1)S(1)}, bf16[256,1792]{1,0:T(8,128)(2,1)}, u32[]{:S(2)}) copy-start(bf16[256,1792]{1,0:T(8,128)(2,1)} %copy-done.32) | copy-start | bytes 2752516
  216.5 39.0 %all-to-all-start.3 = ((bf16[32,8,3584]{2,1,0:T(8,128)(2,1)}), bf16[32,8,3584]{2,1,0:T(8,128)(2,1)}, u32[]{:S(2)}, u32[]{:S(2)}) async-start(bf16[32,8,3584]{2,1,0:T(8,128)(2,1)} %bitcast.84), calls=%async_computation.3 | async-start | bytes 3670016 | tf_op jit(solution)/shard_map/all_to_all | solution.py:395
  224.1 10.6 %copy-start.12 = (bf16[128,1792]{1,0:T(8,128)(2,1)S(1)}, bf16[128,1792]{1,0:T(8,128)(2,1)}, u32[]{:S(2)}) copy-start(bf16[128,1792]{1,0:T(8,128)(2,1)} %copy-done.10) | copy-start | bytes 1376260
  224.1 10.5 %copy-start.15 = (bf16[128,1792]{1,0:T(8,128)(2,1)S(1)}, bf16[128,1792]{1,0:T(8,128)(2,1)}, u32[]{:S(2)}) copy-start(bf16[128,1792]{1,0:T(8,128)(2,1)} %copy-done.13) | copy-start | bytes 1376260
  224.1 10.5 %copy-start.29 = (bf16[256,512]{1,0:T(8,128)(2,1)S(1)}, bf16[256,512]{1,0:T(8,128)(2,1)}, u32[]{:S(2)}) copy-start(bf16[256,512]{1,0:T(8,128)(2,1)} %copy-done.28) | copy-start | bytes 786436
  224.2 6.9 %collective-permute-start.24 = (bf16[128,512]{1,0:T(8,128)(2,1)S(1)}, bf16[128,512]{1,0:T(8,128)(2,1)S(1)}, u32[]{:S(2)}, u32[]{:S(2)}) collective-permute-start(bf16[128,512]{1,0:T(8,128)(2,1)S(1)} %shard_map.153), channel_id=1, source_target_pairs={{0,32},{32,64},{64,96},{96,0},{1,33},{33,65},{65,97},{97,1},{2,34}... | collective-permute-start | bytes 393224 | tf_op jit(solution)/shard_map/ppermute | solution.py:19
  224.3 6.8 %collective-permute-start.25 = (bf16[128,512]{1,0:T(8,128)(2,1)S(1)}, bf16[128,512]{1,0:T(8,128)(2,1)S(1)}, u32[]{:S(2)}, u32[]{:S(2)}) collective-permute-start(bf16[128,512]{1,0:T(8,128)(2,1)S(1)} %shard_map.154), channel_id=1, source_target_pairs={{0,96},{32,0},{64,32},{96,64},{1,97},{33,1},{65,33},{97,65},{2,98}... | collective-permute-start | bytes 393224 | tf_op jit(solution)/shard_map/ppermute | solution.py:19
  231.4 23.0 %collective-permute-start.26 = (bf16[256,1792]{1,0:T(8,128)(2,1)S(1)}, bf16[256,1792]{1,0:T(8,128)(2,1)S(1)}, u32[]{:S(2)}, u32[]{:S(2)}) collective-permute-start(bf16[256,1792]{1,0:T(8,128)(2,1)S(1)} %get-tuple-element.65.refs_7_), channel_id=1, source_target_pairs={{0,32},{32,64},{64,96},{96,0},{1,33},{33,65},{65,97},{97,1},{2,34}... | collective-permute-start | bytes 2752520 | tf_op jit(solution)/shard_map/ppermute | solution.py:19
  231.8 22.6 %copy-start.35 = (bf16[256,1792]{1,0:T(8,128)(2,1)S(1)}, bf16[256,1792]{1,0:T(8,128)(2,1)}, u32[]{:S(2)}) copy-start(bf16[256,1792]{1,0:T(8,128)(2,1)} %copy-done.34) | copy-start | bytes 2752516
  231.8 22.6 %collective-permute-start.27 = (bf16[256,1792]{1,0:T(8,128)(2,1)S(1)}, bf16[256,1792]{1,0:T(8,128)(2,1)S(1)}, u32[]{:S(2)}, u32[]{:S(2)}) collective-permute-start(bf16[256,1792]{1,0:T(8,128)(2,1)S(1)} %get-tuple-element.66.refs_8_), channel_id=1, source_target_pairs={{0,96},{32,0},{64,32},{96,64},{1,97},{33,1},{65,33},{97,65},{2,98}... | collective-permute-start | bytes 2752520 | tf_op jit(solution)/shard_map/ppermute | solution.py:19
  255.5 34.2 %all-to-all-start.4 = ((bf16[32,8,3584]{2,1,0:T(8,128)(2,1)}), bf16[32,8,3584]{2,1,0:T(8,128)(2,1)}, u32[]{:S(2)}, u32[]{:S(2)}) async-start(bf16[32,8,3584]{2,1,0:T(8,128)(2,1)} %bitcast.83), calls=%async_computation.4 | async-start | bytes 3670016 | tf_op jit(solution)/shard_map/all_to_all | solution.py:395
  265.9 25.4 %copy-start.55 = (f32[128]{0:T(128)S(1)}, f32[128]{0:T(128)}, u32[]{:S(2)}) copy-start(f32[128]{0:T(128)} %copy-done.54) | copy-start | bytes 1540
  266.0 25.4 %copy-start.57 = (f32[128]{0:T(128)S(1)}, f32[128]{0:T(128)}, u32[]{:S(2)}) copy-start(f32[128]{0:T(128)} %copy-done.56) | copy-start | bytes 1540
  271.0 23.3 %copy-start.43 = (bf16[128,7168]{1,0:T(8,128)(2,1)S(1)}, bf16[128,7168]{1,0:T(8,128)(2,1)}, u32[]{:S(2)}) copy-start(bf16[128,7168]{1,0:T(8,128)(2,1)} %param.10) | copy-start | bytes 5505028
  271.0 23.3 %copy-start.45 = (bf16[128,1792]{1,0:T(8,128)(2,1)S(1)}, bf16[128,1792]{1,0:T(8,128)(2,1)}, u32[]{:S(2)}) copy-start(bf16[128,1792]{1,0:T(8,128)(2,1)} %param.11) | copy-start | bytes 1376260
  291.4 13.4 %copy-start.53 = (f32[128]{0:T(128)S(1)}, f32[128]{0:T(128)}, u32[]{:S(2)}) copy-start(f32[128]{0:T(128)} %copy-done.52) | copy-start | bytes 1540
  291.4 13.4 %copy-start.59 = (f32[128]{0:T(128)S(1)}, f32[128]{0:T(128)}, u32[]{:S(2)}) copy-start(f32[128]{0:T(128)} %get-tuple-element.87) | copy-start | bytes 1540
  291.4 13.4 %copy-start.60 = (f32[128]{0:T(128)S(1)}, f32[128]{0:T(128)}, u32[]{:S(2)}) copy-start(f32[128]{0:T(128)} %get-tuple-element.91) | copy-start | bytes 1540
  296.0 4.3 %collective-permute-start.30 = (f32[4,128]{1,0:T(4,128)S(1)}, f32[4,128]{1,0:T(4,128)S(1)}, u32[]{:S(2)}, u32[]{:S(2)}) collective-permute-start(f32[4,128]{1,0:T(4,128)S(1)} %pad_maximum_fusion.3), channel_id=1, source_target_pairs={{0,96},{32,0},{64,32},{96,64},{1,97},{33,1},{65,33},{97,65},{2,98}... | collective-permute-start | bytes 6152 | tf_op jit(solution)/shard_map/ppermute | solution.py:19
  299.1 5.1 %collective-permute-start.29 = (f32[4,128]{1,0:T(4,128)S(1)}, f32[4,128]{1,0:T(4,128)S(1)}, u32[]{:S(2)}, u32[]{:S(2)}) collective-permute-start(f32[4,128]{1,0:T(4,128)S(1)} %pad_maximum_fusion.3), channel_id=1, source_target_pairs={{0,64},{32,96},{64,0},{96,32},{1,65},{33,97},{65,1},{97,33},{2,66}... | collective-permute-start | bytes 6152 | tf_op jit(solution)/shard_map/ppermute | solution.py:19
  299.1 5.1 %collective-permute-start.28 = (f32[4,128]{1,0:T(4,128)S(1)}, f32[4,128]{1,0:T(4,128)S(1)}, u32[]{:S(2)}, u32[]{:S(2)}) collective-permute-start(f32[4,128]{1,0:T(4,128)S(1)} %pad_maximum_fusion.3), channel_id=1, source_target_pairs={{0,32},{32,64},{64,96},{96,0},{1,33},{33,65},{65,97},{97,1},{2,34}... | collective-permute-start | bytes 6152 | tf_op jit(solution)/shard_map/ppermute | solution.py:19
  (34 other events, 110.7 us)
